TPU v7x, 256 devices: a whole 4x4x8 slice. The times are simulated.
256 devices in a mesh: docs: 64 (over z, y, x_lo), query: 4 (over x_hi, core).
Axes of the slice: x: 4 (x_hi: 2, x_lo: 2; x = x_hi * 2 + x_lo), y: 4, z: 8, core: 2. Of those that a mesh axis runs over, the one named last changes fastest.
Arguments:
- activations: bfloat16 [4, 8192, 4096], P('query', 'docs'), may hold values from -6 to 6
- out_grads: bfloat16 [4, 8192, 14336], P('query', 'docs'), may hold values from -6 to 6
- proj_in: bfloat16 [4096, 64], replicated, may hold values from -0.09375 to 0.09375
- proj_out: bfloat16 [14336, 64], replicated, may hold values from -0.046875 to 0.046875
- panels: bfloat16 [512, 4096], P('query'), may hold values from -0.09375 to 0.09375
- lengths: int32 [4, 64, 64], P('query', 'docs'), may hold values from 1 to 4, 128 in all within a row
- piece_owner: int32 [4, 64, 64], P('query', 'docs'), may hold values from 0 to 63, each once within a row
- doc_slot: int32 [4, 64, 64], P('query', None, 'docs'), may hold values from 0 to 7
- panel_order: int32 [64, 4], P('docs'), may hold values from 0 to 3, each once within a row
Outputs:
- scores: float32 [4, 512, 512], P('query', 'docs')
Inputs may be any that keep to these rules, and one draw needn't show every extreme that they name: `lengths`: each row sums to 128; the largest entry of every row is exactly 4. `piece_owner`: each row is a permutation of the 64 owners. `panel_order`: each row is a permutation of the 4 panels.
All inputs are finite; a program needn't handle non-finite values.
Results may differ from a plain program's by a relative error of at most 0.0057.
Values may be sent and summed in bfloat16 or wider, within the bound.
No kernel may reach another device: no remote copies, remote signals or barrier semaphores. Data moves between devices by JAX's collectives and lax.ppermute only.
A program may use at most 64 MiB of HBM per device.

v0:
```python
import jax
import jax.numpy as jnp
from jax import lax
from jax.sharding import PartitionSpec as P

DOC_OWN = 8


def from_root(value, axis, source):
    kept = jnp.where(lax.axis_index(axis) == source, value, 0).astype(value.dtype)
    return lax.psum(kept, axis)


def outer_rows(rows, width):
    lead = rows.shape[:-1]
    grad_part = rows[..., :width].astype(jnp.float32)
    act_part = rows[..., width:].astype(jnp.float32)
    product = grad_part[..., :, None] * act_part[..., None, :]
    return product.reshape(lead + (width * width,)).astype(jnp.bfloat16)


def against_panel(grads_now, panel_now):
    return lax.dot_general(
        grads_now, panel_now, (((1,), (1,)), ((), ())), preferred_element_type=jnp.float32
    )


def shards(
    activations, out_grads, proj_in, proj_out, panels, lengths, piece_owner, doc_slot, panel_order
):
    width = proj_in.shape[1]
    act_low = jnp.dot(activations[0], proj_in, preferred_element_type=jnp.float32).astype(
        jnp.bfloat16
    )
    grad_low = jnp.dot(out_grads[0], proj_out, preferred_element_type=jnp.float32).astype(
        jnp.bfloat16
    )
    low_rows = jnp.concatenate([grad_low, act_low], axis=1)
    owners = lax.axis_size("docs")
    row_count = low_rows.shape[0]
    capacity = 2 * row_count // owners
    piece_len = lengths[0, 0]
    piece_dest = piece_owner[0, 0]
    starts = jnp.cumsum(piece_len) - piece_len
    chosen = (piece_dest[None, :] == jnp.arange(owners, dtype=jnp.int32)[:, None]).astype(jnp.int32)
    offset = jnp.sum(chosen * starts[None, :], axis=1)
    amount = jnp.sum(chosen * piece_len[None, :], axis=1)
    column = jnp.arange(capacity, dtype=jnp.int32)
    is_live = column[None, :] < amount[:, None]
    row_index = jnp.where(is_live, offset[:, None] + column[None, :], 0)
    packed = jnp.take(low_rows, row_index.reshape(-1), axis=0).reshape(owners, capacity, 2 * width)
    packed = jnp.where(is_live[:, :, None], packed, jnp.zeros((), jnp.bfloat16))
    arrived = lax.all_to_all(
        outer_rows(packed, width), "docs", split_axis=0, concat_axis=0, tiled=True
    )
    slots = doc_slot[0, :, 0]
    member = (slots[None, :] == jnp.arange(DOC_OWN, dtype=jnp.int32)[:, None]).astype(jnp.bfloat16)
    member_rows = jnp.repeat(member, capacity, axis=1)
    grads_now = jnp.dot(
        member_rows,
        arrived.reshape(owners * capacity, width * width),
        preferred_element_type=jnp.float32,
    ).astype(jnp.bfloat16)
    query_count = lax.axis_size("query")
    my_order = panel_order[0]
    blocks = []
    for step in range(query_count):
        panel_now = from_root(panels, "query", my_order[step])
        blocks.append(against_panel(grads_now, panel_now))
    scores = jnp.concatenate(blocks, axis=1)
    return scores[None]


def solution(mesh):
    placed = (
        P("query", "docs", None),
        P("query", "docs", None),
        P(),
        P(),
        P("query", None),
        P("query", "docs", None),
        P("query", "docs", None),
        P("query", None, "docs"),
        P("docs", None),
    )
    return jax.shard_map(
        shards, mesh=mesh, in_specs=placed, out_specs=P("query", "docs", None), check_vma=False
    )
```

profile of v0, /device:TPU:1, one launch (start us, length us, event | category | flops | bytes accessed | tf_op | source)
XLA Modules:
  0.0 170.7 jit_solution(9992500148212412501)
XLA Ops:
  6.5 0.0 copy-start
  6.5 0.9 copy.21
  7.4 0.1 reduce-window.8
  7.5 0.1 reduce
  7.6 0.7 bitcast_subtract_fusion
  8.3 0.8 select_reduce_fusion.1
  9.1 0.1 iota_compare_fusion.1
  9.2 0.1 add_select_fusion
  9.3 1.8 %convolution_convert_fusion = bf16[128,64]{0,1:T(8,128)(2,1)S(1)} fusion(bf16[4096,64]{0,1:T(8,128)(2,1)} %param.11, bf16[1,128,4096]{2,1,0:T(8,128)(2,1)} %param.9), kind=kOutput, calls=%fused_computation.8 | convolution fusion | flops 67117056 | bytes 1589248 | tf_op jit(solution)/shard_map/dot_general | solution.py:32
  11.1 0.0 copy-done
  11.1 3.4 %fusion.4 = bf16[128,64]{0,1:T(8,128)(2,1)S(1)} fusion(bf16[14336,64]{0,1:T(8,128)(2,1)S(1)} %copy-done, bf16[1,128,14336]{2,1,0:T(8,128)(2,1)} %param.10), kind=kOutput, calls=%fused_computation.7 | convolution fusion | flops 234889216 | bytes 5521408 | tf_op jit(solution)/shard_map/dot_general | solution.py:35
  14.6 0.1 copy.22
  14.7 0.1 select_n.72
  14.8 0.9 gather_fusion
  15.7 0.2 select_select_fusion
  15.9 0.1 slice_convert_fusion.1
  16.0 4.3 %multiply_convert_fusion = bf16[64,4,64,64]{3,2,1,0:T(8,128)(2,1)} fusion(f32[64,4,64]{2,1,0:T(4,128)S(1)} %get-tuple-element.16, f32[64,4,64]{2,1,0:T(4,128)S(1)} %get-tuple-element.15), kind=kLoop, calls=%fused_computation.1 | loop fusion | flops 2097152 | bytes 2228224 | tf_op jit(solution)/shard_map/convert_element_type | solution.py:19
  20.3 7.1 %convert_element_type.36 = bf16[64,4,4096]{2,1,0:T(4,128)(2,1)} reshape(bf16[64,4,64,64]{3,2,1,0:T(8,128)(2,1)} %multiply_convert_fusion) | data formatting | bytes 4194304 | tf_op jit(solution)/shard_map/convert_element_type | solution.py:19
  27.4 0.0 copy-start.4
  27.4 0.0 copy-start.1
  27.4 14.0 %all-to-all-start = ((bf16[64,4,4096]{2,1,0:T(4,128)(2,1)}), bf16[64,4,4096]{2,1,0:T(4,128)(2,1)}, u32[]{:S(2)}, u32[]{:S(2)}) async-start(bf16[64,4,4096]{2,1,0:T(4,128)(2,1)} %convert_element_type.36), calls=%async_computation | async-start | bytes 4194304 | tf_op jit(solution)/shard_map/all_to_all | solution.py:53
  41.4 0.0 all-reduce.3.cloned.1.call-start
  41.4 0.0 copy-done.4
  41.5 0.6 fusion.10
  44.6 0.0 copy-done.1
  44.6 2.0 %broadcast_select_fusion.3 = (bf16[128,4096]{1,0:T(8,128)(2,1)}, bf16[128,4096]{1,0:T(8,128)(2,1)}, bf16[128,4096]{1,0:T(8,128)(2,1)}, bf16[128,4096]{1,0:T(8,128)(2,1)}) fusion(bf16[128,4096]{1,0:T(8,128)(2,1)S(1)} %copy-done.1, pred[]{:T(512)S(6)} %eq.50, pred[]{:T(512)S(6)} %eq.51, pred[]{:T(512)S(6)} %eq.53, pred[]{:T(512)S(6)} %eq.52), kind=kLoop, calls=%fused_computation.13 | loop fusion | flops 2097152 | bytes 5242884 | tf_op jit(solution)/shard_map/jit(_where)/select_n | solution.py:10
  46.6 0.0 copy-start.5
  46.6 0.0 all-reduce.3.cloned.1.call-update
  46.6 0.6 copy-done.5
  47.2 42.1 %all-to-all-done = bf16[64,4,4096]{2,1,0:T(4,128)(2,1)} async-done(((bf16[64,4,4096]{2,1,0:T(4,128)(2,1)}), bf16[64,4,4096]{2,1,0:T(4,128)(2,1)}, u32[]{:S(2)}, u32[]{:S(2)}) %all-to-all-start) | async-done | bytes 2097184 | tf_op jit(solution)/shard_map/all_to_all | solution.py:53
  89.4 3.9 %fusion = bf16[8,4096]{1,0:T(8,128)(2,1)S(1)} fusion(bf16[64,4,4096]{2,1,0:T(4,128)(2,1)} %all-to-all-done, bf16[8,64]{1,0:T(8,128)(2,1)S(1)} %fusion.9), kind=kOutput, calls=%fused_computation.3 | convolution fusion | flops 16809984 | bytes 2163712 | tf_op jit(solution)/shard_map/dot_general | solution.py:59
  93.3 65.8 %all-reduce.3.cloned.1.call-done = (bf16[128,4096]{1,0:T(8,128)(2,1)}, bf16[128,4096]{1,0:T(8,128)(2,1)}, bf16[128,4096]{1,0:T(8,128)(2,1)}, bf16[128,4096]{1,0:T(8,128)(2,1)}) async-done(((bf16[128,4096]{1,0:T(8,128)(2,1)}, bf16[128,4096]{1,0:T(8,128)(2,1)}, bf16[128,4096]{1,0:T(8,128)(2,1)}, bf16[128,4096]{1,0:T(8,128)(2,1)}), (bf16[128,4096]{1,0:T(8,128)(2,1)}, bf16[128,4096]{1,0:T(8,128)(2,1)}, ...) | async-done | bytes 4194320 | tf_op jit(solution)/shard_map/psum | solution.py:11
  159.1 0.0 copy-start.3
  159.1 0.0 copy-start.2
  159.1 1.7 %fusion.14 = f32[8,128]{1,0:T(8,128)S(1)} fusion(bf16[8,4096]{1,0:T(8,128)(2,1)S(1)} %fusion, bf16[128,4096]{1,0:T(8,128)(2,1)} %get-tuple-element.7), kind=kOutput, calls=%fused_computation.36 | convolution fusion | flops 8388608 | bytes 1118208 | tf_op jit(solution)/shard_map/dot_general | solution.py:23
  160.8 1.6 fusion.13
  162.4 0.0 copy-done.3
  162.4 0.4 fusion.12
  162.8 0.0 copy-done.2
  162.8 0.4 fusion.11
  163.2 0.6 maximum_bitcast_fusion
  (4 shorter events, 0.0 us)
Async XLA Ops:
  6.5 4.6 %copy-start = (bf16[14336,64]{0,1:T(8,128)(2,1)S(1)}, bf16[14336,64]{0,1:T(8,128)(2,1)}, u32[]{:S(2)}) copy-start(bf16[14336,64]{0,1:T(8,128)(2,1)} %param.12) | copy-start | bytes 5505028
  27.4 14.0 %copy-start.4 = (s32[1,4]{1,0:T(1,128)S(1)}, s32[1,4]{1,0:T(1,128)}, u32[]{:S(2)}) copy-start(s32[1,4]{1,0:T(1,128)} %param.17) | copy-start | bytes 52
  27.4 17.2 %copy-start.1 = (bf16[128,4096]{1,0:T(8,128)(2,1)S(1)}, bf16[128,4096]{1,0:T(8,128)(2,1)}, u32[]{:S(2)}) copy-start(bf16[128,4096]{1,0:T(8,128)(2,1)} %param.13) | copy-start | bytes 3145732
  27.4 62.0 %all-to-all-start = ((bf16[64,4,4096]{2,1,0:T(4,128)(2,1)}), bf16[64,4,4096]{2,1,0:T(4,128)(2,1)}, u32[]{:S(2)}, u32[]{:S(2)}) async-start(bf16[64,4,4096]{2,1,0:T(4,128)(2,1)} %convert_element_type.36), calls=%async_computation | async-start | bytes 4194304 | tf_op jit(solution)/shard_map/all_to_all | solution.py:53
  41.4 117.7 %all-reduce.3.cloned.1.call-start = ((), (), s32[]{:S(2)}) async-start(), calls=%async_computation.1 | async-start | bytes 8388608 | tf_op jit(solution)/shard_map/psum | solution.py:11
  46.6 0.7 copy-start.5
  159.1 3.4 %copy-start.3 = (bf16[128,4096]{1,0:T(8,128)(2,1)S(1)}, bf16[128,4096]{1,0:T(8,128)(2,1)}, u32[]{:S(2)}) copy-start(bf16[128,4096]{1,0:T(8,128)(2,1)} %get-tuple-element.9) | copy-start | bytes 3145732
  159.1 3.7 %copy-start.2 = (bf16[128,4096]{1,0:T(8,128)(2,1)S(1)}, bf16[128,4096]{1,0:T(8,128)(2,1)}, u32[]{:S(2)}) copy-start(bf16[128,4096]{1,0:T(8,128)(2,1)} %get-tuple-element.10) | copy-start | bytes 3145732
Sparse Core Ops, SparseCore 0:
  46.7 112.2 all-reduce.2
where the time goes:
time: 171 us
  waiting for transfers between devices  108 us (63%)
  between operations  16 us (9%)
  starting transfers between devices  14 us (8%)
  matrix products  13.3 us (8%)
  local copies, waits for them, and re-layouts  10.4 us (6%)
  other arithmetic  9.1 us (5%)
    psum x1, waiting for transfers between devices, from_root(): return lax.psum(kept, axis)  65.8 us
    all_to_all x1, waiting for transfers between devices, shards(): lax.all_to_all(outer_rows(packed, width), 'docs', split_axis=0, concat_ax...  42.1 us
    all_to_all x1, starting transfers between devices, shards(): lax.all_to_all(outer_rows(packed, width), 'docs', split_axis=0, concat_ax...  14 us
    convert_element_type x1, local copies, waits for them, and re-layouts, outer_rows(): return product.reshape(lead + (width * width,)).astype(jnp.bfloat16)  7.12 us
    convert_element_type x1, other arithmetic, outer_rows(): return product.reshape(lead + (width * width,)).astype(jnp.bfloat16)  4.28 us
    dot_general x4, matrix products, against_panel(): lax.dot_general(grads_now, panel_now, (((1,), (1,)), ((), ())), preferred...  4.13 us
    dot_general x1, matrix products, shards(): jnp.dot(member_rows, arrived.reshape(owners * capacity, width * width), p...  3.89 us
    dot_general x1, matrix products, shards(): jnp.dot(out_grads[0], proj_out, preferred_element_type=jnp.float32)  3.42 us
  transfers between devices with their start and end apart: 2, of which 2 were waited for; matrix products, arithmetic and copies ran while one was open for 4% of the time, Pallas kernels for 0%

commit v1 on v0

v1 whole, which is shorter than its diff:
```python
import jax
import jax.numpy as jnp
from jax import lax
from jax.experimental import pallas as pl
from jax.experimental.pallas import tpu as pltpu
from jax.sharding import PartitionSpec as P

DOC_OWN = 8
R = 64
CAP = 4
DOCS = 64
TOK = 128
ROWS = DOCS * CAP
PANEL = 128
QUART = PANEL // 4
NT = (((1,), (1,)), ((), ()))


def column_chunks(width, step):
    return [(at, min(step, width - at)) for at in range(0, width, step)]


def project_kernel(act_hbm, grad_hbm, win_hbm, wout_hbm, len_ref, own_ref, slot_ref,
                   rows_ref, member_ref, act_v, grad_v, win_v, wout_v, sems):
    jobs = []
    for x_hbm, w_hbm, x_v, w_v in (
        (act_hbm, win_hbm, act_v, win_v),
        (grad_hbm, wout_hbm, grad_v, wout_v),
    ):
        for at, size in column_chunks(x_hbm.shape[-1], 2048):
            cols = pl.ds(at, size)
            n = 2 * len(jobs)
            copies = (
                pltpu.make_async_copy(w_hbm.at[:, cols], w_v.at[:, cols], sems.at[n]),
                pltpu.make_async_copy(x_hbm.at[0, :, cols], x_v.at[:, cols], sems.at[n + 1]),
            )
            for copy in copies:
                copy.start()
            jobs.append((copies, x_v, w_v, cols))

    row = lax.broadcasted_iota(jnp.int32, (ROWS, DOCS), 0)
    piece = lax.broadcasted_iota(jnp.int32, (ROWS, DOCS), 1).astype(jnp.float32)
    lens = len_ref[...].astype(jnp.float32)
    chosen = own_ref[...] == (row >> 2)
    place = jnp.sum(jnp.where(chosen, piece, 0.0), axis=1, keepdims=True)
    amount = jnp.sum(jnp.where(chosen, lens, 0.0), axis=1, keepdims=True)
    offset = jnp.sum(jnp.where(piece < place, lens, 0.0), axis=1, keepdims=True)
    within = (lax.broadcasted_iota(jnp.int32, (ROWS, TOK), 0) & (CAP - 1)).astype(jnp.float32)
    token = lax.broadcasted_iota(jnp.int32, (ROWS, TOK), 1).astype(jnp.float32)
    take = jnp.where((token == offset + within) & (within < amount), 1.0, 0.0)
    take = take.astype(jnp.bfloat16)

    doc = lax.broadcasted_iota(jnp.int32, (DOC_OWN, DOCS), 0)
    mine = jnp.where(slot_ref[...] == doc, 1.0, 0.0).astype(jnp.bfloat16)
    source = lax.broadcasted_iota(jnp.int32, (DOCS, ROWS), 0)
    spread = jnp.where((lax.broadcasted_iota(jnp.int32, (DOCS, ROWS), 1) >> 2) == source, 1.0, 0.0)
    member_ref[...] = jnp.dot(mine, spread.astype(jnp.bfloat16), preferred_element_type=jnp.float32)

    low = {}
    for copies, x_v, w_v, cols in jobs:
        for copy in copies:
            copy.wait()
        part = lax.dot_general(x_v[:, cols], w_v[:, cols], NT, preferred_element_type=jnp.float32)
        low[id(x_v)] = part if id(x_v) not in low else low[id(x_v)] + part
    rows = jnp.concatenate([low[id(grad_v)], low[id(act_v)]], axis=1).astype(jnp.bfloat16)
    rows_ref[...] = jnp.dot(take, rows, preferred_element_type=jnp.float32).astype(jnp.bfloat16)


def project(activations, out_grads, proj_in, proj_out, lengths, piece_owner, slots):
    width_in, width_out = activations.shape[-1], out_grads.shape[-1]
    chunks = len(column_chunks(width_in, 2048)) + len(column_chunks(width_out, 2048))
    hbm = pl.BlockSpec(memory_space=pltpu.HBM)
    vmem = pl.BlockSpec(memory_space=pltpu.VMEM)
    return pl.pallas_call(
        project_kernel,
        out_shape=(
            jax.ShapeDtypeStruct((ROWS, 2 * R), jnp.bfloat16),
            jax.ShapeDtypeStruct((DOC_OWN, ROWS), jnp.float32),
        ),
        in_specs=[hbm] * 4 + [vmem] * 3,
        out_specs=(vmem, vmem),
        scratch_shapes=[
            pltpu.VMEM((TOK, width_in), jnp.bfloat16),
            pltpu.VMEM((TOK, width_out), jnp.bfloat16),
            pltpu.VMEM((R, width_in), jnp.bfloat16),
            pltpu.VMEM((R, width_out), jnp.bfloat16),
            pltpu.SemaphoreType.DMA((2 * chunks,)),
        ],
        compiler_params=pltpu.CompilerParams(vmem_limit_bytes=56 << 20),
        cost_estimate=pl.CostEstimate(
            flops=2 * TOK * (width_in + width_out) * R,
            bytes_accessed=2 * (TOK + R) * (width_in + width_out),
            transcendentals=0,
        ),
        name="project",
    )(activations, out_grads, proj_in.T, proj_out.T, lengths, piece_owner, slots)


def score_kernel(place_ref, rows_ref, member_ref, *refs):
    panel_refs, out_ref = refs[:-1], refs[-1]
    rows = rows_ref[...]
    eye = (lax.broadcasted_iota(jnp.int32, (2 * R, 2 * R), 0)
           == lax.broadcasted_iota(jnp.int32, (2 * R, 2 * R), 1))
    eye = jnp.where(eye, 1.0, 0.0).astype(jnp.bfloat16)
    turned = lax.dot_general(eye, rows, NT, preferred_element_type=jnp.float32)
    masked = turned[:R][:, None, :] * member_ref[...][None]
    masked = masked.reshape(R * DOC_OWN, ROWS).astype(jnp.bfloat16)
    wide = rows.astype(jnp.float32)
    lane = lax.broadcasted_iota(jnp.int32, (ROWS, 2 * R), 1)
    twice = jnp.where(lane < R, pltpu.roll(wide, R, 1), wide).astype(jnp.bfloat16)
    grads = jnp.dot(masked, twice, preferred_element_type=jnp.float32)
    grads = grads.reshape(R, DOC_OWN, 2 * R)
    low_half = lax.broadcasted_iota(jnp.int32, (DOC_OWN, 2 * R), 1) < R
    grads = jnp.concatenate(
        [jnp.where(low_half, grads[2 * i], grads[2 * i + 1]) for i in range(R // 2)], axis=1
    ).astype(jnp.bfloat16)

    def against(ref):
        return lax.dot_general(ref[...], grads, NT, preferred_element_type=jnp.float32)

    def put(kth, block):
        at = pl.multiple_of(place_ref[kth] * PANEL, PANEL)
        out_ref[0, :, pl.ds(at, PANEL)] = jnp.transpose(block)

    put(0, against(panel_refs[0]))
    put(1, against(panel_refs[1]))
    mine = place_ref[4]
    for kth in (2, 3):
        parts = [against(ref) for ref in panel_refs[4 * kth - 6:4 * kth - 2]]
        ordered = []
        for quarter in range(4):
            turn = mine ^ quarter
            ordered.append(jnp.where(turn == 0, parts[0], jnp.where(
                turn == 1, parts[1], jnp.where(turn == 2, parts[2], parts[3]))))
        put(kth, jnp.concatenate(ordered, axis=0))


def score(place, arrived, member, panels):
    smem = pl.BlockSpec(memory_space=pltpu.SMEM)
    vmem = pl.BlockSpec(memory_space=pltpu.VMEM)
    return pl.pallas_call(
        score_kernel,
        out_shape=jax.ShapeDtypeStruct((1, DOC_OWN, 4 * PANEL), jnp.float32),
        in_specs=[smem] + [vmem] * (2 + len(panels)),
        out_specs=vmem,
        compiler_params=pltpu.CompilerParams(vmem_limit_bytes=56 << 20),
        name="score",
    )(place, arrived, member, *panels)


def hop(fn):
    pairs = []
    for z in range(8):
        for y in range(4):
            for x in range(4):
                for core in range(2):
                    at = []
                    for c in ((z, y, x, core), fn(z, y, x, core)):
                        at.append((((c[0] * 4 + c[1]) * 2 + c[2] % 2) * 2 + c[2] // 2) * 2 + c[3])
                    pairs.append(tuple(at))
    return pairs


TO_CORE = hop(lambda z, y, x, core: (z, y, x, 1 - core))
TO_CROSS = hop(lambda z, y, x, core: (z, y, 3 - x, core))
TO_X = hop(lambda z, y, x, core: (z, y, x ^ 1, core))
TO_Y = hop(lambda z, y, x, core: (z, y ^ 1, x, core))
TO_Z = hop(lambda z, y, x, core: (z ^ 1, y, x, core))


def send(value, pairs):
    return lax.ppermute(value, ("docs", "query"), pairs)


def shards(
    activations, out_grads, proj_in, proj_out, panels, lengths, piece_owner, doc_slot, panel_order
):
    docs_at = lax.axis_index("docs")
    query_at = lax.axis_index("query")
    quarter = (docs_at & 1) ^ (2 * ((docs_at >> 1) & 1)) ^ (3 * ((docs_at >> 3) & 1))

    across = send(lax.dynamic_slice_in_dim(panels, (quarter ^ 1) * QUART, QUART, 0), TO_CROSS)
    packed, member = project(
        activations, out_grads, proj_in, proj_out,
        lengths[0], piece_owner[0], doc_slot[0].reshape(1, DOCS),
    )
    across, panels, _ = lax.optimization_barrier((across, panels, packed))
    beside = send(panels, TO_CORE)
    parts = [across] + [send(across, to) for to in (TO_X, TO_Y, TO_Z)]
    parts_beside = [send(part, TO_CORE) for part in parts]
    arrived = lax.all_to_all(
        packed.reshape(DOCS, CAP, 2 * R), "docs", split_axis=0, concat_axis=0, tiled=True
    ).reshape(ROWS, 2 * R)

    order = panel_order[0]
    held = query_at ^ jnp.arange(4, dtype=jnp.int32)
    place = jnp.sum((order[None, :] == held[:, None]) * jnp.arange(4, dtype=jnp.int32), axis=1)
    place = jnp.concatenate([place.astype(jnp.int32), quarter.reshape(1).astype(jnp.int32)])
    return score(place, arrived, member, [panels, beside] + parts + parts_beside)


def solution(mesh):
    placed = (
        P("query", "docs", None),
        P("query", "docs", None),
        P(),
        P(),
        P("query", None),
        P("query", "docs", None),
        P("query", "docs", None),
        P("query", None, "docs"),
        P("docs", None),
    )
    return jax.shard_map(
        shards, mesh=mesh, in_specs=placed, out_specs=P("query", "docs", None), check_vma=False
    )
```

time: 171 us -> 42.5 us (0.25)
  waiting for transfers between devices: 108 us -> 6.88 us
  between operations: 16 us -> 0.14 us
  matrix products: 13.3 us -> 0 us
  Pallas kernels: 0 us -> 10.2 us
  local copies, waits for them, and re-layouts: 10.4 us -> 1.99 us
  other arithmetic: 9.1 us -> 0.77 us
  starting transfers between devices: 14 us -> 21.7 us
    psum x1 -> x0, waiting for transfers between devices: 65.8 us -> none  [from_root(): return lax.psum(kept, axis)]
    all_to_all x1, waiting for transfers between devices: 42.1 us -> 6.86 us  [shards(): lax.all_to_all(packed.reshape(DOCS, CAP, 2 * R), 'docs', split_axis=0, co...]
    dot_general x7 -> x0, matrix products: 13.3 us -> none  [the longest x4 4.13 us: against_panel(): lax.dot_general(grads_now, panel_now, (((1,), (1,)), ((), ())), preferred...]
    pallas_call x0 -> x2, Pallas kernels: none -> 10.2 us  [the longest x1 5.79 us: project(): pl.pallas_call(project_kernel, out_shape=(jax.ShapeDtypeStruct((ROWS, 2 *...]
    ppermute x0 -> x9, starting transfers between devices: none -> 9.89 us  [send(): return lax.ppermute(value, ('docs', 'query'), pairs)]
    convert_element_type x1 -> x0, local copies, waits for them, and re-layouts: 7.12 us -> none  [outer_rows(): return product.reshape(lead + (width * width,)).astype(jnp.bfloat16)]
    convert_element_type x3 -> x0, other arithmetic: 4.39 us -> none  [the longest x1 4.28 us: outer_rows(): return product.reshape(lead + (width * width,)).astype(jnp.bfloat16)]
    select_n x4 -> x0, other arithmetic: 2.31 us -> none  [the longest x1 2.02 us: from_root(): jnp.where(lax.axis_index(axis) == source, value, 0).astype(value.dtype)]
  transfers between devices with their start and end apart: 2 -> 10, of which waited for: 2 -> 1; matrix products, arithmetic and copies ran while one was open for 4% -> 2% of each run, Pallas kernels for 0% -> 14%
where the time goes in v1:
time: 42.5 us; the launch traced here: 41.7 us
  starting transfers between devices  21.7 us (51%)
  Pallas kernels  10.2 us (24%)
  waiting for transfers between devices  6.88 us (16%)
  local copies, waits for them, and re-layouts  1.99 us (5%)
  other arithmetic  0.77 us (2%)
    all_to_all x1, starting transfers between devices, shards(): lax.all_to_all(packed.reshape(DOCS, CAP, 2 * R), 'docs', split_axis=0, co...  11.8 us
    ppermute x9, starting transfers between devices, send(): return lax.ppermute(value, ('docs', 'query'), pairs)  9.89 us
    all_to_all x1, waiting for transfers between devices, shards(): lax.all_to_all(packed.reshape(DOCS, CAP, 2 * R), 'docs', split_axis=0, co...  6.86 us
    pallas_call x1, Pallas kernels, project(): pl.pallas_call(project_kernel, out_shape=(jax.ShapeDtypeStruct((ROWS, 2 *...  5.79 us
    pallas_call x1, Pallas kernels, score(): pl.pallas_call(score_kernel, out_shape=jax.ShapeDtypeStruct((1, DOC_OWN,...  4.43 us
    unnamed x18, local copies, waits for them, and re-layouts  1.02 us
    dynamic_slice x1, local copies, waits for them, and re-layouts, shards(): lax.dynamic_slice_in_dim(panels, (quarter ^ 1) * QUART, QUART, 0)  0.97 us
  transfers between devices with their start and end apart: 10, of which 1 were waited for; matrix products, arithmetic and copies ran while one was open for 2% of the time, Pallas kernels for 14%

profile of v1, /device:TPU:1, one launch (start us, length us, event | category | flops | bytes accessed | tf_op | source)
XLA Modules:
  0.0 41.7 jit_solution(16891855103191017901)
XLA Ops:
  0.0 1.0 %constant_dynamic-slice_fusion = bf16[32,4096]{1,0:T(8,128)(2,1)S(1)} fusion(bf16[128,4096]{1,0:T(8,128)(2,1)} %refs_0_, s32[]{:T(128)S(6)} %select_n.3), kind=kLoop, calls=%fused_computation.3 | loop fusion | bytes 524292 | tf_op jit(solution)/shard_map/dynamic_slice | solution.py:182
  1.0 0.0 copy-start
  1.0 0.0 copy-start.8
  1.0 3.4 %collective-permute-start = (bf16[32,4096]{1,0:T(8,128)(2,1)S(1)}, bf16[32,4096]{1,0:T(8,128)(2,1)S(1)}, u32[]{:S(2)}, u32[]{:S(2)}) collective-permute-start(bf16[32,4096]{1,0:T(8,128)(2,1)S(1)} %constant_dynamic-slice_fusion), channel_id=1, source_target_pairs={{0,6},{1,7},{4,2},{5,3},{2,4},{3,5},{6,0},{7,1},{8,14},{9,15},{12,... | collective-permute-start | bytes 786440 | tf_op jit(solution)/shard_map/ppermute | solution.py:172
  4.4 5.8 %project.1 = (bf16[256,128]{1,0:T(8,128)(2,1)}, f32[8,256]{1,0:T(8,128)}) custom-call(bf16[1,128,4096]{2,1,0:T(8,128)(2,1)} %act_hbm.1, bf16[1,128,14336]{2,1,0:T(8,128)(2,1)} %grad_hbm.1, bf16[64,4096]{1,0:T(8,128)(2,1)} %bitcast.10, bf16[64,14336]{1,0:T(8,128)(2,1)} %bitcast.9, s32[1,64]{1,0:T(1,128)} %bitcast.13, s32[1,64]{1,0:T(1,128)} %bitcast.14, ...), custom_call_target="tpu_custom_call" | custom-call | flops 301989888 | bytes 7077888 | tf_op jit(solution)/shard_map/project/pallas_call | solution.py:74
  10.2 0.0 collective-permute-done.refs_2_
  10.2 0.0 copy-start.3
  10.2 0.0 copy-done
  10.2 1.7 %collective-permute-start.1 = (bf16[128,4096]{1,0:T(8,128)(2,1)S(1)}, bf16[128,4096]{1,0:T(8,128)(2,1)S(1)}, u32[]{:S(2)}, u32[]{:S(2)}) collective-permute-start(bf16[128,4096]{1,0:T(8,128)(2,1)S(1)} %copy-done), channel_id=1, source_target_pairs={{0,1},{1,0},{4,5},{5,4},{2,3},{3,2},{6,7},{7,6},{8,9},{9,8},{12,13... | collective-permute-start | bytes 3145736 | tf_op jit(solution)/shard_map/ppermute | solution.py:172
  11.9 1.6 %collective-permute-start.4 = (bf16[32,4096]{1,0:T(8,128)(2,1)S(1)}, bf16[32,4096]{1,0:T(8,128)(2,1)S(1)}, u32[]{:S(2)}, u32[]{:S(2)}) collective-permute-start(bf16[32,4096]{1,0:T(8,128)(2,1)S(1)} %collective-permute-done.refs_2_), channel_id=1, source_target_pairs={{0,32},{1,33},{4,36},{5,37},{2,34},{3,35},{6,38},{7,39},{8,40},{9,... | collective-permute-start | bytes 786440 | tf_op jit(solution)/shard_map/ppermute | solution.py:172
  13.5 1.3 %collective-permute-start.3 = (bf16[32,4096]{1,0:T(8,128)(2,1)S(1)}, bf16[32,4096]{1,0:T(8,128)(2,1)S(1)}, u32[]{:S(2)}, u32[]{:S(2)}) collective-permute-start(bf16[32,4096]{1,0:T(8,128)(2,1)S(1)} %collective-permute-done.refs_2_), channel_id=1, source_target_pairs={{0,8},{1,9},{4,12},{5,13},{2,10},{3,11},{6,14},{7,15},{8,0},{9,1},... | collective-permute-start | bytes 786440 | tf_op jit(solution)/shard_map/ppermute | solution.py:172
  14.8 0.0 collective-permute-start.2
  14.8 11.8 %all-to-all-start = ((bf16[64,4,128]{2,1,0:T(4,128)(2,1)}), bf16[64,4,128]{2,1,0:T(4,128)(2,1)S(1)}, u32[]{:S(2)}, u32[]{:S(2)}) async-start(bf16[64,4,128]{2,1,0:T(4,128)(2,1)} %bitcast.12), calls=%async_computation | async-start | bytes 131072 | tf_op jit(solution)/shard_map/all_to_all | solution.py:191
  26.6 1.3 %collective-permute-start.5 = (bf16[32,4096]{1,0:T(8,128)(2,1)S(1)}, bf16[32,4096]{1,0:T(8,128)(2,1)S(1)}, u32[]{:S(2)}, u32[]{:S(2)}) collective-permute-start(bf16[32,4096]{1,0:T(8,128)(2,1)S(1)} %collective-permute-done.refs_2_), channel_id=1, source_target_pairs={{0,1},{1,0},{4,5},{5,4},{2,3},{3,2},{6,7},{7,6},{8,9},{9,8},{12,13... | collective-permute-start | bytes 786440 | tf_op jit(solution)/shard_map/ppermute | solution.py:172
  27.9 0.0 collective-permute-done.4.refs_5_
  27.9 0.0 copy-start.4
  27.9 0.1 collective-permute-start.8
  28.0 0.0 collective-permute-done.3.refs_4_
  28.0 0.0 copy-start.5
  28.0 0.4 collective-permute-start.7
  28.4 0.0 collective-permute-done.2.refs_3_
  28.4 0.0 copy-start.6
  28.4 0.1 collective-permute-start.6
  28.6 0.0 copy-done.8
  28.6 0.2 select_reduce_fusion
  28.7 0.6 %pad_add_fusion.place_ref = s32[5]{0:T(128)} fusion(s32[1]{0:T(128)} %bitcast.1, s32[4]{0:T(128)S(1)} %select_reduce_fusion), kind=kLoop, calls=%fused_computation.1 | loop fusion | flops 5 | bytes 40 | tf_op jit(solution)/shard_map/concatenate | solution.py:198
  29.3 6.9 %all-to-all-done = bf16[64,4,128]{2,1,0:T(4,128)(2,1)S(1)} async-done(((bf16[64,4,128]{2,1,0:T(4,128)(2,1)}), bf16[64,4,128]{2,1,0:T(4,128)(2,1)S(1)}, u32[]{:S(2)}, u32[]{:S(2)}) %all-to-all-start) | async-done | bytes 65568 | tf_op jit(solution)/shard_map/all_to_all | solution.py:191
  36.2 0.0 copy-start.2
  36.2 0.0 collective-permute-done.5.refs_6_
  36.2 0.0 copy-start.7
  36.2 0.0 collective-permute-done.8.refs_9_
  36.2 0.0 collective-permute-done.7.refs_8_
  36.2 0.0 collective-permute-done.6.refs_7_
  36.2 0.0 collective-permute-done.1.refs_1_
  36.2 0.0 copy-start.1
  36.2 0.0 copy-done.3
  36.2 0.0 copy-done.4
  36.3 0.0 copy-done.5
  36.3 0.0 copy-done.6
  36.3 0.5 %copy-done.2 = bf16[64,4,128]{2,1,0:T(4,128)(2,1)} copy-done((bf16[64,4,128]{2,1,0:T(4,128)(2,1)}, bf16[64,4,128]{2,1,0:T(4,128)(2,1)S(1)}, u32[]{:S(2)}) %copy-start.2) | copy-done | bytes 65560
  36.8 0.1 copy-done.7
  36.9 0.4 copy-done.1
  37.3 4.4 %score.1 = f32[1,8,512]{2,1,0:T(8,128)} custom-call(s32[5]{0:T(128)} %pad_add_fusion.place_ref, bf16[256,128]{1,0:T(8,128)(2,1)} %bitcast.11, f32[8,256]{1,0:T(8,128)} %get-tuple-element.10.member_ref, bf16[128,4096]{1,0:T(8,128)(2,1)} %refs_0_, bf16[128,4096]{1,0:T(8,128)(2,1)} %copy-done.1, bf16[32,4096]{1,0:T(8,128)(2,1)} %copy-done.3, ...), custom_call_target="tpu_custom_call" | custom-call | tf_op jit(solution)/shard_map/score/pallas_call | solution.py:141
  (1 shorter events, 0.0 us)
Async XLA Ops:
  1.0 9.2 %copy-start = (bf16[128,4096]{1,0:T(8,128)(2,1)S(1)}, bf16[128,4096]{1,0:T(8,128)(2,1)}, u32[]{:S(2)}) copy-start(bf16[128,4096]{1,0:T(8,128)(2,1)} %refs_0_) | copy-start | bytes 3145732
  1.0 27.6 %copy-start.8 = (s32[1,4]{1,0:T(1,128)S(1)}, s32[1,4]{1,0:T(1,128)}, u32[]{:S(2)}) copy-start(s32[1,4]{1,0:T(1,128)} %param.17) | copy-start | bytes 52
  1.0 9.2 %collective-permute-start = (bf16[32,4096]{1,0:T(8,128)(2,1)S(1)}, bf16[32,4096]{1,0:T(8,128)(2,1)S(1)}, u32[]{:S(2)}, u32[]{:S(2)}) collective-permute-start(bf16[32,4096]{1,0:T(8,128)(2,1)S(1)} %constant_dynamic-slice_fusion), channel_id=1, source_target_pairs={{0,6},{1,7},{4,2},{5,3},{2,4},{3,5},{6,0},{7,1},{8,14},{9,15},{12,... | collective-permute-start | bytes 786440 | tf_op jit(solution)/shard_map/ppermute | solution.py:172
  10.2 26.0 %copy-start.3 = (bf16[32,4096]{1,0:T(8,128)(2,1)}, bf16[32,4096]{1,0:T(8,128)(2,1)S(1)}, u32[]{:S(2)}) copy-start(bf16[32,4096]{1,0:T(8,128)(2,1)S(1)} %collective-permute-done.refs_2_) | copy-start | bytes 786436
  10.2 26.0 %collective-permute-start.1 = (bf16[128,4096]{1,0:T(8,128)(2,1)S(1)}, bf16[128,4096]{1,0:T(8,128)(2,1)S(1)}, u32[]{:S(2)}, u32[]{:S(2)}) collective-permute-start(bf16[128,4096]{1,0:T(8,128)(2,1)S(1)} %copy-done), channel_id=1, source_target_pairs={{0,1},{1,0},{4,5},{5,4},{2,3},{3,2},{6,7},{7,6},{8,9},{9,8},{12,13... | collective-permute-start | bytes 3145736 | tf_op jit(solution)/shard_map/ppermute | solution.py:172
  11.9 16.0 %collective-permute-start.4 = (bf16[32,4096]{1,0:T(8,128)(2,1)S(1)}, bf16[32,4096]{1,0:T(8,128)(2,1)S(1)}, u32[]{:S(2)}, u32[]{:S(2)}) collective-permute-start(bf16[32,4096]{1,0:T(8,128)(2,1)S(1)} %collective-permute-done.refs_2_), channel_id=1, source_target_pairs={{0,32},{1,33},{4,36},{5,37},{2,34},{3,35},{6,38},{7,39},{8,40},{9,... | collective-permute-start | bytes 786440 | tf_op jit(solution)/shard_map/ppermute | solution.py:172
  13.5 14.5 %collective-permute-start.3 = (bf16[32,4096]{1,0:T(8,128)(2,1)S(1)}, bf16[32,4096]{1,0:T(8,128)(2,1)S(1)}, u32[]{:S(2)}, u32[]{:S(2)}) collective-permute-start(bf16[32,4096]{1,0:T(8,128)(2,1)S(1)} %collective-permute-done.refs_2_), channel_id=1, source_target_pairs={{0,8},{1,9},{4,12},{5,13},{2,10},{3,11},{6,14},{7,15},{8,0},{9,1},... | collective-permute-start | bytes 786440 | tf_op jit(solution)/shard_map/ppermute | solution.py:172
  14.8 13.6 %collective-permute-start.2 = (bf16[32,4096]{1,0:T(8,128)(2,1)S(1)}, bf16[32,4096]{1,0:T(8,128)(2,1)S(1)}, u32[]{:S(2)}, u32[]{:S(2)}) collective-permute-start(bf16[32,4096]{1,0:T(8,128)(2,1)S(1)} %collective-permute-done.refs_2_), channel_id=1, source_target_pairs={{0,4},{1,5},{4,0},{5,1},{2,6},{3,7},{6,2},{7,3},{8,12},{9,13},{12,... | collective-permute-start | bytes 786440 | tf_op jit(solution)/shard_map/ppermute | solution.py:172
  14.8 21.4 %all-to-all-start = ((bf16[64,4,128]{2,1,0:T(4,128)(2,1)}), bf16[64,4,128]{2,1,0:T(4,128)(2,1)S(1)}, u32[]{:S(2)}, u32[]{:S(2)}) async-start(bf16[64,4,128]{2,1,0:T(4,128)(2,1)} %bitcast.12), calls=%async_computation | async-start | bytes 131072 | tf_op jit(solution)/shard_map/all_to_all | solution.py:191
  26.6 9.6 %collective-permute-start.5 = (bf16[32,4096]{1,0:T(8,128)(2,1)S(1)}, bf16[32,4096]{1,0:T(8,128)(2,1)S(1)}, u32[]{:S(2)}, u32[]{:S(2)}) collective-permute-start(bf16[32,4096]{1,0:T(8,128)(2,1)S(1)} %collective-permute-done.refs_2_), channel_id=1, source_target_pairs={{0,1},{1,0},{4,5},{5,4},{2,3},{3,2},{6,7},{7,6},{8,9},{9,8},{12,13... | collective-permute-start | bytes 786440 | tf_op jit(solution)/shard_map/ppermute | solution.py:172
  27.9 8.3 %copy-start.4 = (bf16[32,4096]{1,0:T(8,128)(2,1)}, bf16[32,4096]{1,0:T(8,128)(2,1)S(1)}, u32[]{:S(2)}) copy-start(bf16[32,4096]{1,0:T(8,128)(2,1)S(1)} %collective-permute-done.4.refs_5_) | copy-start | bytes 786436
  27.9 8.3 %collective-permute-start.8 = (bf16[32,4096]{1,0:T(8,128)(2,1)S(1)}, bf16[32,4096]{1,0:T(8,128)(2,1)}, u32[]{:S(2)}, u32[]{:S(2)}) collective-permute-start(bf16[32,4096]{1,0:T(8,128)(2,1)S(1)} %collective-permute-done.4.refs_5_), channel_id=1, source_target_pairs={{0,1},{1,0},{4,5},{5,4},{2,3},{3,2},{6,7},{7,6},{8,9},{9,8},{12,13... | collective-permute-start | bytes 786440 | tf_op jit(solution)/shard_map/ppermute | solution.py:172
  28.0 8.2 %copy-start.5 = (bf16[32,4096]{1,0:T(8,128)(2,1)}, bf16[32,4096]{1,0:T(8,128)(2,1)S(1)}, u32[]{:S(2)}) copy-start(bf16[32,4096]{1,0:T(8,128)(2,1)S(1)} %collective-permute-done.3.refs_4_) | copy-start | bytes 786436
  28.0 8.2 %collective-permute-start.7 = (bf16[32,4096]{1,0:T(8,128)(2,1)S(1)}, bf16[32,4096]{1,0:T(8,128)(2,1)}, u32[]{:S(2)}, u32[]{:S(2)}) collective-permute-start(bf16[32,4096]{1,0:T(8,128)(2,1)S(1)} %collective-permute-done.3.refs_4_), channel_id=1, source_target_pairs={{0,1},{1,0},{4,5},{5,4},{2,3},{3,2},{6,7},{7,6},{8,9},{9,8},{12,13... | collective-permute-start | bytes 786440 | tf_op jit(solution)/shard_map/ppermute | solution.py:172
  28.4 7.8 %copy-start.6 = (bf16[32,4096]{1,0:T(8,128)(2,1)}, bf16[32,4096]{1,0:T(8,128)(2,1)S(1)}, u32[]{:S(2)}) copy-start(bf16[32,4096]{1,0:T(8,128)(2,1)S(1)} %collective-permute-done.2.refs_3_) | copy-start | bytes 786436
  28.4 7.8 %collective-permute-start.6 = (bf16[32,4096]{1,0:T(8,128)(2,1)S(1)}, bf16[32,4096]{1,0:T(8,128)(2,1)}, u32[]{:S(2)}, u32[]{:S(2)}) collective-permute-start(bf16[32,4096]{1,0:T(8,128)(2,1)S(1)} %collective-permute-done.2.refs_3_), channel_id=1, source_target_pairs={{0,1},{1,0},{4,5},{5,4},{2,3},{3,2},{6,7},{7,6},{8,9},{9,8},{12,13... | collective-permute-start | bytes 786440 | tf_op jit(solution)/shard_map/ppermute | solution.py:172
  36.2 0.6 %copy-start.2 = (bf16[64,4,128]{2,1,0:T(4,128)(2,1)}, bf16[64,4,128]{2,1,0:T(4,128)(2,1)S(1)}, u32[]{:S(2)}) copy-start(bf16[64,4,128]{2,1,0:T(4,128)(2,1)S(1)} %all-to-all-done) | copy-start | bytes 196612
  36.2 0.7 %copy-start.7 = (bf16[32,4096]{1,0:T(8,128)(2,1)}, bf16[32,4096]{1,0:T(8,128)(2,1)S(1)}, u32[]{:S(2)}) copy-start(bf16[32,4096]{1,0:T(8,128)(2,1)S(1)} %collective-permute-done.5.refs_6_) | copy-start | bytes 786436
  36.2 1.0 %copy-start.1 = (bf16[128,4096]{1,0:T(8,128)(2,1)}, bf16[128,4096]{1,0:T(8,128)(2,1)S(1)}, u32[]{:S(2)}) copy-start(bf16[128,4096]{1,0:T(8,128)(2,1)S(1)} %collective-permute-done.1.refs_1_) | copy-start | bytes 3145732

commit v2 on v1

v2 whole, which is shorter than its diff:
```python
import jax
import jax.numpy as jnp
from jax import lax
from jax.experimental import pallas as pl
from jax.experimental.pallas import tpu as pltpu
from jax.sharding import PartitionSpec as P

DOC_OWN = 8
R = 64
CAP = 4
DOCS = 64
TOK = 128
ROWS = DOCS * CAP
PANEL = 128
QUART = PANEL // 4
NT = (((1,), (1,)), ((), ()))


ACT_STEPS = (4096,)
GRAD_STEPS = (7168, 4096, 3072)


def project_kernel(act_hbm, grad_hbm, win_hbm, wout_hbm, len_hbm, own_hbm, panel_hbm,
                   rows_ref, quarter_ref, act_v, grad_v, win_v, wout_v, len_ref, own_ref, sems):
    jobs = []
    for x_hbm, w_hbm, x_v, w_v, sizes in (
        (act_hbm, win_hbm, act_v, win_v, ACT_STEPS),
        (grad_hbm, wout_hbm, grad_v, wout_v, GRAD_STEPS),
    ):
        at = 0
        for size in sizes:
            cols = pl.ds(at, size)
            n = 2 * len(jobs)
            copies = (
                pltpu.make_async_copy(w_hbm.at[:, cols], w_v.at[:, cols], sems.at[n]),
                pltpu.make_async_copy(x_hbm.at[0, :, cols], x_v.at[:, cols], sems.at[n + 1]),
            )
            for copy in copies:
                copy.start()
            jobs.append((copies, x_v, w_v, cols))
            at += size
    ints = (
        pltpu.make_async_copy(len_hbm, len_ref, sems.at[2 * len(jobs)]),
        pltpu.make_async_copy(own_hbm, own_ref, sems.at[2 * len(jobs) + 1]),
    )
    for copy in ints:
        copy.start()
    given = pl.multiple_of((quarter_of(lax.axis_index("docs")) ^ 1) * QUART, QUART)
    given = pltpu.make_async_copy(
        panel_hbm.at[pl.ds(given, QUART)], quarter_ref, sems.at[2 * len(jobs) + 2]
    )
    given.start()

    def low_part(job):
        copies, x_v, w_v, cols = job
        for copy in copies:
            copy.wait()
        return lax.dot_general(x_v[:, cols], w_v[:, cols], NT, preferred_element_type=jnp.float32)

    act_low = sum(low_part(job) for job in jobs[:len(ACT_STEPS)])

    for copy in ints:
        copy.wait()
    lens = len_ref[...].astype(jnp.float32)
    owners = own_ref[...].astype(jnp.float32)
    one = lax.broadcasted_iota(jnp.int32, (DOCS, DOCS), 0)
    other = lax.broadcasted_iota(jnp.int32, (DOCS, DOCS), 1)
    start = jnp.sum(jnp.where(other < one, lens, 0.0), axis=1, keepdims=True)
    size = jnp.sum(jnp.where(other == one, lens, 0.0), axis=1, keepdims=True)
    owner = jnp.sum(jnp.where(other == one, owners, 0.0), axis=1, keepdims=True)
    token = lax.broadcasted_iota(jnp.int32, (DOCS, TOK), 1).astype(jnp.float32)
    inside = (token >= start) & (token < start + size)
    goal = jnp.sum(jnp.where(inside, CAP * owner + token - start, 0.0), axis=0, keepdims=True)
    row = lax.broadcasted_iota(jnp.int32, (ROWS, TOK), 0).astype(jnp.float32)
    take = jnp.where(row == goal, 1.0, 0.0).astype(jnp.bfloat16)

    grad_low = sum(low_part(job) for job in jobs[len(ACT_STEPS):])
    rows = jnp.concatenate([grad_low, act_low], axis=1).astype(jnp.bfloat16)
    rows_ref[...] = jnp.dot(take, rows, preferred_element_type=jnp.float32).astype(jnp.bfloat16)
    given.wait()


def project(activations, out_grads, proj_in, proj_out, lengths, piece_owner, panels):
    width_in, width_out = activations.shape[-1], out_grads.shape[-1]
    hbm = pl.BlockSpec(memory_space=pltpu.HBM)
    vmem = pl.BlockSpec(memory_space=pltpu.VMEM)
    return pl.pallas_call(
        project_kernel,
        out_shape=(
            jax.ShapeDtypeStruct((ROWS, 2 * R), jnp.bfloat16),
            jax.ShapeDtypeStruct((QUART, panels.shape[1]), jnp.bfloat16),
        ),
        in_specs=[hbm] * 7,
        out_specs=(vmem, vmem),
        scratch_shapes=[
            pltpu.VMEM((TOK, width_in), jnp.bfloat16),
            pltpu.VMEM((TOK, width_out), jnp.bfloat16),
            pltpu.VMEM((R, width_in), jnp.bfloat16),
            pltpu.VMEM((R, width_out), jnp.bfloat16),
            pltpu.VMEM((1, DOCS), jnp.int32),
            pltpu.VMEM((1, DOCS), jnp.int32),
            pltpu.SemaphoreType.DMA((2 * len(ACT_STEPS + GRAD_STEPS) + 3,)),
        ],
        compiler_params=pltpu.CompilerParams(vmem_limit_bytes=56 << 20),
        cost_estimate=pl.CostEstimate(
            flops=2 * TOK * (width_in + width_out) * R,
            bytes_accessed=2 * (TOK + R) * (width_in + width_out),
            transcendentals=0,
        ),
        name="project",
    )(activations, out_grads, proj_in.T, proj_out.T, lengths, piece_owner, panels)


def call(kernel, out_shape, cost_us, in_specs, *given, **more):
    return pl.pallas_call(
        kernel,
        out_shape=out_shape,
        in_specs=in_specs,
        out_specs=pl.BlockSpec(memory_space=pltpu.VMEM),
        compiler_params=pltpu.CompilerParams(vmem_limit_bytes=16 << 20),
        cost_estimate=pl.CostEstimate(
            flops=cost_us * 10**9, bytes_accessed=cost_us * 10**6, transcendentals=0
        ),
        **more,
    )(*given)


def document_kernel(slot_ref, rows_ref, grads_ref):
    doc = lax.broadcasted_iota(jnp.int32, (DOC_OWN, DOCS), 0)
    mine = jnp.where(slot_ref[...] == doc, 1.0, 0.0).astype(jnp.bfloat16)
    source = lax.broadcasted_iota(jnp.int32, (DOCS, ROWS), 0)
    spread = jnp.where((lax.broadcasted_iota(jnp.int32, (DOCS, ROWS), 1) >> 2) == source, 1.0, 0.0)
    member = jnp.dot(mine, spread.astype(jnp.bfloat16), preferred_element_type=jnp.float32)

    rows = rows_ref[...]
    eye = (lax.broadcasted_iota(jnp.int32, (2 * R, 2 * R), 0)
           == lax.broadcasted_iota(jnp.int32, (2 * R, 2 * R), 1))
    eye = jnp.where(eye, 1.0, 0.0).astype(jnp.bfloat16)
    turned = lax.dot_general(eye, rows, NT, preferred_element_type=jnp.float32)
    masked = turned[:R][:, None, :] * member[None]
    masked = masked.reshape(R * DOC_OWN, ROWS).astype(jnp.bfloat16)
    wide = rows.astype(jnp.float32)
    lane = lax.broadcasted_iota(jnp.int32, (ROWS, 2 * R), 1)
    twice = jnp.where(lane < R, pltpu.roll(wide, R, 1), wide).astype(jnp.bfloat16)
    grads = jnp.dot(masked, twice, preferred_element_type=jnp.float32)
    grads = grads.reshape(R, DOC_OWN, 2 * R)
    low_half = lax.broadcasted_iota(jnp.int32, (DOC_OWN, 2 * R), 1) < R
    grads_ref[...] = jnp.concatenate(
        [jnp.where(low_half, grads[2 * i], grads[2 * i + 1]) for i in range(R // 2)], axis=1
    ).astype(jnp.bfloat16)


def against(panel_ref, grads):
    return lax.dot_general(panel_ref[...], grads, NT, preferred_element_type=jnp.float32)


def near_kernel(grads_ref, own_ref, beside_ref, out_ref):
    grads = grads_ref[...]
    out_ref[:, :PANEL] = jnp.transpose(against(own_ref, grads))
    out_ref[:, PANEL:] = jnp.transpose(against(beside_ref, grads))


def far_kernel(order_ref, grads_ref, near_ref, *refs):
    quarter_refs, out_ref, column_ref = refs[:-2], refs[-2], refs[-1]
    query_at = lax.axis_index("query")
    mine = quarter_of(lax.axis_index("docs"))
    grads = grads_ref[...]
    for n, ref in enumerate(quarter_refs):
        row = (n // 4) * PANEL + (mine ^ (n % 4)) * QUART
        column_ref[pl.ds(pl.multiple_of(row, QUART), QUART), :] = against(ref, grads)

    far = jnp.transpose(column_ref[...])
    blocks = [near_ref[:, :PANEL], near_ref[:, PANEL:], far[:, :PANEL], far[:, PANEL:]]
    for kth, block in enumerate(blocks):
        held = query_at ^ kth
        at = sum(jnp.where(order_ref[0, b] == held, b, 0) for b in range(1, 4)) * PANEL
        out_ref[0, :, pl.ds(pl.multiple_of(at, PANEL), PANEL)] = block


def quarter_of(docs_at):
    return (docs_at & 1) ^ (2 * ((docs_at >> 1) & 1)) ^ (3 * ((docs_at >> 3) & 1))


def hop(fn):
    pairs = []
    for z in range(8):
        for y in range(4):
            for x in range(4):
                for core in range(2):
                    at = []
                    for c in ((z, y, x, core), fn(z, y, x, core)):
                        at.append((((c[0] * 4 + c[1]) * 2 + c[2] % 2) * 2 + c[2] // 2) * 2 + c[3])
                    pairs.append(tuple(at))
    return pairs


TO_CORE = hop(lambda z, y, x, core: (z, y, x, 1 - core))
TO_CROSS = hop(lambda z, y, x, core: (z, y, 3 - x, core))
TO_X = hop(lambda z, y, x, core: (z, y, x ^ 1, core))
TO_Y = hop(lambda z, y, x, core: (z, y ^ 1, x, core))
TO_Z = hop(lambda z, y, x, core: (z ^ 1, y, x, core))


def send(value, pairs):
    return lax.ppermute(value, ("docs", "query"), pairs)


def shards(
    activations, out_grads, proj_in, proj_out, panels, lengths, piece_owner, doc_slot, panel_order
):
    smem = pl.BlockSpec(memory_space=pltpu.SMEM)
    vmem = pl.BlockSpec(memory_space=pltpu.VMEM)
    packed, given = project(
        activations, out_grads, proj_in, proj_out, lengths[0], piece_owner[0], panels
    )
    arrived = lax.all_to_all(
        packed.reshape(DOCS, CAP, 2 * R), "docs", split_axis=0, concat_axis=0, tiled=True
    ).reshape(ROWS, 2 * R)

    beside = send(panels, TO_CORE)
    across = send(given, TO_CROSS)
    parts = [across] + [send(across, to) for to in (TO_X, TO_Y, TO_Z)]
    parts_beside = [send(part, TO_CORE) for part in parts]

    grads = call(
        document_kernel, jax.ShapeDtypeStruct((DOC_OWN, R * R), jnp.bfloat16), 10,
        [vmem] * 2, doc_slot[0].reshape(1, DOCS), arrived, name="documents",
    )
    near = call(
        near_kernel, jax.ShapeDtypeStruct((DOC_OWN, 2 * PANEL), jnp.float32), 10,
        [vmem] * 3, grads, panels, beside, name="near",
    )
    return call(
        far_kernel, jax.ShapeDtypeStruct((1, DOC_OWN, 4 * PANEL), jnp.float32), 10,
        [smem] + [vmem] * 10, panel_order, grads, near, *parts, *parts_beside, name="far",
        scratch_shapes=[pltpu.VMEM((2 * PANEL, DOC_OWN), jnp.float32)],
    )


def solution(mesh):
    placed = (
        P("query", "docs", None),
        P("query", "docs", None),
        P(),
        P(),
        P("query", None),
        P("query", "docs", None),
        P("query", "docs", None),
        P("query", None, "docs"),
        P("docs", None),
    )
    return jax.shard_map(
        shards, mesh=mesh, in_specs=placed, out_specs=P("query", "docs", None), check_vma=False
    )
```

time: 42.5 us -> 37.6 us (0.88); the launches traced: 41.7 us -> 37.5 us
  local copies, waits for them, and re-layouts: 1.99 us -> 0.01 us
  Pallas kernels: 10.2 us -> 8.56 us
  starting transfers between devices: 21.7 us -> 23.3 us
  waiting for transfers between devices: 6.88 us -> 5.49 us
  other arithmetic: 0.77 us -> 0 us
    all_to_all x1, waiting for transfers between devices: 6.86 us -> 4.52 us  [shards(): lax.all_to_all(packed.reshape(DOCS, CAP, 2 * R), 'docs', split_axis=0, co...]
    ppermute x9, starting transfers between devices: 9.89 us -> 11.5 us  [send(): return lax.ppermute(value, ('docs', 'query'), pairs)]
    pallas_call x1 -> x3, Pallas kernels: 4.43 us -> 3.05 us  [call(): pl.pallas_call(kernel, out_shape=out_shape, in_specs=in_specs, out_specs=...]
    unnamed x18 -> x6, local copies, waits for them, and re-layouts: 1.02 us -> 0.01 us
    dynamic_slice x1 -> x0, local copies, waits for them, and re-layouts: 0.97 us -> none  [shards(): lax.dynamic_slice_in_dim(panels, (quarter ^ 1) * QUART, QUART, 0)]
    ppermute x9, waiting for transfers between devices: 0.02 us -> 0.97 us  [send(): return lax.ppermute(value, ('docs', 'query'), pairs)]
    concatenate x1 -> x0, other arithmetic: 0.58 us -> none  [shards(): jnp.concatenate([place.astype(jnp.int32), quarter.reshape(1).astype(jnp.i...]
  transfers between devices with their start and end apart: 10 -> 10, of which waited for: 1 -> 4; matrix products, arithmetic and copies ran while one was open for 2% -> 0% of each run, Pallas kernels for 14% -> 3%
where the time goes in v2:
time: 37.6 us; the launch traced here: 37.5 us
  starting transfers between devices  23.3 us (62%)
  Pallas kernels  8.56 us (23%)
  waiting for transfers between devices  5.49 us (15%)
    all_to_all x1, starting transfers between devices, shards(): lax.all_to_all(packed.reshape(DOCS, CAP, 2 * R), 'docs', split_axis=0, co...  11.8 us
    ppermute x9, starting transfers between devices, send(): return lax.ppermute(value, ('docs', 'query'), pairs)  11.5 us
    pallas_call x1, Pallas kernels, project(): pl.pallas_call(project_kernel, out_shape=(jax.ShapeDtypeStruct((ROWS, 2 *...  5.51 us
    all_to_all x1, waiting for transfers between devices, shards(): lax.all_to_all(packed.reshape(DOCS, CAP, 2 * R), 'docs', split_axis=0, co...  4.52 us
    pallas_call x3, Pallas kernels, call(): pl.pallas_call(kernel, out_shape=out_shape, in_specs=in_specs, out_specs=...  3.05 us
    ppermute x9, waiting for transfers between devices, send(): return lax.ppermute(value, ('docs', 'query'), pairs)  0.97 us
  transfers between devices with their start and end apart: 10, of which 4 were waited for; matrix products, arithmetic and copies ran while one was open for 0% of the time, Pallas kernels for 3%

profile of v2, /device:TPU:1, one launch (start us, length us, event | category | flops | bytes accessed | tf_op | source)
XLA Modules:
  0.0 37.5 jit_solution(13750187178629742734)
XLA Ops:
  0.0 0.0 copy-start
  0.0 0.0 copy-start.1
  0.0 5.5 %project.1 = (bf16[256,128]{1,0:T(8,128)(2,1)}, bf16[32,4096]{1,0:T(8,128)(2,1)}) custom-call(bf16[1,128,4096]{2,1,0:T(8,128)(2,1)} %act_hbm.1, bf16[1,128,14336]{2,1,0:T(8,128)(2,1)} %grad_hbm.1, bf16[64,4096]{1,0:T(8,128)(2,1)} %bitcast.10, bf16[64,14336]{1,0:T(8,128)(2,1)} %bitcast.9, s32[1,64]{1,0:T(1,128)} %bitcast.12, s32[1,64]{1,0:T(1,128)} %bitcast.13, ...), custom_call_target="tpu_custom_call" | custom-call | flops 301989888 | bytes 7077888 | tf_op jit(solution)/shard_map/project/pallas_call | solution.py:87
  5.5 3.4 %collective-permute-start.1 = (bf16[32,4096]{1,0:T(8,128)(2,1)}, bf16[32,4096]{1,0:T(8,128)(2,1)S(1)}, u32[]{:S(2)}, u32[]{:S(2)}) collective-permute-start(bf16[32,4096]{1,0:T(8,128)(2,1)} %get-tuple-element.8), channel_id=1, source_target_pairs={{0,6},{1,7},{4,2},{5,3},{2,4},{3,5},{6,0},{7,1},{8,14},{9,15},{12,... | collective-permute-start | bytes 786440 | tf_op jit(solution)/shard_map/ppermute | solution.py:205
  8.9 11.8 %all-to-all-start = ((bf16[64,4,128]{2,1,0:T(4,128)(2,1)}), bf16[64,4,128]{2,1,0:T(4,128)(2,1)S(1)}, u32[]{:S(2)}, u32[]{:S(2)}) async-start(bf16[64,4,128]{2,1,0:T(4,128)(2,1)} %bitcast.11), calls=%async_computation | async-start | bytes 131072 | tf_op jit(solution)/shard_map/all_to_all | solution.py:216
  20.8 0.0 copy-done
  20.8 1.3 %collective-permute-start = (bf16[128,4096]{1,0:T(8,128)(2,1)S(1)}, bf16[128,4096]{1,0:T(8,128)(2,1)S(1)}, u32[]{:S(2)}, u32[]{:S(2)}) collective-permute-start(bf16[128,4096]{1,0:T(8,128)(2,1)S(1)} %copy-done), channel_id=1, source_target_pairs={{0,1},{1,0},{4,5},{5,4},{2,3},{3,2},{6,7},{7,6},{8,9},{9,8},{12,13... | collective-permute-start | bytes 3145736 | tf_op jit(solution)/shard_map/ppermute | solution.py:205
  22.1 0.0 collective-permute-done.1.refs_0_
  22.1 1.3 %collective-permute-start.2 = (bf16[32,4096]{1,0:T(8,128)(2,1)S(1)}, bf16[32,4096]{1,0:T(8,128)(2,1)S(1)}, u32[]{:S(2)}, u32[]{:S(2)}) collective-permute-start(bf16[32,4096]{1,0:T(8,128)(2,1)S(1)} %collective-permute-done.1.refs_0_), channel_id=1, source_target_pairs={{0,4},{1,5},{4,0},{5,1},{2,6},{3,7},{6,2},{7,3},{8,12},{9,13},{12,... | collective-permute-start | bytes 786440 | tf_op jit(solution)/shard_map/ppermute | solution.py:205
  23.4 1.2 %collective-permute-start.3 = (bf16[32,4096]{1,0:T(8,128)(2,1)S(1)}, bf16[32,4096]{1,0:T(8,128)(2,1)S(1)}, u32[]{:S(2)}, u32[]{:S(2)}) collective-permute-start(bf16[32,4096]{1,0:T(8,128)(2,1)S(1)} %collective-permute-done.1.refs_0_), channel_id=1, source_target_pairs={{0,8},{1,9},{4,12},{5,13},{2,10},{3,11},{6,14},{7,15},{8,0},{9,1},... | collective-permute-start | bytes 786440 | tf_op jit(solution)/shard_map/ppermute | solution.py:205
  24.6 1.2 %collective-permute-start.4 = (bf16[32,4096]{1,0:T(8,128)(2,1)S(1)}, bf16[32,4096]{1,0:T(8,128)(2,1)S(1)}, u32[]{:S(2)}, u32[]{:S(2)}) collective-permute-start(bf16[32,4096]{1,0:T(8,128)(2,1)S(1)} %collective-permute-done.1.refs_0_), channel_id=1, source_target_pairs={{0,32},{1,33},{4,36},{5,37},{2,34},{3,35},{6,38},{7,39},{8,40},{9,... | collective-permute-start | bytes 786440 | tf_op jit(solution)/shard_map/ppermute | solution.py:205
  25.8 4.5 %all-to-all-done = bf16[64,4,128]{2,1,0:T(4,128)(2,1)S(1)} async-done(((bf16[64,4,128]{2,1,0:T(4,128)(2,1)}), bf16[64,4,128]{2,1,0:T(4,128)(2,1)S(1)}, u32[]{:S(2)}, u32[]{:S(2)}) %all-to-all-start) | async-done | bytes 65568 | tf_op jit(solution)/shard_map/all_to_all | solution.py:216
  30.3 0.0 copy-done.1
  30.3 0.4 documents.1.grads_ref
  30.7 0.0 copy-start.2
  30.7 2.5 %collective-permute-start.5 = (bf16[32,4096]{1,0:T(8,128)(2,1)S(1)}, bf16[32,4096]{1,0:T(8,128)(2,1)S(1)}, u32[]{:S(2)}, u32[]{:S(2)}) collective-permute-start(bf16[32,4096]{1,0:T(8,128)(2,1)S(1)} %collective-permute-done.1.refs_0_), channel_id=1, source_target_pairs={{0,1},{1,0},{4,5},{5,4},{2,3},{3,2},{6,7},{7,6},{8,9},{9,8},{12,13... | collective-permute-start | bytes 786440 | tf_op jit(solution)/shard_map/ppermute | solution.py:205
  33.2 0.0 collective-permute-done.2.refs_1_
  33.2 0.1 collective-permute-start.6
  33.3 0.0 collective-permute-done.3.refs_2_
  33.3 0.4 %collective-permute-start.7 = (bf16[32,4096]{1,0:T(8,128)(2,1)S(1)}, bf16[32,4096]{1,0:T(8,128)(2,1)S(1)}, u32[]{:S(2)}, u32[]{:S(2)}) collective-permute-start(bf16[32,4096]{1,0:T(8,128)(2,1)S(1)} %collective-permute-done.3.refs_2_), channel_id=1, source_target_pairs={{0,1},{1,0},{4,5},{5,4},{2,3},{3,2},{6,7},{7,6},{8,9},{9,8},{12,13... | collective-permute-start | bytes 786440 | tf_op jit(solution)/shard_map/ppermute | solution.py:205
  33.7 0.0 collective-permute-done.4.refs_3_
  33.7 0.1 collective-permute-start.8
  33.8 0.0 collective-permute-done.beside_ref
  33.8 0.7 %near.1.near_ref = f32[8,256]{1,0:T(8,128)S(1)} custom-call(bf16[8,4096]{1,0:T(8,128)(2,1)S(1)} %documents.1.grads_ref, bf16[128,4096]{1,0:T(8,128)(2,1)S(1)} %copy-done, bf16[128,4096]{1,0:T(8,128)(2,1)S(1)} %collective-permute-done.beside_ref), custom_call_target="tpu_custom_call" | custom-call | flops 10000000000 | bytes 10000000 | tf_op jit(solution)/shard_map/near/pallas_call | solution.py:115
  34.5 0.0 collective-permute-done.5.refs_4_
  34.5 0.2 collective-permute-done.6.refs_5_
  34.7 0.4 collective-permute-done.7.refs_6_
  35.1 0.4 %collective-permute-done.8.refs_7_ = bf16[32,4096]{1,0:T(8,128)(2,1)S(1)} collective-permute-done((bf16[32,4096]{1,0:T(8,128)(2,1)S(1)}, bf16[32,4096]{1,0:T(8,128)(2,1)S(1)}, u32[]{:S(2)}, u32[]{:S(2)}) %collective-permute-start.8) | collective-permute-done | bytes 262176 | tf_op jit(solution)/shard_map/ppermute | solution.py:205
  35.5 0.0 copy-done.2
  35.5 2.0 %far.1 = f32[1,8,512]{2,1,0:T(8,128)} custom-call(s32[1,4]{1,0:T(1,128)S(1)} %copy-done.2, bf16[8,4096]{1,0:T(8,128)(2,1)S(1)} %documents.1.grads_ref, f32[8,256]{1,0:T(8,128)S(1)} %near.1.near_ref, bf16[32,4096]{1,0:T(8,128)(2,1)S(1)} %collective-permute-done.1.refs_0_, bf16[32,4096]{1,0:T(8,128)(2,1)S(1)} %collective-permute-done.2.refs_1_, ...), custom_call_target="tpu_custom_call" | custom-call | flops 10000000000 | bytes 10000000 | tf_op jit(solution)/shard_map/far/pallas_call | solution.py:115
Async XLA Ops:
  0.0 20.8 %copy-start = (bf16[128,4096]{1,0:T(8,128)(2,1)S(1)}, bf16[128,4096]{1,0:T(8,128)(2,1)}, u32[]{:S(2)}) copy-start(bf16[128,4096]{1,0:T(8,128)(2,1)} %own_ref.1) | copy-start | bytes 3145732
  0.0 30.3 %copy-start.1 = (s32[1,64,1]{1,2,0:T(1,128)S(1)}, s32[1,64,1]{1,2,0:T(1,128)}, u32[]{:S(2)}) copy-start(s32[1,64,1]{1,2,0:T(1,128)} %param.16) | copy-start | bytes 772
  5.5 16.6 %collective-permute-start.1 = (bf16[32,4096]{1,0:T(8,128)(2,1)}, bf16[32,4096]{1,0:T(8,128)(2,1)S(1)}, u32[]{:S(2)}, u32[]{:S(2)}) collective-permute-start(bf16[32,4096]{1,0:T(8,128)(2,1)} %get-tuple-element.8), channel_id=1, source_target_pairs={{0,6},{1,7},{4,2},{5,3},{2,4},{3,5},{6,0},{7,1},{8,14},{9,15},{12,... | collective-permute-start | bytes 786440 | tf_op jit(solution)/shard_map/ppermute | solution.py:205
  8.9 21.4 %all-to-all-start = ((bf16[64,4,128]{2,1,0:T(4,128)(2,1)}), bf16[64,4,128]{2,1,0:T(4,128)(2,1)S(1)}, u32[]{:S(2)}, u32[]{:S(2)}) async-start(bf16[64,4,128]{2,1,0:T(4,128)(2,1)} %bitcast.11), calls=%async_computation | async-start | bytes 131072 | tf_op jit(solution)/shard_map/all_to_all | solution.py:216
  20.8 13.0 %collective-permute-start = (bf16[128,4096]{1,0:T(8,128)(2,1)S(1)}, bf16[128,4096]{1,0:T(8,128)(2,1)S(1)}, u32[]{:S(2)}, u32[]{:S(2)}) collective-permute-start(bf16[128,4096]{1,0:T(8,128)(2,1)S(1)} %copy-done), channel_id=1, source_target_pairs={{0,1},{1,0},{4,5},{5,4},{2,3},{3,2},{6,7},{7,6},{8,9},{9,8},{12,13... | collective-permute-start | bytes 3145736 | tf_op jit(solution)/shard_map/ppermute | solution.py:205
  22.1 11.1 %collective-permute-start.2 = (bf16[32,4096]{1,0:T(8,128)(2,1)S(1)}, bf16[32,4096]{1,0:T(8,128)(2,1)S(1)}, u32[]{:S(2)}, u32[]{:S(2)}) collective-permute-start(bf16[32,4096]{1,0:T(8,128)(2,1)S(1)} %collective-permute-done.1.refs_0_), channel_id=1, source_target_pairs={{0,4},{1,5},{4,0},{5,1},{2,6},{3,7},{6,2},{7,3},{8,12},{9,13},{12,... | collective-permute-start | bytes 786440 | tf_op jit(solution)/shard_map/ppermute | solution.py:205
  23.4 9.9 %collective-permute-start.3 = (bf16[32,4096]{1,0:T(8,128)(2,1)S(1)}, bf16[32,4096]{1,0:T(8,128)(2,1)S(1)}, u32[]{:S(2)}, u32[]{:S(2)}) collective-permute-start(bf16[32,4096]{1,0:T(8,128)(2,1)S(1)} %collective-permute-done.1.refs_0_), channel_id=1, source_target_pairs={{0,8},{1,9},{4,12},{5,13},{2,10},{3,11},{6,14},{7,15},{8,0},{9,1},... | collective-permute-start | bytes 786440 | tf_op jit(solution)/shard_map/ppermute | solution.py:205
  24.6 9.1 %collective-permute-start.4 = (bf16[32,4096]{1,0:T(8,128)(2,1)S(1)}, bf16[32,4096]{1,0:T(8,128)(2,1)S(1)}, u32[]{:S(2)}, u32[]{:S(2)}) collective-permute-start(bf16[32,4096]{1,0:T(8,128)(2,1)S(1)} %collective-permute-done.1.refs_0_), channel_id=1, source_target_pairs={{0,32},{1,33},{4,36},{5,37},{2,34},{3,35},{6,38},{7,39},{8,40},{9,... | collective-permute-start | bytes 786440 | tf_op jit(solution)/shard_map/ppermute | solution.py:205
  30.7 4.8 %copy-start.2 = (s32[1,4]{1,0:T(1,128)S(1)}, s32[1,4]{1,0:T(1,128)}, u32[]{:S(2)}) copy-start(s32[1,4]{1,0:T(1,128)} %order_ref.1) | copy-start | bytes 52
  30.7 3.8 %collective-permute-start.5 = (bf16[32,4096]{1,0:T(8,128)(2,1)S(1)}, bf16[32,4096]{1,0:T(8,128)(2,1)S(1)}, u32[]{:S(2)}, u32[]{:S(2)}) collective-permute-start(bf16[32,4096]{1,0:T(8,128)(2,1)S(1)} %collective-permute-done.1.refs_0_), channel_id=1, source_target_pairs={{0,1},{1,0},{4,5},{5,4},{2,3},{3,2},{6,7},{7,6},{8,9},{9,8},{12,13... | collective-permute-start | bytes 786440 | tf_op jit(solution)/shard_map/ppermute | solution.py:205
  33.2 1.5 %collective-permute-start.6 = (bf16[32,4096]{1,0:T(8,128)(2,1)S(1)}, bf16[32,4096]{1,0:T(8,128)(2,1)S(1)}, u32[]{:S(2)}, u32[]{:S(2)}) collective-permute-start(bf16[32,4096]{1,0:T(8,128)(2,1)S(1)} %collective-permute-done.2.refs_1_), channel_id=1, source_target_pairs={{0,1},{1,0},{4,5},{5,4},{2,3},{3,2},{6,7},{7,6},{8,9},{9,8},{12,13... | collective-permute-start | bytes 786440 | tf_op jit(solution)/shard_map/ppermute | solution.py:205
  33.3 1.8 %collective-permute-start.7 = (bf16[32,4096]{1,0:T(8,128)(2,1)S(1)}, bf16[32,4096]{1,0:T(8,128)(2,1)S(1)}, u32[]{:S(2)}, u32[]{:S(2)}) collective-permute-start(bf16[32,4096]{1,0:T(8,128)(2,1)S(1)} %collective-permute-done.3.refs_2_), channel_id=1, source_target_pairs={{0,1},{1,0},{4,5},{5,4},{2,3},{3,2},{6,7},{7,6},{8,9},{9,8},{12,13... | collective-permute-start | bytes 786440 | tf_op jit(solution)/shard_map/ppermute | solution.py:205
  33.7 1.8 %collective-permute-start.8 = (bf16[32,4096]{1,0:T(8,128)(2,1)S(1)}, bf16[32,4096]{1,0:T(8,128)(2,1)S(1)}, u32[]{:S(2)}, u32[]{:S(2)}) collective-permute-start(bf16[32,4096]{1,0:T(8,128)(2,1)S(1)} %collective-permute-done.4.refs_3_), channel_id=1, source_target_pairs={{0,1},{1,0},{4,5},{5,4},{2,3},{3,2},{6,7},{7,6},{8,9},{9,8},{12,13... | collective-permute-start | bytes 786440 | tf_op jit(solution)/shard_map/ppermute | solution.py:205

commit v3 on v2

--- a/solution.py
+++ b/solution.py
@@ -12,8 +12,10 @@
 TOK = 128
 ROWS = DOCS * CAP
 PANEL = 128
-QUART = PANEL // 4
+SHARE = 768
+REST = R * R - 4 * SHARE
 NT = (((1,), (1,)), ((), ()))
+FIRST = 62
 
 
 ACT_STEPS = (4096,)
@@ -21,7 +23,7 @@
 
 
 def project_kernel(act_hbm, grad_hbm, win_hbm, wout_hbm, len_hbm, own_hbm, panel_hbm,
-                   rows_ref, quarter_ref, act_v, grad_v, win_v, wout_v, len_ref, own_ref, sems):
+                   rows_ref, share_ref, rest_ref, act_v, grad_v, win_v, wout_v, len_ref, own_ref, sems):
     jobs = []
     for x_hbm, w_hbm, x_v, w_v, sizes in (
         (act_hbm, win_hbm, act_v, win_v, ACT_STEPS),
@@ -45,11 +47,17 @@
     )
     for copy in ints:
         copy.start()
-    given = pl.multiple_of((quarter_of(lax.axis_index("docs")) ^ 1) * QUART, QUART)
-    given = pltpu.make_async_copy(
-        panel_hbm.at[pl.ds(given, QUART)], quarter_ref, sems.at[2 * len(jobs) + 2]
-    )
-    given.start()
+    share = pl.multiple_of((share_of(lax.axis_index("docs")) ^ 1) * SHARE, SHARE)
+    given = (
+        pltpu.make_async_copy(
+            panel_hbm.at[:, pl.ds(share, SHARE)], share_ref, sems.at[2 * len(jobs) + 2]
+        ),
+        pltpu.make_async_copy(
+            panel_hbm.at[:, pl.ds(4 * SHARE, REST)], rest_ref, sems.at[2 * len(jobs) + 3]
+        ),
+    )
+    for copy in given:
+        copy.start()
 
     def low_part(job):
         copies, x_v, w_v, cols = job
@@ -62,7 +70,7 @@
     for copy in ints:
         copy.wait()
     lens = len_ref[...].astype(jnp.float32)
-    owners = own_ref[...].astype(jnp.float32)
+    owners = (own_ref[...] ^ FIRST).astype(jnp.float32)
     one = lax.broadcasted_iota(jnp.int32, (DOCS, DOCS), 0)
     other = lax.broadcasted_iota(jnp.int32, (DOCS, DOCS), 1)
     start = jnp.sum(jnp.where(other < one, lens, 0.0), axis=1, keepdims=True)
@@ -77,7 +85,8 @@
     grad_low = sum(low_part(job) for job in jobs[len(ACT_STEPS):])
     rows = jnp.concatenate([grad_low, act_low], axis=1).astype(jnp.bfloat16)
     rows_ref[...] = jnp.dot(take, rows, preferred_element_type=jnp.float32).astype(jnp.bfloat16)
-    given.wait()
+    for copy in given:
+        copy.wait()
 
 
 def project(activations, out_grads, proj_in, proj_out, lengths, piece_owner, panels):
@@ -88,10 +97,11 @@
         project_kernel,
         out_shape=(
             jax.ShapeDtypeStruct((ROWS, 2 * R), jnp.bfloat16),
-            jax.ShapeDtypeStruct((QUART, panels.shape[1]), jnp.bfloat16),
+            jax.ShapeDtypeStruct((PANEL, SHARE), jnp.bfloat16),
+            jax.ShapeDtypeStruct((PANEL, REST), jnp.bfloat16),
         ),
         in_specs=[hbm] * 7,
-        out_specs=(vmem, vmem),
+        out_specs=(vmem, vmem, vmem),
         scratch_shapes=[
             pltpu.VMEM((TOK, width_in), jnp.bfloat16),
             pltpu.VMEM((TOK, width_out), jnp.bfloat16),
@@ -99,7 +109,7 @@
             pltpu.VMEM((R, width_out), jnp.bfloat16),
             pltpu.VMEM((1, DOCS), jnp.int32),
             pltpu.VMEM((1, DOCS), jnp.int32),
-            pltpu.SemaphoreType.DMA((2 * len(ACT_STEPS + GRAD_STEPS) + 3,)),
+            pltpu.SemaphoreType.DMA((2 * len(ACT_STEPS + GRAD_STEPS) + 4,)),
         ],
         compiler_params=pltpu.CompilerParams(vmem_limit_bytes=56 << 20),
         cost_estimate=pl.CostEstimate(
@@ -116,7 +126,7 @@
         kernel,
         out_shape=out_shape,
         in_specs=in_specs,
-        out_specs=pl.BlockSpec(memory_space=pltpu.VMEM),
+        out_specs=jax.tree.map(lambda _: pl.BlockSpec(memory_space=pltpu.VMEM), out_shape),
         compiler_params=pltpu.CompilerParams(vmem_limit_bytes=16 << 20),
         cost_estimate=pl.CostEstimate(
             flops=cost_us * 10**9, bytes_accessed=cost_us * 10**6, transcendentals=0
@@ -129,7 +139,8 @@
     doc = lax.broadcasted_iota(jnp.int32, (DOC_OWN, DOCS), 0)
     mine = jnp.where(slot_ref[...] == doc, 1.0, 0.0).astype(jnp.bfloat16)
     source = lax.broadcasted_iota(jnp.int32, (DOCS, ROWS), 0)
-    spread = jnp.where((lax.broadcasted_iota(jnp.int32, (DOCS, ROWS), 1) >> 2) == source, 1.0, 0.0)
+    place = lax.broadcasted_iota(jnp.int32, (DOCS, ROWS), 1) >> 2
+    spread = jnp.where((place ^ FIRST) == source, 1.0, 0.0)
     member = jnp.dot(mine, spread.astype(jnp.bfloat16), preferred_element_type=jnp.float32)
 
     rows = rows_ref[...]
@@ -150,34 +161,48 @@
     ).astype(jnp.bfloat16)
 
 
-def against(panel_ref, grads):
-    return lax.dot_general(panel_ref[...], grads, NT, preferred_element_type=jnp.float32)
-
-
-def near_kernel(grads_ref, own_ref, beside_ref, out_ref):
-    grads = grads_ref[...]
-    out_ref[:, :PANEL] = jnp.transpose(against(own_ref, grads))
-    out_ref[:, PANEL:] = jnp.transpose(against(beside_ref, grads))
-
-
-def far_kernel(order_ref, grads_ref, near_ref, *refs):
-    quarter_refs, out_ref, column_ref = refs[:-2], refs[-2], refs[-1]
+def against(grads_ref, panel_ref, at):
+    grads = grads_ref[:, pl.ds(at, panel_ref.shape[1])]
+    return lax.dot_general(grads, panel_ref[...], NT, preferred_element_type=jnp.float32)
+
+
+def share_at(kth):
+    return pl.multiple_of((share_of(lax.axis_index("docs")) ^ kth) * SHARE, SHARE)
+
+
+def near_kernel(grads_ref, own_ref, across_ref, out_ref):
+    out_ref[:, :PANEL] = against(grads_ref, own_ref, 0)
+    out_ref[:, PANEL:] = against(grads_ref, across_ref, share_at(0))
+
+
+def far_kernel(grads_ref, mate_grads_ref, near_ref, mate_near_ref, rest_ref, *refs):
+    part_refs, out_ref, mate_out_ref = refs[:-2], refs[-2], refs[-1]
+    both = None
+    for ref, at in [(rest_ref, 4 * SHARE)] + [(r, share_at(k + 1)) for k, r in enumerate(part_refs)]:
+        cols = pl.ds(at, ref.shape[1])
+        grads = jnp.concatenate([grads_ref[:, cols], mate_grads_ref[:, cols]], axis=0)
+        part = lax.dot_general(grads, ref[...], NT, preferred_element_type=jnp.float32)
+        both = part if both is None else both + part
+    out_ref[...] = near_ref[:, PANEL:] + both[:DOC_OWN]
+    mate_out_ref[:, :PANEL] = mate_near_ref[:, :PANEL]
+    mate_out_ref[:, PANEL:] = mate_near_ref[:, PANEL:] + both[DOC_OWN:]
+
+
+def last_kernel(order_ref, near_ref, far_ref, mate_ref, out_ref):
     query_at = lax.axis_index("query")
-    mine = quarter_of(lax.axis_index("docs"))
-    grads = grads_ref[...]
-    for n, ref in enumerate(quarter_refs):
-        row = (n // 4) * PANEL + (mine ^ (n % 4)) * QUART
-        column_ref[pl.ds(pl.multiple_of(row, QUART), QUART), :] = against(ref, grads)
-
-    far = jnp.transpose(column_ref[...])
-    blocks = [near_ref[:, :PANEL], near_ref[:, PANEL:], far[:, :PANEL], far[:, PANEL:]]
-    for kth, block in enumerate(blocks):
+
+    def put(kth, block):
         held = query_at ^ kth
         at = sum(jnp.where(order_ref[0, b] == held, b, 0) for b in range(1, 4)) * PANEL
         out_ref[0, :, pl.ds(pl.multiple_of(at, PANEL), PANEL)] = block
 
-
-def quarter_of(docs_at):
+    put(0, near_ref[:, :PANEL])
+    put(1, mate_ref[:, :PANEL])
+    put(2, far_ref[...])
+    put(3, mate_ref[:, PANEL:])
+
+
+def share_of(docs_at):
     return (docs_at & 1) ^ (2 * ((docs_at >> 1) & 1)) ^ (3 * ((docs_at >> 3) & 1))
 
 
@@ -210,30 +235,41 @@
 ):
     smem = pl.BlockSpec(memory_space=pltpu.SMEM)
     vmem = pl.BlockSpec(memory_space=pltpu.VMEM)
-    packed, given = project(
+    packed, share, rest = project(
         activations, out_grads, proj_in, proj_out, lengths[0], piece_owner[0], panels
     )
     arrived = lax.all_to_all(
-        packed.reshape(DOCS, CAP, 2 * R), "docs", split_axis=0, concat_axis=0, tiled=True
+        packed.reshape(DOCS, CAP, 2 * R), "docs", split_axis=0, concat_axis=0, tiled=True,
+        axis_index_groups=[[place ^ FIRST for place in range(DOCS)]],
     ).reshape(ROWS, 2 * R)
 
-    beside = send(panels, TO_CORE)
-    across = send(given, TO_CROSS)
-    parts = [across] + [send(across, to) for to in (TO_X, TO_Y, TO_Z)]
-    parts_beside = [send(part, TO_CORE) for part in parts]
+    across = send(share, TO_CROSS)
+    rest = send(rest, TO_CROSS)
+    parts = [send(across, to) for to in (TO_X, TO_Y, TO_Z)]
+
+    def block(width):
+        return jax.ShapeDtypeStruct((DOC_OWN, width), jnp.float32)
 
     grads = call(
         document_kernel, jax.ShapeDtypeStruct((DOC_OWN, R * R), jnp.bfloat16), 10,
         [vmem] * 2, doc_slot[0].reshape(1, DOCS), arrived, name="documents",
     )
+    mate_grads = send(grads, TO_CORE)
     near = call(
-        near_kernel, jax.ShapeDtypeStruct((DOC_OWN, 2 * PANEL), jnp.float32), 10,
-        [vmem] * 3, grads, panels, beside, name="near",
-    )
+        near_kernel, block(2 * PANEL), 0, [vmem] * 3, grads, panels, across, name="near",
+    )
+    near, mate_grads = lax.optimization_barrier((near, mate_grads))
+    mate_near = call(
+        near_kernel, block(2 * PANEL), 0, [vmem] * 3, mate_grads, panels, across, name="mate",
+    )
+    far, mate_scores = call(
+        far_kernel, (block(PANEL), block(2 * PANEL)), 0, [vmem] * 8,
+        grads, mate_grads, near, mate_near, rest, *parts, name="far",
+    )
+    mate_scores = send(mate_scores, TO_CORE)
     return call(
-        far_kernel, jax.ShapeDtypeStruct((1, DOC_OWN, 4 * PANEL), jnp.float32), 10,
-        [smem] + [vmem] * 10, panel_order, grads, near, *parts, *parts_beside, name="far",
-        scratch_shapes=[pltpu.VMEM((2 * PANEL, DOC_OWN), jnp.float32)],
+        last_kernel, jax.ShapeDtypeStruct((1, DOC_OWN, 4 * PANEL), jnp.float32), 0,
+        [smem] + [vmem] * 3, panel_order, near, far, mate_scores, name="last",
     )
 
 

time: 37.6 us -> 34.2 us (0.910)
  starting transfers between devices: 23.3 us -> 21.5 us
  waiting for transfers between devices: 5.49 us -> 4.26 us
    ppermute x9 -> x7, starting transfers between devices: 11.5 us -> 9.06 us  [send(): return lax.ppermute(value, ('docs', 'query'), pairs)]
    all_to_all x1, waiting for transfers between devices: 4.52 us -> 2.92 us  [shards(): lax.all_to_all(packed.reshape(DOCS, CAP, 2 * R), 'docs', split_axis=0, co...]
    all_to_all x1, starting transfers between devices: 11.8 us -> 12.5 us  [shards(): lax.all_to_all(packed.reshape(DOCS, CAP, 2 * R), 'docs', split_axis=0, co...]
    ppermute x9 -> x7, waiting for transfers between devices: 0.97 us -> 1.34 us  [send(): return lax.ppermute(value, ('docs', 'query'), pairs)]
    pallas_call x3 -> x5, Pallas kernels: 3.05 us -> 2.71 us  [call(): pl.pallas_call(kernel, out_shape=out_shape, in_specs=in_specs, out_specs=...]
  transfers between devices with their start and end apart: 10 -> 8, of which waited for: 4 -> 3; matrix products, arithmetic and copies ran while one was open for 0% -> 0% of each run, Pallas kernels for 3% -> 4%
where the time goes in v3:
time: 34.2 us; the launch traced here: 34 us
  starting transfers between devices  21.5 us (63%)
  Pallas kernels  8.21 us (24%)
  waiting for transfers between devices  4.26 us (12%)
    all_to_all x1, starting transfers between devices, shards(): lax.all_to_all(packed.reshape(DOCS, CAP, 2 * R), 'docs', split_axis=0, co...  12.5 us
    ppermute x7, starting transfers between devices, send(): return lax.ppermute(value, ('docs', 'query'), pairs)  9.06 us
    pallas_call x1, Pallas kernels, project(): pl.pallas_call(project_kernel, out_shape=(jax.ShapeDtypeStruct((ROWS, 2 *...  5.5 us
    all_to_all x1, waiting for transfers between devices, shards(): lax.all_to_all(packed.reshape(DOCS, CAP, 2 * R), 'docs', split_axis=0, co...  2.92 us
    pallas_call x5, Pallas kernels, call(): pl.pallas_call(kernel, out_shape=out_shape, in_specs=in_specs, out_specs=...  2.71 us
    ppermute x7, waiting for transfers between devices, send(): return lax.ppermute(value, ('docs', 'query'), pairs)  1.34 us
  transfers between devices with their start and end apart: 8, of which 3 were waited for; matrix products, arithmetic and copies ran while one was open for 0% of the time, Pallas kernels for 4%

profile of v3, /device:TPU:1, one launch (start us, length us, event | category | flops | bytes accessed | tf_op | source)
XLA Modules:
  0.0 34.0 jit_solution(12945773542513458083)
XLA Ops:
  0.0 0.0 copy-start.2
  0.0 5.5 %project.1 = (bf16[256,128]{1,0:T(8,128)(2,1)}, bf16[128,768]{1,0:T(8,128)(2,1)}, bf16[128,1024]{1,0:T(8,128)(2,1)}) custom-call(bf16[1,128,4096]{2,1,0:T(8,128)(2,1)} %act_hbm.1, bf16[1,128,14336]{2,1,0:T(8,128)(2,1)} %grad_hbm.1, bf16[64,4096]{1,0:T(8,128)(2,1)} %bitcast.10, bf16[64,14336]{1,0:T(8,128)(2,1)} %bitcast.9, s32[1,64]{1,0:T(1,128)} %bitcast.12, ...), custom_call_target="tpu_custom_call" | custom-call | flops 301989888 | bytes 7077888 | tf_op jit(solution)/shard_map/project/pallas_call | solution.py:96
  5.5 3.4 %collective-permute-start = (bf16[128,768]{1,0:T(8,128)(2,1)}, bf16[128,768]{1,0:T(8,128)(2,1)S(1)}, u32[]{:S(2)}, u32[]{:S(2)}) collective-permute-start(bf16[128,768]{1,0:T(8,128)(2,1)} %get-tuple-element.13), channel_id=1, source_target_pairs={{0,6},{1,7},{4,2},{5,3},{2,4},{3,5},{6,0},{7,1},{8,14},{9,15},{12,... | collective-permute-start | bytes 589832 | tf_op jit(solution)/shard_map/ppermute | solution.py:230
  8.9 12.5 %all-to-all-start = ((bf16[64,4,128]{2,1,0:T(4,128)(2,1)}), bf16[64,4,128]{2,1,0:T(4,128)(2,1)S(1)}, u32[]{:S(2)}, u32[]{:S(2)}) async-start(bf16[64,4,128]{2,1,0:T(4,128)(2,1)} %bitcast.11), calls=%async_computation | async-start | bytes 131072 | tf_op jit(solution)/shard_map/all_to_all | solution.py:241
  21.4 1.2 %collective-permute-start.2 = (bf16[128,1024]{1,0:T(8,128)(2,1)}, bf16[128,1024]{1,0:T(8,128)(2,1)S(1)}, u32[]{:S(2)}, u32[]{:S(2)}) collective-permute-start(bf16[128,1024]{1,0:T(8,128)(2,1)} %get-tuple-element.16), channel_id=1, source_target_pairs={{0,6},{1,7},{4,2},{5,3},{2,4},{3,5},{6,0},{7,1},{8,14},{9,15},{12,... | collective-permute-start | bytes 786440 | tf_op jit(solution)/shard_map/ppermute | solution.py:230
  22.6 0.0 collective-permute-done.across_ref
  22.6 0.2 collective-permute-start.3
  22.8 0.6 %collective-permute-start.4 = (bf16[128,768]{1,0:T(8,128)(2,1)S(1)}, bf16[128,768]{1,0:T(8,128)(2,1)S(1)}, u32[]{:S(2)}, u32[]{:S(2)}) collective-permute-start(bf16[128,768]{1,0:T(8,128)(2,1)S(1)} %collective-permute-done.across_ref), channel_id=1, source_target_pairs={{0,8},{1,9},{4,12},{5,13},{2,10},{3,11},{6,14},{7,15},{8,0},{9,1},... | collective-permute-start | bytes 589832 | tf_op jit(solution)/shard_map/ppermute | solution.py:230
  23.3 1.1 %collective-permute-start.5 = (bf16[128,768]{1,0:T(8,128)(2,1)S(1)}, bf16[128,768]{1,0:T(8,128)(2,1)S(1)}, u32[]{:S(2)}, u32[]{:S(2)}) collective-permute-start(bf16[128,768]{1,0:T(8,128)(2,1)S(1)} %collective-permute-done.across_ref), channel_id=1, source_target_pairs={{0,32},{1,33},{4,36},{5,37},{2,34},{3,35},{6,38},{7,39},{8,40},{9,... | collective-permute-start | bytes 589832 | tf_op jit(solution)/shard_map/ppermute | solution.py:230
  24.4 2.9 %all-to-all-done = bf16[64,4,128]{2,1,0:T(4,128)(2,1)S(1)} async-done(((bf16[64,4,128]{2,1,0:T(4,128)(2,1)}), bf16[64,4,128]{2,1,0:T(4,128)(2,1)S(1)}, u32[]{:S(2)}, u32[]{:S(2)}) %all-to-all-start) | async-done | bytes 65568 | tf_op jit(solution)/shard_map/all_to_all | solution.py:241
  27.4 0.0 copy-done.2
  27.4 0.0 copy-start
  27.4 0.0 copy-start.1
  27.4 0.4 %documents.1.grads_ref = bf16[8,4096]{1,0:T(8,128)(2,1)S(1)} custom-call(s32[1,64]{1,0:T(1,128)S(1)} %bitcast.8, bf16[256,128]{1,0:T(8,128)(2,1)S(1)} %bitcast.7), custom_call_target="tpu_custom_call" | custom-call | flops 10000000000 | bytes 10000000 | tf_op jit(solution)/shard_map/documents/pallas_call | solution.py:125
  27.7 2.2 %collective-permute-start.1 = (bf16[8,4096]{1,0:T(8,128)(2,1)S(1)}, bf16[8,4096]{1,0:T(8,128)(2,1)S(1)}, u32[]{:S(2)}, u32[]{:S(2)}) collective-permute-start(bf16[8,4096]{1,0:T(8,128)(2,1)S(1)} %documents.1.grads_ref), channel_id=1, source_target_pairs={{0,1},{1,0},{4,5},{5,4},{2,3},{3,2},{6,7},{7,6},{8,9},{9,8},{12,13... | collective-permute-start | bytes 196616 | tf_op jit(solution)/shard_map/ppermute | solution.py:230
  29.9 0.0 copy-done
  29.9 0.4 %near.1.near_ref = f32[8,256]{1,0:T(8,128)S(1)} custom-call(bf16[8,4096]{1,0:T(8,128)(2,1)S(1)} %documents.1.grads_ref, bf16[128,4096]{1,0:T(8,128)(2,1)S(1)} %copy-done, bf16[128,768]{1,0:T(8,128)(2,1)S(1)} %collective-permute-done.across_ref), custom_call_target="tpu_custom_call" | custom-call | tf_op jit(solution)/shard_map/near/pallas_call | solution.py:125
  30.4 0.5 %collective-permute-done.1.grads_ref.mate_grads_ref = bf16[8,4096]{1,0:T(8,128)(2,1)S(1)} collective-permute-done((bf16[8,4096]{1,0:T(8,128)(2,1)S(1)}, bf16[8,4096]{1,0:T(8,128)(2,1)S(1)}, u32[]{:S(2)}, u32[]{:S(2)}) %collective-permute-start.1) | collective-permute-done | bytes 65568 | tf_op jit(solution)/shard_map/ppermute | solution.py:230
  30.8 0.4 %mate.1.mate_near_ref = f32[8,256]{1,0:T(8,128)S(1)} custom-call(bf16[8,4096]{1,0:T(8,128)(2,1)S(1)} %collective-permute-done.1.grads_ref.mate_grads_ref, bf16[128,4096]{1,0:T(8,128)(2,1)S(1)} %copy-done, bf16[128,768]{1,0:T(8,128)(2,1)S(1)} %collective-permute-done.across_ref), custom_call_target="tpu_custom_call" | custom-call | tf_op jit(solution)/shard_map/mate/pallas_call | solution.py:125
  31.2 0.0 collective-permute-done.2.rest_ref
  31.3 0.0 collective-permute-done.3.refs_0_
  31.3 0.0 collective-permute-done.4.refs_1_
  31.3 0.0 collective-permute-done.5.refs_2_
  31.3 0.3 far.1
  31.6 0.4 %collective-permute-start.6 = (f32[8,256]{1,0:T(8,128)S(1)}, f32[8,256]{1,0:T(8,128)S(1)}, u32[]{:S(2)}, u32[]{:S(2)}) collective-permute-start(f32[8,256]{1,0:T(8,128)S(1)} %get-tuple-element.18), channel_id=1, source_target_pairs={{0,1},{1,0},{4,5},{5,4},{2,3},{3,2},{6,7},{7,6},{8,9},{9,8},{12,13... | collective-permute-start | bytes 24584 | tf_op jit(solution)/shard_map/ppermute | solution.py:230
  32.0 0.8 %collective-permute-done.6.mate_ref = f32[8,256]{1,0:T(8,128)S(1)} collective-permute-done((f32[8,256]{1,0:T(8,128)S(1)}, f32[8,256]{1,0:T(8,128)S(1)}, u32[]{:S(2)}, u32[]{:S(2)}) %collective-permute-start.6) | collective-permute-done | bytes 8224 | tf_op jit(solution)/shard_map/ppermute | solution.py:230
  32.9 0.0 copy-done.1
  32.9 1.2 %last.1 = f32[1,8,512]{2,1,0:T(8,128)} custom-call(s32[1,4]{1,0:T(1,128)S(1)} %copy-done.1, f32[8,256]{1,0:T(8,128)S(1)} %near.1.near_ref, f32[8,128]{1,0:T(8,128)S(1)} %get-tuple-element.17.far_ref, f32[8,256]{1,0:T(8,128)S(1)} %collective-permute-done.6.mate_ref), custom_call_target="tpu_custom_call" | custom-call | tf_op jit(solution)/shard_map/last/pallas_call | solution.py:125
Async XLA Ops:
  0.0 27.4 %copy-start.2 = (s32[1,64,1]{1,2,0:T(1,128)S(1)}, s32[1,64,1]{1,2,0:T(1,128)}, u32[]{:S(2)}) copy-start(s32[1,64,1]{1,2,0:T(1,128)} %param.16) | copy-start | bytes 772
  5.5 17.0 %collective-permute-start = (bf16[128,768]{1,0:T(8,128)(2,1)}, bf16[128,768]{1,0:T(8,128)(2,1)S(1)}, u32[]{:S(2)}, u32[]{:S(2)}) collective-permute-start(bf16[128,768]{1,0:T(8,128)(2,1)} %get-tuple-element.13), channel_id=1, source_target_pairs={{0,6},{1,7},{4,2},{5,3},{2,4},{3,5},{6,0},{7,1},{8,14},{9,15},{12,... | collective-permute-start | bytes 589832 | tf_op jit(solution)/shard_map/ppermute | solution.py:230
  8.9 18.5 %all-to-all-start = ((bf16[64,4,128]{2,1,0:T(4,128)(2,1)}), bf16[64,4,128]{2,1,0:T(4,128)(2,1)S(1)}, u32[]{:S(2)}, u32[]{:S(2)}) async-start(bf16[64,4,128]{2,1,0:T(4,128)(2,1)} %bitcast.11), calls=%async_computation | async-start | bytes 131072 | tf_op jit(solution)/shard_map/all_to_all | solution.py:241
  21.4 9.9 %collective-permute-start.2 = (bf16[128,1024]{1,0:T(8,128)(2,1)}, bf16[128,1024]{1,0:T(8,128)(2,1)S(1)}, u32[]{:S(2)}, u32[]{:S(2)}) collective-permute-start(bf16[128,1024]{1,0:T(8,128)(2,1)} %get-tuple-element.16), channel_id=1, source_target_pairs={{0,6},{1,7},{4,2},{5,3},{2,4},{3,5},{6,0},{7,1},{8,14},{9,15},{12,... | collective-permute-start | bytes 786440 | tf_op jit(solution)/shard_map/ppermute | solution.py:230
  22.6 8.7 %collective-permute-start.3 = (bf16[128,768]{1,0:T(8,128)(2,1)S(1)}, bf16[128,768]{1,0:T(8,128)(2,1)S(1)}, u32[]{:S(2)}, u32[]{:S(2)}) collective-permute-start(bf16[128,768]{1,0:T(8,128)(2,1)S(1)} %collective-permute-done.across_ref), channel_id=1, source_target_pairs={{0,4},{1,5},{4,0},{5,1},{2,6},{3,7},{6,2},{7,3},{8,12},{9,13},{12,... | collective-permute-start | bytes 589832 | tf_op jit(solution)/shard_map/ppermute | solution.py:230
  22.8 8.5 %collective-permute-start.4 = (bf16[128,768]{1,0:T(8,128)(2,1)S(1)}, bf16[128,768]{1,0:T(8,128)(2,1)S(1)}, u32[]{:S(2)}, u32[]{:S(2)}) collective-permute-start(bf16[128,768]{1,0:T(8,128)(2,1)S(1)} %collective-permute-done.across_ref), channel_id=1, source_target_pairs={{0,8},{1,9},{4,12},{5,13},{2,10},{3,11},{6,14},{7,15},{8,0},{9,1},... | collective-permute-start | bytes 589832 | tf_op jit(solution)/shard_map/ppermute | solution.py:230
  23.3 8.0 %collective-permute-start.5 = (bf16[128,768]{1,0:T(8,128)(2,1)S(1)}, bf16[128,768]{1,0:T(8,128)(2,1)S(1)}, u32[]{:S(2)}, u32[]{:S(2)}) collective-permute-start(bf16[128,768]{1,0:T(8,128)(2,1)S(1)} %collective-permute-done.across_ref), channel_id=1, source_target_pairs={{0,32},{1,33},{4,36},{5,37},{2,34},{3,35},{6,38},{7,39},{8,40},{9,... | collective-permute-start | bytes 589832 | tf_op jit(solution)/shard_map/ppermute | solution.py:230
  27.4 2.6 %copy-start = (bf16[128,4096]{1,0:T(8,128)(2,1)S(1)}, bf16[128,4096]{1,0:T(8,128)(2,1)}, u32[]{:S(2)}) copy-start(bf16[128,4096]{1,0:T(8,128)(2,1)} %own_ref.3) | copy-start | bytes 3145732
  27.4 5.5 %copy-start.1 = (s32[1,4]{1,0:T(1,128)S(1)}, s32[1,4]{1,0:T(1,128)}, u32[]{:S(2)}) copy-start(s32[1,4]{1,0:T(1,128)} %order_ref.1) | copy-start | bytes 52
  27.7 3.1 %collective-permute-start.1 = (bf16[8,4096]{1,0:T(8,128)(2,1)S(1)}, bf16[8,4096]{1,0:T(8,128)(2,1)S(1)}, u32[]{:S(2)}, u32[]{:S(2)}) collective-permute-start(bf16[8,4096]{1,0:T(8,128)(2,1)S(1)} %documents.1.grads_ref), channel_id=1, source_target_pairs={{0,1},{1,0},{4,5},{5,4},{2,3},{3,2},{6,7},{7,6},{8,9},{9,8},{12,13... | collective-permute-start | bytes 196616 | tf_op jit(solution)/shard_map/ppermute | solution.py:230
  31.6 1.2 %collective-permute-start.6 = (f32[8,256]{1,0:T(8,128)S(1)}, f32[8,256]{1,0:T(8,128)S(1)}, u32[]{:S(2)}, u32[]{:S(2)}) collective-permute-start(f32[8,256]{1,0:T(8,128)S(1)} %get-tuple-element.18), channel_id=1, source_target_pairs={{0,1},{1,0},{4,5},{5,4},{2,3},{3,2},{6,7},{7,6},{8,9},{9,8},{12,13... | collective-permute-start | bytes 24584 | tf_op jit(solution)/shard_map/ppermute | solution.py:230

commit v4 on v3

--- a/solution.py
+++ b/solution.py
@@ -135,7 +135,7 @@
     )(*given)
 
 
-def document_kernel(slot_ref, rows_ref, grads_ref):
+def document_kernel(slot_ref, rows_ref, panel_ref, grads_ref):
     doc = lax.broadcasted_iota(jnp.int32, (DOC_OWN, DOCS), 0)
     mine = jnp.where(slot_ref[...] == doc, 1.0, 0.0).astype(jnp.bfloat16)
     source = lax.broadcasted_iota(jnp.int32, (DOCS, ROWS), 0)
@@ -191,15 +191,12 @@
 def last_kernel(order_ref, near_ref, far_ref, mate_ref, out_ref):
     query_at = lax.axis_index("query")
 
-    def put(kth, block):
-        held = query_at ^ kth
-        at = sum(jnp.where(order_ref[0, b] == held, b, 0) for b in range(1, 4)) * PANEL
-        out_ref[0, :, pl.ds(pl.multiple_of(at, PANEL), PANEL)] = block
-
-    put(0, near_ref[:, :PANEL])
-    put(1, mate_ref[:, :PANEL])
-    put(2, far_ref[...])
-    put(3, mate_ref[:, PANEL:])
+    blocks = [near_ref[:, :PANEL], mate_ref[:, :PANEL], far_ref[...], mate_ref[:, PANEL:]]
+    for at in range(4):
+        wanted = order_ref[:, at:at + 1]
+        out_ref[0, :, at * PANEL:(at + 1) * PANEL] = sum(
+            jnp.where(wanted == (query_at ^ kth), block, 0.0) for kth, block in enumerate(blocks)
+        )
 
 
 def share_of(docs_at):
@@ -233,7 +230,6 @@
 def shards(
     activations, out_grads, proj_in, proj_out, panels, lengths, piece_owner, doc_slot, panel_order
 ):
-    smem = pl.BlockSpec(memory_space=pltpu.SMEM)
     vmem = pl.BlockSpec(memory_space=pltpu.VMEM)
     packed, share, rest = project(
         activations, out_grads, proj_in, proj_out, lengths[0], piece_owner[0], panels
@@ -252,7 +248,7 @@
 
     grads = call(
         document_kernel, jax.ShapeDtypeStruct((DOC_OWN, R * R), jnp.bfloat16), 10,
-        [vmem] * 2, doc_slot[0].reshape(1, DOCS), arrived, name="documents",
+        [vmem] * 3, doc_slot[0].reshape(1, DOCS), arrived, panels, name="documents",
     )
     mate_grads = send(grads, TO_CORE)
     near = call(
@@ -269,7 +265,7 @@
     mate_scores = send(mate_scores, TO_CORE)
     return call(
         last_kernel, jax.ShapeDtypeStruct((1, DOC_OWN, 4 * PANEL), jnp.float32), 0,
-        [smem] + [vmem] * 3, panel_order, near, far, mate_scores, name="last",
+        [vmem] * 4, panel_order, near, far, mate_scores, name="last",
     )
 
 

time: 34.2 us -> 33.8 us (0.988)
  Pallas kernels: 8.21 us -> 7.82 us
    pallas_call x5, Pallas kernels: 2.71 us -> 2.25 us  [call(): pl.pallas_call(kernel, out_shape=out_shape, in_specs=in_specs, out_specs=...]
where the time goes in v4:
time: 33.8 us; the launch traced here: 33.7 us
  starting transfers between devices  21.5 us (64%)
  Pallas kernels  7.82 us (23%)
  waiting for transfers between devices  4.26 us (13%)
    all_to_all x1, starting transfers between devices, shards(): lax.all_to_all(packed.reshape(DOCS, CAP, 2 * R), 'docs', split_axis=0, co...  12.5 us
    ppermute x7, starting transfers between devices, send(): return lax.ppermute(value, ('docs', 'query'), pairs)  9.05 us
    pallas_call x1, Pallas kernels, project(): pl.pallas_call(project_kernel, out_shape=(jax.ShapeDtypeStruct((ROWS, 2 *...  5.58 us
    all_to_all x1, waiting for transfers between devices, shards(): lax.all_to_all(packed.reshape(DOCS, CAP, 2 * R), 'docs', split_axis=0, co...  2.92 us
    pallas_call x5, Pallas kernels, call(): pl.pallas_call(kernel, out_shape=out_shape, in_specs=in_specs, out_specs=...  2.25 us
    ppermute x7, waiting for transfers between devices, send(): return lax.ppermute(value, ('docs', 'query'), pairs)  1.34 us
  transfers between devices with their start and end apart: 8, of which 3 were waited for; matrix products, arithmetic and copies ran while one was open for 0% of the time, Pallas kernels for 4%

profile of v4, /device:TPU:1, one launch (start us, length us, event | category | flops | bytes accessed | tf_op | source)
XLA Modules:
  0.0 33.7 jit_solution(2531861732268700631)
XLA Ops:
  0.0 0.0 copy-start
  0.0 0.0 copy-start.2
  0.0 5.6 %project.1 = (bf16[256,128]{1,0:T(8,128)(2,1)}, bf16[128,768]{1,0:T(8,128)(2,1)}, bf16[128,1024]{1,0:T(8,128)(2,1)}) custom-call(bf16[1,128,4096]{2,1,0:T(8,128)(2,1)} %act_hbm.1, bf16[1,128,14336]{2,1,0:T(8,128)(2,1)} %grad_hbm.1, bf16[64,4096]{1,0:T(8,128)(2,1)} %bitcast.10, bf16[64,14336]{1,0:T(8,128)(2,1)} %bitcast.9, s32[1,64]{1,0:T(1,128)} %bitcast.12, ...), custom_call_target="tpu_custom_call" | custom-call | flops 301989888 | bytes 7077888 | tf_op jit(solution)/shard_map/project/pallas_call | solution.py:96
  5.6 3.4 %collective-permute-start = (bf16[128,768]{1,0:T(8,128)(2,1)}, bf16[128,768]{1,0:T(8,128)(2,1)S(1)}, u32[]{:S(2)}, u32[]{:S(2)}) collective-permute-start(bf16[128,768]{1,0:T(8,128)(2,1)} %get-tuple-element.13), channel_id=1, source_target_pairs={{0,6},{1,7},{4,2},{5,3},{2,4},{3,5},{6,0},{7,1},{8,14},{9,15},{12,... | collective-permute-start | bytes 589832 | tf_op jit(solution)/shard_map/ppermute | solution.py:227
  9.0 12.5 %all-to-all-start = ((bf16[64,4,128]{2,1,0:T(4,128)(2,1)}), bf16[64,4,128]{2,1,0:T(4,128)(2,1)S(1)}, u32[]{:S(2)}, u32[]{:S(2)}) async-start(bf16[64,4,128]{2,1,0:T(4,128)(2,1)} %bitcast.11), calls=%async_computation | async-start | bytes 131072 | tf_op jit(solution)/shard_map/all_to_all | solution.py:237
  21.4 1.2 %collective-permute-start.2 = (bf16[128,1024]{1,0:T(8,128)(2,1)}, bf16[128,1024]{1,0:T(8,128)(2,1)S(1)}, u32[]{:S(2)}, u32[]{:S(2)}) collective-permute-start(bf16[128,1024]{1,0:T(8,128)(2,1)} %get-tuple-element.16), channel_id=1, source_target_pairs={{0,6},{1,7},{4,2},{5,3},{2,4},{3,5},{6,0},{7,1},{8,14},{9,15},{12,... | collective-permute-start | bytes 786440 | tf_op jit(solution)/shard_map/ppermute | solution.py:227
  22.6 0.0 collective-permute-done.across_ref
  22.6 0.2 collective-permute-start.3
  22.8 0.6 %collective-permute-start.4 = (bf16[128,768]{1,0:T(8,128)(2,1)S(1)}, bf16[128,768]{1,0:T(8,128)(2,1)S(1)}, u32[]{:S(2)}, u32[]{:S(2)}) collective-permute-start(bf16[128,768]{1,0:T(8,128)(2,1)S(1)} %collective-permute-done.across_ref), channel_id=1, source_target_pairs={{0,8},{1,9},{4,12},{5,13},{2,10},{3,11},{6,14},{7,15},{8,0},{9,1},... | collective-permute-start | bytes 589832 | tf_op jit(solution)/shard_map/ppermute | solution.py:227
  23.4 1.1 %collective-permute-start.5 = (bf16[128,768]{1,0:T(8,128)(2,1)S(1)}, bf16[128,768]{1,0:T(8,128)(2,1)S(1)}, u32[]{:S(2)}, u32[]{:S(2)}) collective-permute-start(bf16[128,768]{1,0:T(8,128)(2,1)S(1)} %collective-permute-done.across_ref), channel_id=1, source_target_pairs={{0,32},{1,33},{4,36},{5,37},{2,34},{3,35},{6,38},{7,39},{8,40},{9,... | collective-permute-start | bytes 589832 | tf_op jit(solution)/shard_map/ppermute | solution.py:227
  24.5 2.9 %all-to-all-done = bf16[64,4,128]{2,1,0:T(4,128)(2,1)S(1)} async-done(((bf16[64,4,128]{2,1,0:T(4,128)(2,1)}), bf16[64,4,128]{2,1,0:T(4,128)(2,1)S(1)}, u32[]{:S(2)}, u32[]{:S(2)}) %all-to-all-start) | async-done | bytes 65568 | tf_op jit(solution)/shard_map/all_to_all | solution.py:237
  27.4 0.0 copy-done
  27.4 0.0 copy-done.2
  27.5 0.0 copy-start.1
  27.5 0.4 %documents.1.grads_ref = bf16[8,4096]{1,0:T(8,128)(2,1)S(1)} custom-call(s32[1,64]{1,0:T(1,128)S(1)} %bitcast.8, bf16[256,128]{1,0:T(8,128)(2,1)S(1)} %bitcast.7, bf16[128,4096]{1,0:T(8,128)(2,1)S(1)} %copy-done), custom_call_target="tpu_custom_call" | custom-call | flops 10000000000 | bytes 10000000 | tf_op jit(solution)/shard_map/documents/pallas_call | solution.py:125
  27.8 2.2 %collective-permute-start.1 = (bf16[8,4096]{1,0:T(8,128)(2,1)S(1)}, bf16[8,4096]{1,0:T(8,128)(2,1)S(1)}, u32[]{:S(2)}, u32[]{:S(2)}) collective-permute-start(bf16[8,4096]{1,0:T(8,128)(2,1)S(1)} %documents.1.grads_ref), channel_id=1, source_target_pairs={{0,1},{1,0},{4,5},{5,4},{2,3},{3,2},{6,7},{7,6},{8,9},{9,8},{12,13... | collective-permute-start | bytes 196616 | tf_op jit(solution)/shard_map/ppermute | solution.py:227
  30.0 0.4 %near.1.near_ref = f32[8,256]{1,0:T(8,128)S(1)} custom-call(bf16[8,4096]{1,0:T(8,128)(2,1)S(1)} %documents.1.grads_ref, bf16[128,4096]{1,0:T(8,128)(2,1)S(1)} %copy-done, bf16[128,768]{1,0:T(8,128)(2,1)S(1)} %collective-permute-done.across_ref), custom_call_target="tpu_custom_call" | custom-call | tf_op jit(solution)/shard_map/near/pallas_call | solution.py:125
  30.4 0.5 %collective-permute-done.1.grads_ref.mate_grads_ref = bf16[8,4096]{1,0:T(8,128)(2,1)S(1)} collective-permute-done((bf16[8,4096]{1,0:T(8,128)(2,1)S(1)}, bf16[8,4096]{1,0:T(8,128)(2,1)S(1)}, u32[]{:S(2)}, u32[]{:S(2)}) %collective-permute-start.1) | collective-permute-done | bytes 65568 | tf_op jit(solution)/shard_map/ppermute | solution.py:227
  30.9 0.4 %mate.1.mate_near_ref = f32[8,256]{1,0:T(8,128)S(1)} custom-call(bf16[8,4096]{1,0:T(8,128)(2,1)S(1)} %collective-permute-done.1.grads_ref.mate_grads_ref, bf16[128,4096]{1,0:T(8,128)(2,1)S(1)} %copy-done, bf16[128,768]{1,0:T(8,128)(2,1)S(1)} %collective-permute-done.across_ref), custom_call_target="tpu_custom_call" | custom-call | tf_op jit(solution)/shard_map/mate/pallas_call | solution.py:125
  31.3 0.0 collective-permute-done.2.rest_ref
  31.3 0.0 collective-permute-done.3.refs_0_
  31.3 0.0 collective-permute-done.4.refs_1_
  31.4 0.0 collective-permute-done.5.refs_2_
  31.4 0.3 far.1
  31.7 0.4 %collective-permute-start.6 = (f32[8,256]{1,0:T(8,128)S(1)}, f32[8,256]{1,0:T(8,128)S(1)}, u32[]{:S(2)}, u32[]{:S(2)}) collective-permute-start(f32[8,256]{1,0:T(8,128)S(1)} %get-tuple-element.18), channel_id=1, source_target_pairs={{0,1},{1,0},{4,5},{5,4},{2,3},{3,2},{6,7},{7,6},{8,9},{9,8},{12,13... | collective-permute-start | bytes 24584 | tf_op jit(solution)/shard_map/ppermute | solution.py:227
  32.1 0.8 %collective-permute-done.6.mate_ref = f32[8,256]{1,0:T(8,128)S(1)} collective-permute-done((f32[8,256]{1,0:T(8,128)S(1)}, f32[8,256]{1,0:T(8,128)S(1)}, u32[]{:S(2)}, u32[]{:S(2)}) %collective-permute-start.6) | collective-permute-done | bytes 8224 | tf_op jit(solution)/shard_map/ppermute | solution.py:227
  32.9 0.0 copy-done.1
  32.9 0.7 %last.1 = f32[1,8,512]{2,1,0:T(8,128)} custom-call(s32[1,4]{1,0:T(1,128)S(1)} %copy-done.1, f32[8,256]{1,0:T(8,128)S(1)} %near.1.near_ref, f32[8,128]{1,0:T(8,128)S(1)} %get-tuple-element.17.far_ref, f32[8,256]{1,0:T(8,128)S(1)} %collective-permute-done.6.mate_ref), custom_call_target="tpu_custom_call" | custom-call | tf_op jit(solution)/shard_map/last/pallas_call | solution.py:125
Async XLA Ops:
  0.0 27.4 %copy-start = (bf16[128,4096]{1,0:T(8,128)(2,1)S(1)}, bf16[128,4096]{1,0:T(8,128)(2,1)}, u32[]{:S(2)}) copy-start(bf16[128,4096]{1,0:T(8,128)(2,1)} %own_ref.3) | copy-start | bytes 3145732
  0.0 27.4 %copy-start.2 = (s32[1,64,1]{1,2,0:T(1,128)S(1)}, s32[1,64,1]{1,2,0:T(1,128)}, u32[]{:S(2)}) copy-start(s32[1,64,1]{1,2,0:T(1,128)} %param.16) | copy-start | bytes 772
  5.6 17.0 %collective-permute-start = (bf16[128,768]{1,0:T(8,128)(2,1)}, bf16[128,768]{1,0:T(8,128)(2,1)S(1)}, u32[]{:S(2)}, u32[]{:S(2)}) collective-permute-start(bf16[128,768]{1,0:T(8,128)(2,1)} %get-tuple-element.13), channel_id=1, source_target_pairs={{0,6},{1,7},{4,2},{5,3},{2,4},{3,5},{6,0},{7,1},{8,14},{9,15},{12,... | collective-permute-start | bytes 589832 | tf_op jit(solution)/shard_map/ppermute | solution.py:227
  9.0 18.5 %all-to-all-start = ((bf16[64,4,128]{2,1,0:T(4,128)(2,1)}), bf16[64,4,128]{2,1,0:T(4,128)(2,1)S(1)}, u32[]{:S(2)}, u32[]{:S(2)}) async-start(bf16[64,4,128]{2,1,0:T(4,128)(2,1)} %bitcast.11), calls=%async_computation | async-start | bytes 131072 | tf_op jit(solution)/shard_map/all_to_all | solution.py:237
  21.4 9.9 %collective-permute-start.2 = (bf16[128,1024]{1,0:T(8,128)(2,1)}, bf16[128,1024]{1,0:T(8,128)(2,1)S(1)}, u32[]{:S(2)}, u32[]{:S(2)}) collective-permute-start(bf16[128,1024]{1,0:T(8,128)(2,1)} %get-tuple-element.16), channel_id=1, source_target_pairs={{0,6},{1,7},{4,2},{5,3},{2,4},{3,5},{6,0},{7,1},{8,14},{9,15},{12,... | collective-permute-start | bytes 786440 | tf_op jit(solution)/shard_map/ppermute | solution.py:227
  22.6 8.7 %collective-permute-start.3 = (bf16[128,768]{1,0:T(8,128)(2,1)S(1)}, bf16[128,768]{1,0:T(8,128)(2,1)S(1)}, u32[]{:S(2)}, u32[]{:S(2)}) collective-permute-start(bf16[128,768]{1,0:T(8,128)(2,1)S(1)} %collective-permute-done.across_ref), channel_id=1, source_target_pairs={{0,4},{1,5},{4,0},{5,1},{2,6},{3,7},{6,2},{7,3},{8,12},{9,13},{12,... | collective-permute-start | bytes 589832 | tf_op jit(solution)/shard_map/ppermute | solution.py:227
  22.8 8.5 %collective-permute-start.4 = (bf16[128,768]{1,0:T(8,128)(2,1)S(1)}, bf16[128,768]{1,0:T(8,128)(2,1)S(1)}, u32[]{:S(2)}, u32[]{:S(2)}) collective-permute-start(bf16[128,768]{1,0:T(8,128)(2,1)S(1)} %collective-permute-done.across_ref), channel_id=1, source_target_pairs={{0,8},{1,9},{4,12},{5,13},{2,10},{3,11},{6,14},{7,15},{8,0},{9,1},... | collective-permute-start | bytes 589832 | tf_op jit(solution)/shard_map/ppermute | solution.py:227
  23.4 8.0 %collective-permute-start.5 = (bf16[128,768]{1,0:T(8,128)(2,1)S(1)}, bf16[128,768]{1,0:T(8,128)(2,1)S(1)}, u32[]{:S(2)}, u32[]{:S(2)}) collective-permute-start(bf16[128,768]{1,0:T(8,128)(2,1)S(1)} %collective-permute-done.across_ref), channel_id=1, source_target_pairs={{0,32},{1,33},{4,36},{5,37},{2,34},{3,35},{6,38},{7,39},{8,40},{9,... | collective-permute-start | bytes 589832 | tf_op jit(solution)/shard_map/ppermute | solution.py:227
  27.5 5.5 %copy-start.1 = (s32[1,4]{1,0:T(1,128)S(1)}, s32[1,4]{1,0:T(1,128)}, u32[]{:S(2)}) copy-start(s32[1,4]{1,0:T(1,128)} %order_ref.1) | copy-start | bytes 52
  27.8 3.1 %collective-permute-start.1 = (bf16[8,4096]{1,0:T(8,128)(2,1)S(1)}, bf16[8,4096]{1,0:T(8,128)(2,1)S(1)}, u32[]{:S(2)}, u32[]{:S(2)}) collective-permute-start(bf16[8,4096]{1,0:T(8,128)(2,1)S(1)} %documents.1.grads_ref), channel_id=1, source_target_pairs={{0,1},{1,0},{4,5},{5,4},{2,3},{3,2},{6,7},{7,6},{8,9},{9,8},{12,13... | collective-permute-start | bytes 196616 | tf_op jit(solution)/shard_map/ppermute | solution.py:227
  31.7 1.2 %collective-permute-start.6 = (f32[8,256]{1,0:T(8,128)S(1)}, f32[8,256]{1,0:T(8,128)S(1)}, u32[]{:S(2)}, u32[]{:S(2)}) collective-permute-start(f32[8,256]{1,0:T(8,128)S(1)} %get-tuple-element.18), channel_id=1, source_target_pairs={{0,1},{1,0},{4,5},{5,4},{2,3},{3,2},{6,7},{7,6},{8,9},{9,8},{12,13... | collective-permute-start | bytes 24584 | tf_op jit(solution)/shard_map/ppermute | solution.py:227

commit v5 on v4

--- a/solution.py
+++ b/solution.py
@@ -22,53 +22,38 @@
 GRAD_STEPS = (7168, 4096, 3072)
 
 
-def project_kernel(act_hbm, grad_hbm, win_hbm, wout_hbm, len_hbm, own_hbm, panel_hbm,
-                   rows_ref, share_ref, rest_ref, act_v, grad_v, win_v, wout_v, len_ref, own_ref, sems):
-    jobs = []
-    for x_hbm, w_hbm, x_v, w_v, sizes in (
-        (act_hbm, win_hbm, act_v, win_v, ACT_STEPS),
-        (grad_hbm, wout_hbm, grad_v, wout_v, GRAD_STEPS),
-    ):
-        at = 0
-        for size in sizes:
-            cols = pl.ds(at, size)
-            n = 2 * len(jobs)
-            copies = (
-                pltpu.make_async_copy(w_hbm.at[:, cols], w_v.at[:, cols], sems.at[n]),
-                pltpu.make_async_copy(x_hbm.at[0, :, cols], x_v.at[:, cols], sems.at[n + 1]),
-            )
-            for copy in copies:
-                copy.start()
-            jobs.append((copies, x_v, w_v, cols))
-            at += size
-    ints = (
-        pltpu.make_async_copy(len_hbm, len_ref, sems.at[2 * len(jobs)]),
-        pltpu.make_async_copy(own_hbm, own_ref, sems.at[2 * len(jobs) + 1]),
-    )
-    for copy in ints:
+GIVEN_US = 10
+
+
+def given_kernel(panel_hbm, share_ref, rest_ref, sems):
+    share = pl.multiple_of((share_of(lax.axis_index("docs")) ^ 1) * SHARE, SHARE)
+    copies = (
+        pltpu.make_async_copy(panel_hbm.at[:, pl.ds(share, SHARE)], share_ref, sems.at[0]),
+        pltpu.make_async_copy(panel_hbm.at[:, pl.ds(4 * SHARE, REST)], rest_ref, sems.at[1]),
+    )
+    for copy in copies:
         copy.start()
-    share = pl.multiple_of((share_of(lax.axis_index("docs")) ^ 1) * SHARE, SHARE)
-    given = (
-        pltpu.make_async_copy(
-            panel_hbm.at[:, pl.ds(share, SHARE)], share_ref, sems.at[2 * len(jobs) + 2]
+    for copy in copies:
+        copy.wait()
+
+
+def given(panels):
+    return pl.pallas_call(
+        given_kernel,
+        out_shape=(
+            jax.ShapeDtypeStruct((PANEL, SHARE), jnp.bfloat16),
+            jax.ShapeDtypeStruct((PANEL, REST), jnp.bfloat16),
         ),
-        pltpu.make_async_copy(
-            panel_hbm.at[:, pl.ds(4 * SHARE, REST)], rest_ref, sems.at[2 * len(jobs) + 3]
-        ),
-    )
-    for copy in given:
-        copy.start()
-
-    def low_part(job):
-        copies, x_v, w_v, cols = job
-        for copy in copies:
-            copy.wait()
-        return lax.dot_general(x_v[:, cols], w_v[:, cols], NT, preferred_element_type=jnp.float32)
-
-    act_low = sum(low_part(job) for job in jobs[:len(ACT_STEPS)])
-
-    for copy in ints:
-        copy.wait()
+        in_specs=[pl.BlockSpec(memory_space=pltpu.HBM)],
+        out_specs=(pl.BlockSpec(memory_space=pltpu.VMEM),) * 2,
+        scratch_shapes=[pltpu.SemaphoreType.DMA((2,))],
+        compiler_params=pltpu.CompilerParams(vmem_limit_bytes=8 << 20),
+        cost_estimate=pl.CostEstimate(flops=GIVEN_US * 10**9, bytes_accessed=GIVEN_US * 10**6, transcendentals=0),
+        name="given",
+    )(panels)
+
+
+def take_kernel(len_ref, own_ref, take_ref):
     lens = len_ref[...].astype(jnp.float32)
     owners = (own_ref[...] ^ FIRST).astype(jnp.float32)
     one = lax.broadcasted_iota(jnp.int32, (DOCS, DOCS), 0)
@@ -80,45 +65,35 @@
     inside = (token >= start) & (token < start + size)
     goal = jnp.sum(jnp.where(inside, CAP * owner + token - start, 0.0), axis=0, keepdims=True)
     row = lax.broadcasted_iota(jnp.int32, (ROWS, TOK), 0).astype(jnp.float32)
-    take = jnp.where(row == goal, 1.0, 0.0).astype(jnp.bfloat16)
-
-    grad_low = sum(low_part(job) for job in jobs[len(ACT_STEPS):])
-    rows = jnp.concatenate([grad_low, act_low], axis=1).astype(jnp.bfloat16)
-    rows_ref[...] = jnp.dot(take, rows, preferred_element_type=jnp.float32).astype(jnp.bfloat16)
-    for copy in given:
-        copy.wait()
-
-
-def project(activations, out_grads, proj_in, proj_out, lengths, piece_owner, panels):
-    width_in, width_out = activations.shape[-1], out_grads.shape[-1]
-    hbm = pl.BlockSpec(memory_space=pltpu.HBM)
+    take_ref[...] = jnp.where(row == goal, 1.0, 0.0).astype(jnp.bfloat16)
+
+
+def grad_kernel(grad_ref, wout_ref, low_ref):
+    low_ref[...] = lax.dot_general(grad_ref[0], wout_ref[...], NT, preferred_element_type=jnp.float32)
+
+
+def pack_kernel(act_ref, win_ref, take_ref, low_ref, rows_ref):
+    act_low = lax.dot_general(act_ref[0], win_ref[...], NT, preferred_element_type=jnp.float32)
+    rows = jnp.concatenate([low_ref[...], act_low], axis=1).astype(jnp.bfloat16)
+    rows_ref[...] = jnp.dot(
+        take_ref[...], rows, preferred_element_type=jnp.float32
+    ).astype(jnp.bfloat16)
+
+
+def project(activations, out_grads, proj_in, proj_out, lengths, piece_owner):
     vmem = pl.BlockSpec(memory_space=pltpu.VMEM)
-    return pl.pallas_call(
-        project_kernel,
-        out_shape=(
-            jax.ShapeDtypeStruct((ROWS, 2 * R), jnp.bfloat16),
-            jax.ShapeDtypeStruct((PANEL, SHARE), jnp.bfloat16),
-            jax.ShapeDtypeStruct((PANEL, REST), jnp.bfloat16),
-        ),
-        in_specs=[hbm] * 7,
-        out_specs=(vmem, vmem, vmem),
-        scratch_shapes=[
-            pltpu.VMEM((TOK, width_in), jnp.bfloat16),
-            pltpu.VMEM((TOK, width_out), jnp.bfloat16),
-            pltpu.VMEM((R, width_in), jnp.bfloat16),
-            pltpu.VMEM((R, width_out), jnp.bfloat16),
-            pltpu.VMEM((1, DOCS), jnp.int32),
-            pltpu.VMEM((1, DOCS), jnp.int32),
-            pltpu.SemaphoreType.DMA((2 * len(ACT_STEPS + GRAD_STEPS) + 4,)),
-        ],
-        compiler_params=pltpu.CompilerParams(vmem_limit_bytes=56 << 20),
-        cost_estimate=pl.CostEstimate(
-            flops=2 * TOK * (width_in + width_out) * R,
-            bytes_accessed=2 * (TOK + R) * (width_in + width_out),
-            transcendentals=0,
-        ),
-        name="project",
-    )(activations, out_grads, proj_in.T, proj_out.T, lengths, piece_owner, panels)
+    take = call(
+        take_kernel, jax.ShapeDtypeStruct((ROWS, TOK), jnp.bfloat16), 0, [vmem] * 2,
+        lengths, piece_owner, name="take",
+    )
+    grad_low = call(
+        grad_kernel, jax.ShapeDtypeStruct((TOK, R), jnp.float32), 0, [vmem] * 2,
+        out_grads, proj_out.T, name="grads",
+    )
+    return call(
+        pack_kernel, jax.ShapeDtypeStruct((ROWS, 2 * R), jnp.bfloat16), 10, [vmem] * 4,
+        activations, proj_in.T, take, grad_low, name="pack",
+    )
 
 
 def call(kernel, out_shape, cost_us, in_specs, *given, **more):
@@ -231,9 +206,8 @@
     activations, out_grads, proj_in, proj_out, panels, lengths, piece_owner, doc_slot, panel_order
 ):
     vmem = pl.BlockSpec(memory_space=pltpu.VMEM)
-    packed, share, rest = project(
-        activations, out_grads, proj_in, proj_out, lengths[0], piece_owner[0], panels
-    )
+    share, rest = given(panels)
+    packed = project(activations, out_grads, proj_in, proj_out, lengths[0], piece_owner[0])
     arrived = lax.all_to_all(
         packed.reshape(DOCS, CAP, 2 * R), "docs", split_axis=0, concat_axis=0, tiled=True,
         axis_index_groups=[[place ^ FIRST for place in range(DOCS)]],

time: 33.8 us -> 33.2 us (0.982)
  Pallas kernels: 7.82 us -> 4.82 us
  starting transfers between devices: 21.5 us -> 23.6 us
  local copies, waits for them, and re-layouts: 0.01 us -> 1.27 us
  waiting for transfers between devices: 4.26 us -> 3.13 us
    pallas_call x1, Pallas kernels: 5.58 us -> 0.08 us  [given(): pl.pallas_call(given_kernel, out_shape=(jax.ShapeDtypeStruct((PANEL, SHAR...]
    pallas_call x5 -> x8, Pallas kernels: 2.25 us -> 4.73 us  [call(): pl.pallas_call(kernel, out_shape=out_shape, in_specs=in_specs, out_specs=...]
    ppermute x7, starting transfers between devices: 9.05 us -> 10.5 us  [send(): return lax.ppermute(value, ('docs', 'query'), pairs)]
    unnamed x6 -> x20, local copies, waits for them, and re-layouts: 0.01 us -> 1.27 us
    all_to_all x1, waiting for transfers between devices: 2.92 us -> 1.79 us  [shards(): lax.all_to_all(packed.reshape(DOCS, CAP, 2 * R), 'docs', split_axis=0, co...]
    all_to_all x1, starting transfers between devices: 12.5 us -> 13.2 us  [shards(): lax.all_to_all(packed.reshape(DOCS, CAP, 2 * R), 'docs', split_axis=0, co...]
  transfers between devices with their start and end apart: 8 -> 8, of which waited for: 3 -> 3; matrix products, arithmetic and copies ran while one was open for 0% -> 0% of each run, Pallas kernels for 4% -> 11%
where the time goes in v5:
time: 33.2 us; the launch traced here: 33 us
  starting transfers between devices  23.6 us (71%)
  Pallas kernels  4.82 us (15%)
  waiting for transfers between devices  3.13 us (9%)
  local copies, waits for them, and re-layouts  1.27 us (4%)
    all_to_all x1, starting transfers between devices, shards(): lax.all_to_all(packed.reshape(DOCS, CAP, 2 * R), 'docs', split_axis=0, co...  13.2 us
    ppermute x7, starting transfers between devices, send(): return lax.ppermute(value, ('docs', 'query'), pairs)  10.5 us
    pallas_call x8, Pallas kernels, call(): pl.pallas_call(kernel, out_shape=out_shape, in_specs=in_specs, out_specs=...  4.73 us
    all_to_all x1, waiting for transfers between devices, shards(): lax.all_to_all(packed.reshape(DOCS, CAP, 2 * R), 'docs', split_axis=0, co...  1.79 us
    ppermute x7, waiting for transfers between devices, send(): return lax.ppermute(value, ('docs', 'query'), pairs)  1.35 us
    unnamed x20, local copies, waits for them, and re-layouts  1.27 us
  transfers between devices with their start and end apart: 8, of which 3 were waited for; matrix products, arithmetic and copies ran while one was open for 0% of the time, Pallas kernels for 11%

profile of v5, /device:TPU:1, one launch (start us, length us, event | category | flops | bytes accessed | tf_op | source)
XLA Modules:
  0.0 33.0 jit_solution(9303824165775169347)
XLA Ops:
  0.0 0.0 copy-start
  0.0 1.2 %copy-done = bf16[128,4096]{1,0:T(8,128)(2,1)S(1)} copy-done((bf16[128,4096]{1,0:T(8,128)(2,1)S(1)}, bf16[128,4096]{1,0:T(8,128)(2,1)}, u32[]{:S(2)}) %copy-start) | copy-done | bytes 1048600
  1.2 0.0 copy-start.4
  1.2 0.0 copy-start.5
  1.2 0.0 copy-start.2
  1.2 0.0 copy-start.3
  1.2 0.1 given.1
  1.3 0.0 copy-start.7
  1.3 0.0 copy-start.8
  1.4 3.4 %collective-permute-start = (bf16[128,768]{1,0:T(8,128)(2,1)S(1)}, bf16[128,768]{1,0:T(8,128)(2,1)S(1)}, u32[]{:S(2)}, u32[]{:S(2)}) collective-permute-start(bf16[128,768]{1,0:T(8,128)(2,1)S(1)} %get-tuple-element.11), channel_id=1, source_target_pairs={{0,6},{1,7},{4,2},{5,3},{2,4},{3,5},{6,0},{7,1},{8,14},{9,15},{12,... | collective-permute-start | bytes 589832 | tf_op jit(solution)/shard_map/ppermute | solution.py:202
  4.7 0.0 copy-done.4
  4.8 0.0 copy-done.5
  4.8 0.1 take.1.take_ref
  4.9 0.0 copy-done.2
  4.9 0.0 copy-done.3
  4.9 1.1 %grads.1.low_ref = f32[128,64]{1,0:T(8,128)S(1)} custom-call(bf16[1,128,14336]{2,1,0:T(8,128)(2,1)S(1)} %copy-done.2, bf16[64,14336]{1,0:T(8,128)(2,1)S(1)} %bitcast.7), custom_call_target="tpu_custom_call" | custom-call | tf_op jit(solution)/shard_map/grads/pallas_call | solution.py:100
  6.0 0.0 copy-done.7
  6.0 0.0 copy-done.8
  6.0 0.0 copy-start.1
  6.0 0.0 copy-start.9
  6.1 1.3 %pack.1 = bf16[256,128]{1,0:T(8,128)(2,1)} custom-call(bf16[1,128,4096]{2,1,0:T(8,128)(2,1)S(1)} %copy-done.7, bf16[64,4096]{1,0:T(8,128)(2,1)S(1)} %bitcast.11, bf16[256,128]{1,0:T(8,128)(2,1)S(1)} %take.1.take_ref, f32[128,64]{1,0:T(8,128)S(1)} %grads.1.low_ref), custom_call_target="tpu_custom_call" | custom-call | flops 10000000000 | bytes 10000000 | tf_op jit(solution)/shard_map/pack/pallas_call | solution.py:100
  7.3 13.2 %all-to-all-start = ((bf16[64,4,128]{2,1,0:T(4,128)(2,1)}), bf16[64,4,128]{2,1,0:T(4,128)(2,1)S(1)}, u32[]{:S(2)}, u32[]{:S(2)}) async-start(bf16[64,4,128]{2,1,0:T(4,128)(2,1)} %bitcast.5), calls=%async_computation | async-start | bytes 131072 | tf_op jit(solution)/shard_map/all_to_all | solution.py:211
  20.5 2.5 %collective-permute-start.2 = (bf16[128,1024]{1,0:T(8,128)(2,1)S(1)}, bf16[128,1024]{1,0:T(8,128)(2,1)S(1)}, u32[]{:S(2)}, u32[]{:S(2)}) collective-permute-start(bf16[128,1024]{1,0:T(8,128)(2,1)S(1)} %get-tuple-element.14), channel_id=1, source_target_pairs={{0,6},{1,7},{4,2},{5,3},{2,4},{3,5},{6,0},{7,1},{8,14},{9,15},{12,... | collective-permute-start | bytes 786440 | tf_op jit(solution)/shard_map/ppermute | solution.py:202
  23.0 0.0 collective-permute-done.across_ref
  23.0 0.0 collective-permute-start.3
  23.0 0.6 %collective-permute-start.4 = (bf16[128,768]{1,0:T(8,128)(2,1)S(1)}, bf16[128,768]{1,0:T(8,128)(2,1)S(1)}, u32[]{:S(2)}, u32[]{:S(2)}) collective-permute-start(bf16[128,768]{1,0:T(8,128)(2,1)S(1)} %collective-permute-done.across_ref), channel_id=1, source_target_pairs={{0,8},{1,9},{4,12},{5,13},{2,10},{3,11},{6,14},{7,15},{8,0},{9,1},... | collective-permute-start | bytes 589832 | tf_op jit(solution)/shard_map/ppermute | solution.py:202
  23.6 1.1 %collective-permute-start.5 = (bf16[128,768]{1,0:T(8,128)(2,1)S(1)}, bf16[128,768]{1,0:T(8,128)(2,1)S(1)}, u32[]{:S(2)}, u32[]{:S(2)}) collective-permute-start(bf16[128,768]{1,0:T(8,128)(2,1)S(1)} %collective-permute-done.across_ref), channel_id=1, source_target_pairs={{0,32},{1,33},{4,36},{5,37},{2,34},{3,35},{6,38},{7,39},{8,40},{9,... | collective-permute-start | bytes 589832 | tf_op jit(solution)/shard_map/ppermute | solution.py:202
  24.7 1.8 %all-to-all-done = bf16[64,4,128]{2,1,0:T(4,128)(2,1)S(1)} async-done(((bf16[64,4,128]{2,1,0:T(4,128)(2,1)}), bf16[64,4,128]{2,1,0:T(4,128)(2,1)S(1)}, u32[]{:S(2)}, u32[]{:S(2)}) %all-to-all-start) | async-done | bytes 65568 | tf_op jit(solution)/shard_map/all_to_all | solution.py:211
  26.5 0.0 copy-done.1
  26.5 0.0 copy-done.9
  26.5 0.0 copy-start.6
  26.5 0.4 %documents.1.grads_ref = bf16[8,4096]{1,0:T(8,128)(2,1)S(1)} custom-call(s32[1,64]{1,0:T(1,128)S(1)} %bitcast.12, bf16[256,128]{1,0:T(8,128)(2,1)S(1)} %bitcast.8, bf16[128,4096]{1,0:T(8,128)(2,1)S(1)} %copy-done.1), custom_call_target="tpu_custom_call" | custom-call | flops 10000000000 | bytes 10000000 | tf_op jit(solution)/shard_map/documents/pallas_call | solution.py:100
  26.9 1.9 %collective-permute-start.1 = (bf16[8,4096]{1,0:T(8,128)(2,1)S(1)}, bf16[8,4096]{1,0:T(8,128)(2,1)S(1)}, u32[]{:S(2)}, u32[]{:S(2)}) collective-permute-start(bf16[8,4096]{1,0:T(8,128)(2,1)S(1)} %documents.1.grads_ref), channel_id=1, source_target_pairs={{0,1},{1,0},{4,5},{5,4},{2,3},{3,2},{6,7},{7,6},{8,9},{9,8},{12,13... | collective-permute-start | bytes 196616 | tf_op jit(solution)/shard_map/ppermute | solution.py:202
  28.8 0.4 %near.1.near_ref = f32[8,256]{1,0:T(8,128)S(1)} custom-call(bf16[8,4096]{1,0:T(8,128)(2,1)S(1)} %documents.1.grads_ref, bf16[128,4096]{1,0:T(8,128)(2,1)S(1)} %copy-done.1, bf16[128,768]{1,0:T(8,128)(2,1)S(1)} %collective-permute-done.across_ref), custom_call_target="tpu_custom_call" | custom-call | tf_op jit(solution)/shard_map/near/pallas_call | solution.py:100
  29.2 0.5 %collective-permute-done.1.grads_ref.mate_grads_ref = bf16[8,4096]{1,0:T(8,128)(2,1)S(1)} collective-permute-done((bf16[8,4096]{1,0:T(8,128)(2,1)S(1)}, bf16[8,4096]{1,0:T(8,128)(2,1)S(1)}, u32[]{:S(2)}, u32[]{:S(2)}) %collective-permute-start.1) | collective-permute-done | bytes 65568 | tf_op jit(solution)/shard_map/ppermute | solution.py:202
  29.7 0.4 %mate.1.mate_near_ref = f32[8,256]{1,0:T(8,128)S(1)} custom-call(bf16[8,4096]{1,0:T(8,128)(2,1)S(1)} %collective-permute-done.1.grads_ref.mate_grads_ref, bf16[128,4096]{1,0:T(8,128)(2,1)S(1)} %copy-done.1, bf16[128,768]{1,0:T(8,128)(2,1)S(1)} %collective-permute-done.across_ref), custom_call_target="tpu_custom_call" | custom-call | tf_op jit(solution)/shard_map/mate/pallas_call | solution.py:100
  30.1 0.0 collective-permute-done.2.rest_ref
  30.1 0.0 collective-permute-done.3.refs_0_
  30.1 0.0 collective-permute-done.4.refs_1_
  30.1 0.0 collective-permute-done.5.refs_2_
  30.2 0.3 %far.1 = (f32[8,128]{1,0:T(8,128)S(1)}, f32[8,256]{1,0:T(8,128)S(1)}) custom-call(bf16[8,4096]{1,0:T(8,128)(2,1)S(1)} %documents.1.grads_ref, bf16[8,4096]{1,0:T(8,128)(2,1)S(1)} %collective-permute-done.1.grads_ref.mate_grads_ref, f32[8,256]{1,0:T(8,128)S(1)} %near.1.near_ref, f32[8,256]{1,0:T(8,128)S(1)} %mate.1.mate_near_ref, ...), custom_call_target="tpu_custom_call" | custom-call | tf_op jit(solution)/shard_map/far/pallas_call | solution.py:100
  30.5 1.0 %collective-permute-start.6 = (f32[8,256]{1,0:T(8,128)S(1)}, f32[8,256]{1,0:T(8,128)S(1)}, u32[]{:S(2)}, u32[]{:S(2)}) collective-permute-start(f32[8,256]{1,0:T(8,128)S(1)} %get-tuple-element.16), channel_id=1, source_target_pairs={{0,1},{1,0},{4,5},{5,4},{2,3},{3,2},{6,7},{7,6},{8,9},{9,8},{12,13... | collective-permute-start | bytes 24584 | tf_op jit(solution)/shard_map/ppermute | solution.py:202
  31.5 0.8 %collective-permute-done.6.mate_ref = f32[8,256]{1,0:T(8,128)S(1)} collective-permute-done((f32[8,256]{1,0:T(8,128)S(1)}, f32[8,256]{1,0:T(8,128)S(1)}, u32[]{:S(2)}, u32[]{:S(2)}) %collective-permute-start.6) | collective-permute-done | bytes 8224 | tf_op jit(solution)/shard_map/ppermute | solution.py:202
  32.3 0.0 copy-done.6
  32.3 0.7 %last.1 = f32[1,8,512]{2,1,0:T(8,128)} custom-call(s32[1,4]{1,0:T(1,128)S(1)} %copy-done.6, f32[8,256]{1,0:T(8,128)S(1)} %near.1.near_ref, f32[8,128]{1,0:T(8,128)S(1)} %get-tuple-element.15.far_ref, f32[8,256]{1,0:T(8,128)S(1)} %collective-permute-done.6.mate_ref), custom_call_target="tpu_custom_call" | custom-call | tf_op jit(solution)/shard_map/last/pallas_call | solution.py:100
Async XLA Ops:
  0.0 1.2 %copy-start = (bf16[128,4096]{1,0:T(8,128)(2,1)S(1)}, bf16[128,4096]{1,0:T(8,128)(2,1)}, u32[]{:S(2)}) copy-start(bf16[128,4096]{1,0:T(8,128)(2,1)} %own_ref.3) | copy-start | bytes 3145732
  1.2 3.5 %copy-start.4 = (s32[1,1,64]{2,1,0:T(1,128)S(1)}, s32[1,1,64]{2,1,0:T(1,128)}, u32[]{:S(2)}) copy-start(s32[1,1,64]{2,1,0:T(1,128)} %param.14) | copy-start | bytes 772
  1.2 3.5 %copy-start.5 = (s32[1,1,64]{2,1,0:T(1,128)S(1)}, s32[1,1,64]{2,1,0:T(1,128)}, u32[]{:S(2)}) copy-start(s32[1,1,64]{2,1,0:T(1,128)} %param.15) | copy-start | bytes 772
  1.2 3.7 %copy-start.2 = (bf16[1,128,14336]{2,1,0:T(8,128)(2,1)S(1)}, bf16[1,128,14336]{2,1,0:T(8,128)(2,1)}, u32[]{:S(2)}) copy-start(bf16[1,128,14336]{2,1,0:T(8,128)(2,1)} %grad_ref.1) | copy-start | bytes 11010052
  1.2 3.7 %copy-start.3 = (bf16[14336,64]{0,1:T(8,128)(2,1)S(1)}, bf16[14336,64]{0,1:T(8,128)(2,1)}, u32[]{:S(2)}) copy-start(bf16[14336,64]{0,1:T(8,128)(2,1)} %param.12) | copy-start | bytes 5505028
  1.3 4.7 %copy-start.7 = (bf16[1,128,4096]{2,1,0:T(8,128)(2,1)S(1)}, bf16[1,128,4096]{2,1,0:T(8,128)(2,1)}, u32[]{:S(2)}) copy-start(bf16[1,128,4096]{2,1,0:T(8,128)(2,1)} %act_ref.1) | copy-start | bytes 3145732
  1.3 4.7 %copy-start.8 = (bf16[4096,64]{0,1:T(8,128)(2,1)S(1)}, bf16[4096,64]{0,1:T(8,128)(2,1)}, u32[]{:S(2)}) copy-start(bf16[4096,64]{0,1:T(8,128)(2,1)} %param.11) | copy-start | bytes 1572868
  1.4 21.7 %collective-permute-start = (bf16[128,768]{1,0:T(8,128)(2,1)S(1)}, bf16[128,768]{1,0:T(8,128)(2,1)S(1)}, u32[]{:S(2)}, u32[]{:S(2)}) collective-permute-start(bf16[128,768]{1,0:T(8,128)(2,1)S(1)} %get-tuple-element.11), channel_id=1, source_target_pairs={{0,6},{1,7},{4,2},{5,3},{2,4},{3,5},{6,0},{7,1},{8,14},{9,15},{12,... | collective-permute-start | bytes 589832 | tf_op jit(solution)/shard_map/ppermute | solution.py:202
  6.0 20.5 %copy-start.1 = (bf16[128,4096]{1,0:T(8,128)(2,1)S(1)}, bf16[128,4096]{1,0:T(8,128)(2,1)}, u32[]{:S(2)}) copy-start(bf16[128,4096]{1,0:T(8,128)(2,1)} %own_ref.3) | copy-start | bytes 3145732
  6.0 20.5 %copy-start.9 = (s32[1,64,1]{1,2,0:T(1,128)S(1)}, s32[1,64,1]{1,2,0:T(1,128)}, u32[]{:S(2)}) copy-start(s32[1,64,1]{1,2,0:T(1,128)} %param.16) | copy-start | bytes 772
  7.3 19.2 %all-to-all-start = ((bf16[64,4,128]{2,1,0:T(4,128)(2,1)}), bf16[64,4,128]{2,1,0:T(4,128)(2,1)S(1)}, u32[]{:S(2)}, u32[]{:S(2)}) async-start(bf16[64,4,128]{2,1,0:T(4,128)(2,1)} %bitcast.5), calls=%async_computation | async-start | bytes 131072 | tf_op jit(solution)/shard_map/all_to_all | solution.py:211
  20.5 9.6 %collective-permute-start.2 = (bf16[128,1024]{1,0:T(8,128)(2,1)S(1)}, bf16[128,1024]{1,0:T(8,128)(2,1)S(1)}, u32[]{:S(2)}, u32[]{:S(2)}) collective-permute-start(bf16[128,1024]{1,0:T(8,128)(2,1)S(1)} %get-tuple-element.14), channel_id=1, source_target_pairs={{0,6},{1,7},{4,2},{5,3},{2,4},{3,5},{6,0},{7,1},{8,14},{9,15},{12,... | collective-permute-start | bytes 786440 | tf_op jit(solution)/shard_map/ppermute | solution.py:202
  23.0 7.1 %collective-permute-start.3 = (bf16[128,768]{1,0:T(8,128)(2,1)S(1)}, bf16[128,768]{1,0:T(8,128)(2,1)S(1)}, u32[]{:S(2)}, u32[]{:S(2)}) collective-permute-start(bf16[128,768]{1,0:T(8,128)(2,1)S(1)} %collective-permute-done.across_ref), channel_id=1, source_target_pairs={{0,4},{1,5},{4,0},{5,1},{2,6},{3,7},{6,2},{7,3},{8,12},{9,13},{12,... | collective-permute-start | bytes 589832 | tf_op jit(solution)/shard_map/ppermute | solution.py:202
  23.0 7.1 %collective-permute-start.4 = (bf16[128,768]{1,0:T(8,128)(2,1)S(1)}, bf16[128,768]{1,0:T(8,128)(2,1)S(1)}, u32[]{:S(2)}, u32[]{:S(2)}) collective-permute-start(bf16[128,768]{1,0:T(8,128)(2,1)S(1)} %collective-permute-done.across_ref), channel_id=1, source_target_pairs={{0,8},{1,9},{4,12},{5,13},{2,10},{3,11},{6,14},{7,15},{8,0},{9,1},... | collective-permute-start | bytes 589832 | tf_op jit(solution)/shard_map/ppermute | solution.py:202
  23.6 6.5 %collective-permute-start.5 = (bf16[128,768]{1,0:T(8,128)(2,1)S(1)}, bf16[128,768]{1,0:T(8,128)(2,1)S(1)}, u32[]{:S(2)}, u32[]{:S(2)}) collective-permute-start(bf16[128,768]{1,0:T(8,128)(2,1)S(1)} %collective-permute-done.across_ref), channel_id=1, source_target_pairs={{0,32},{1,33},{4,36},{5,37},{2,34},{3,35},{6,38},{7,39},{8,40},{9,... | collective-permute-start | bytes 589832 | tf_op jit(solution)/shard_map/ppermute | solution.py:202
  26.5 5.8 %copy-start.6 = (s32[1,4]{1,0:T(1,128)S(1)}, s32[1,4]{1,0:T(1,128)}, u32[]{:S(2)}) copy-start(s32[1,4]{1,0:T(1,128)} %order_ref.1) | copy-start | bytes 52
  26.9 2.8 %collective-permute-start.1 = (bf16[8,4096]{1,0:T(8,128)(2,1)S(1)}, bf16[8,4096]{1,0:T(8,128)(2,1)S(1)}, u32[]{:S(2)}, u32[]{:S(2)}) collective-permute-start(bf16[8,4096]{1,0:T(8,128)(2,1)S(1)} %documents.1.grads_ref), channel_id=1, source_target_pairs={{0,1},{1,0},{4,5},{5,4},{2,3},{3,2},{6,7},{7,6},{8,9},{9,8},{12,13... | collective-permute-start | bytes 196616 | tf_op jit(solution)/shard_map/ppermute | solution.py:202
  30.5 1.8 %collective-permute-start.6 = (f32[8,256]{1,0:T(8,128)S(1)}, f32[8,256]{1,0:T(8,128)S(1)}, u32[]{:S(2)}, u32[]{:S(2)}) collective-permute-start(f32[8,256]{1,0:T(8,128)S(1)} %get-tuple-element.16), channel_id=1, source_target_pairs={{0,1},{1,0},{4,5},{5,4},{2,3},{3,2},{6,7},{7,6},{8,9},{9,8},{12,13... | collective-permute-start | bytes 24584 | tf_op jit(solution)/shard_map/ppermute | solution.py:202

commit v6 on v5

--- a/solution.py
+++ b/solution.py
@@ -12,45 +12,14 @@
 TOK = 128
 ROWS = DOCS * CAP
 PANEL = 128
-SHARE = 768
-REST = R * R - 4 * SHARE
 NT = (((1,), (1,)), ((), ()))
 FIRST = 62
 
 
-ACT_STEPS = (4096,)
-GRAD_STEPS = (7168, 4096, 3072)
-
-
-GIVEN_US = 10
-
-
-def given_kernel(panel_hbm, share_ref, rest_ref, sems):
-    share = pl.multiple_of((share_of(lax.axis_index("docs")) ^ 1) * SHARE, SHARE)
-    copies = (
-        pltpu.make_async_copy(panel_hbm.at[:, pl.ds(share, SHARE)], share_ref, sems.at[0]),
-        pltpu.make_async_copy(panel_hbm.at[:, pl.ds(4 * SHARE, REST)], rest_ref, sems.at[1]),
-    )
-    for copy in copies:
-        copy.start()
-    for copy in copies:
-        copy.wait()
-
-
-def given(panels):
-    return pl.pallas_call(
-        given_kernel,
-        out_shape=(
-            jax.ShapeDtypeStruct((PANEL, SHARE), jnp.bfloat16),
-            jax.ShapeDtypeStruct((PANEL, REST), jnp.bfloat16),
-        ),
-        in_specs=[pl.BlockSpec(memory_space=pltpu.HBM)],
-        out_specs=(pl.BlockSpec(memory_space=pltpu.VMEM),) * 2,
-        scratch_shapes=[pltpu.SemaphoreType.DMA((2,))],
-        compiler_params=pltpu.CompilerParams(vmem_limit_bytes=8 << 20),
-        cost_estimate=pl.CostEstimate(flops=GIVEN_US * 10**9, bytes_accessed=GIVEN_US * 10**6, transcendentals=0),
-        name="given",
-    )(panels)
+def spread_kernel(spread_ref):
+    source = lax.broadcasted_iota(jnp.int32, (DOCS, ROWS), 0)
+    place = lax.broadcasted_iota(jnp.int32, (DOCS, ROWS), 1) >> 2
+    spread_ref[...] = jnp.where((place ^ FIRST) == source, 1.0, 0.0).astype(jnp.bfloat16)
 
 
 def take_kernel(len_ref, own_ref, take_ref):
@@ -91,7 +60,7 @@
         out_grads, proj_out.T, name="grads",
     )
     return call(
-        pack_kernel, jax.ShapeDtypeStruct((ROWS, 2 * R), jnp.bfloat16), 10, [vmem] * 4,
+        pack_kernel, jax.ShapeDtypeStruct((ROWS, 2 * R), jnp.bfloat16), 0, [vmem] * 4,
         activations, proj_in.T, take, grad_low, name="pack",
     )
 
@@ -110,13 +79,10 @@
     )(*given)
 
 
-def document_kernel(slot_ref, rows_ref, panel_ref, grads_ref):
+def document_kernel(slot_ref, spread_ref, rows_ref, panel_ref, grads_ref):
     doc = lax.broadcasted_iota(jnp.int32, (DOC_OWN, DOCS), 0)
     mine = jnp.where(slot_ref[...] == doc, 1.0, 0.0).astype(jnp.bfloat16)
-    source = lax.broadcasted_iota(jnp.int32, (DOCS, ROWS), 0)
-    place = lax.broadcasted_iota(jnp.int32, (DOCS, ROWS), 1) >> 2
-    spread = jnp.where((place ^ FIRST) == source, 1.0, 0.0)
-    member = jnp.dot(mine, spread.astype(jnp.bfloat16), preferred_element_type=jnp.float32)
+    member = jnp.dot(mine, spread_ref[...], preferred_element_type=jnp.float32)
 
     rows = rows_ref[...]
     eye = (lax.broadcasted_iota(jnp.int32, (2 * R, 2 * R), 0)
@@ -136,46 +102,32 @@
     ).astype(jnp.bfloat16)
 
 
-def against(grads_ref, panel_ref, at):
-    grads = grads_ref[:, pl.ds(at, panel_ref.shape[1])]
-    return lax.dot_general(grads, panel_ref[...], NT, preferred_element_type=jnp.float32)
-
-
-def share_at(kth):
-    return pl.multiple_of((share_of(lax.axis_index("docs")) ^ kth) * SHARE, SHARE)
-
-
-def near_kernel(grads_ref, own_ref, across_ref, out_ref):
-    out_ref[:, :PANEL] = against(grads_ref, own_ref, 0)
-    out_ref[:, PANEL:] = against(grads_ref, across_ref, share_at(0))
-
-
-def far_kernel(grads_ref, mate_grads_ref, near_ref, mate_near_ref, rest_ref, *refs):
-    part_refs, out_ref, mate_out_ref = refs[:-2], refs[-2], refs[-1]
-    both = None
-    for ref, at in [(rest_ref, 4 * SHARE)] + [(r, share_at(k + 1)) for k, r in enumerate(part_refs)]:
-        cols = pl.ds(at, ref.shape[1])
-        grads = jnp.concatenate([grads_ref[:, cols], mate_grads_ref[:, cols]], axis=0)
-        part = lax.dot_general(grads, ref[...], NT, preferred_element_type=jnp.float32)
-        both = part if both is None else both + part
-    out_ref[...] = near_ref[:, PANEL:] + both[:DOC_OWN]
-    mate_out_ref[:, :PANEL] = mate_near_ref[:, :PANEL]
-    mate_out_ref[:, PANEL:] = mate_near_ref[:, PANEL:] + both[DOC_OWN:]
+def near_kernel(grads_ref, own_ref, out_ref):
+    out_ref[...] = lax.dot_general(
+        grads_ref[...], own_ref[...], NT, preferred_element_type=jnp.float32
+    )
+
+
+def far_kernel(grads_ref, mate_grads_ref, own_ref, across_ref, out_ref, mate_out_ref):
+    mate_grads = mate_grads_ref[...]
+    mate_out_ref[:, :PANEL] = lax.dot_general(
+        mate_grads, own_ref[...], NT, preferred_element_type=jnp.float32
+    )
+    both = jnp.concatenate([grads_ref[...], mate_grads], axis=0)
+    both = lax.dot_general(both, across_ref[...], NT, preferred_element_type=jnp.float32)
+    out_ref[...] = both[:DOC_OWN]
+    mate_out_ref[:, PANEL:] = both[DOC_OWN:]
 
 
 def last_kernel(order_ref, near_ref, far_ref, mate_ref, out_ref):
     query_at = lax.axis_index("query")
 
-    blocks = [near_ref[:, :PANEL], mate_ref[:, :PANEL], far_ref[...], mate_ref[:, PANEL:]]
+    blocks = [near_ref[...], mate_ref[:, :PANEL], far_ref[...], mate_ref[:, PANEL:]]
     for at in range(4):
         wanted = order_ref[:, at:at + 1]
         out_ref[0, :, at * PANEL:(at + 1) * PANEL] = sum(
             jnp.where(wanted == (query_at ^ kth), block, 0.0) for kth, block in enumerate(blocks)
         )
-
-
-def share_of(docs_at):
-    return (docs_at & 1) ^ (2 * ((docs_at >> 1) & 1)) ^ (3 * ((docs_at >> 3) & 1))
 
 
 def hop(fn):
@@ -193,9 +145,6 @@
 
 TO_CORE = hop(lambda z, y, x, core: (z, y, x, 1 - core))
 TO_CROSS = hop(lambda z, y, x, core: (z, y, 3 - x, core))
-TO_X = hop(lambda z, y, x, core: (z, y, x ^ 1, core))
-TO_Y = hop(lambda z, y, x, core: (z, y ^ 1, x, core))
-TO_Z = hop(lambda z, y, x, core: (z ^ 1, y, x, core))
 
 
 def send(value, pairs):
@@ -206,35 +155,30 @@
     activations, out_grads, proj_in, proj_out, panels, lengths, piece_owner, doc_slot, panel_order
 ):
     vmem = pl.BlockSpec(memory_space=pltpu.VMEM)
-    share, rest = given(panels)
+    spread = call(
+        spread_kernel, jax.ShapeDtypeStruct((DOCS, ROWS), jnp.bfloat16), 10, [], name="spread",
+    )
+    leaving, spread = lax.optimization_barrier((panels, spread))
+    across = send(leaving, TO_CROSS)
     packed = project(activations, out_grads, proj_in, proj_out, lengths[0], piece_owner[0])
     arrived = lax.all_to_all(
         packed.reshape(DOCS, CAP, 2 * R), "docs", split_axis=0, concat_axis=0, tiled=True,
         axis_index_groups=[[place ^ FIRST for place in range(DOCS)]],
     ).reshape(ROWS, 2 * R)
 
-    across = send(share, TO_CROSS)
-    rest = send(rest, TO_CROSS)
-    parts = [send(across, to) for to in (TO_X, TO_Y, TO_Z)]
-
     def block(width):
         return jax.ShapeDtypeStruct((DOC_OWN, width), jnp.float32)
 
     grads = call(
-        document_kernel, jax.ShapeDtypeStruct((DOC_OWN, R * R), jnp.bfloat16), 10,
-        [vmem] * 3, doc_slot[0].reshape(1, DOCS), arrived, panels, name="documents",
+        document_kernel, jax.ShapeDtypeStruct((DOC_OWN, R * R), jnp.bfloat16), 0,
+        [vmem] * 4, doc_slot[0].reshape(1, DOCS), spread, arrived, panels, name="documents",
     )
     mate_grads = send(grads, TO_CORE)
-    near = call(
-        near_kernel, block(2 * PANEL), 0, [vmem] * 3, grads, panels, across, name="near",
-    )
+    near = call(near_kernel, block(PANEL), 0, [vmem] * 2, grads, panels, name="near")
     near, mate_grads = lax.optimization_barrier((near, mate_grads))
-    mate_near = call(
-        near_kernel, block(2 * PANEL), 0, [vmem] * 3, mate_grads, panels, across, name="mate",
-    )
     far, mate_scores = call(
-        far_kernel, (block(PANEL), block(2 * PANEL)), 0, [vmem] * 8,
-        grads, mate_grads, near, mate_near, rest, *parts, name="far",
+        far_kernel, (block(PANEL), block(2 * PANEL)), 0, [vmem] * 4,
+        grads, mate_grads, panels, across, name="far",
     )
     mate_scores = send(mate_scores, TO_CORE)
     return call(

time: 33.2 us -> 31 us (0.934)
  blocking collectives: 0 us -> 18.4 us
  starting transfers between devices: 23.6 us -> 5.94 us
  waiting for transfers between devices: 3.13 us -> 1.36 us
  Pallas kernels: 4.82 us -> 3.95 us
    all_to_all x0 -> x1, blocking collectives: none -> 18.4 us  [shards(): lax.all_to_all(packed.reshape(DOCS, CAP, 2 * R), 'docs', split_axis=0, co...]
    all_to_all x1 -> x0, starting transfers between devices: 13.2 us -> none  [shards(): lax.all_to_all(packed.reshape(DOCS, CAP, 2 * R), 'docs', split_axis=0, co...]
    ppermute x7 -> x3, starting transfers between devices: 10.5 us -> 5.94 us  [send(): return lax.ppermute(value, ('docs', 'query'), pairs)]
    all_to_all x1 -> x0, waiting for transfers between devices: 1.79 us -> none  [shards(): lax.all_to_all(packed.reshape(DOCS, CAP, 2 * R), 'docs', split_axis=0, co...]
    pallas_call x8, Pallas kernels: 4.73 us -> 3.95 us  [call(): pl.pallas_call(kernel, out_shape=out_shape, in_specs=in_specs, out_specs=...]
    unnamed x20 -> x18, local copies, waits for them, and re-layouts: 1.27 us -> 1.23 us
    ppermute x7 -> x3, waiting for transfers between devices: 1.35 us -> 1.36 us  [send(): return lax.ppermute(value, ('docs', 'query'), pairs)]
  transfers between devices with their start and end apart: 8 -> 3, of which waited for: 3 -> 2; matrix products, arithmetic and copies ran while one was open for 0% -> 0% of each run, Pallas kernels for 11% -> 8%
where the time goes in v6:
time: 31 us; the launch traced here: 30.9 us
  blocking collectives  18.4 us (59%)
  starting transfers between devices  5.94 us (19%)
  Pallas kernels  3.95 us (13%)
  waiting for transfers between devices  1.36 us (4%)
  local copies, waits for them, and re-layouts  1.23 us (4%)
    all_to_all x1, blocking collectives, shards(): lax.all_to_all(packed.reshape(DOCS, CAP, 2 * R), 'docs', split_axis=0, co...  18.4 us
    ppermute x3, starting transfers between devices, send(): return lax.ppermute(value, ('docs', 'query'), pairs)  5.94 us
    pallas_call x8, Pallas kernels, call(): pl.pallas_call(kernel, out_shape=out_shape, in_specs=in_specs, out_specs=...  3.95 us
    ppermute x3, waiting for transfers between devices, send(): return lax.ppermute(value, ('docs', 'query'), pairs)  1.36 us
    unnamed x18, local copies, waits for them, and re-layouts  1.23 us
  transfers between devices with their start and end apart: 3, of which 2 were waited for; matrix products, arithmetic and copies ran while one was open for 0% of the time, Pallas kernels for 8%

profile of v6, /device:TPU:1, one launch (start us, length us, event | category | flops | bytes accessed | tf_op | source)
XLA Modules:
  0.0 30.9 jit_solution(9627295814547387804)
XLA Ops:
  0.0 0.0 copy-start
  0.0 0.0 copy-start.2
  0.0 0.0 copy-start.1
  0.0 1.2 %copy-done = bf16[128,4096]{1,0:T(8,128)(2,1)S(1)} copy-done((bf16[128,4096]{1,0:T(8,128)(2,1)S(1)}, bf16[128,4096]{1,0:T(8,128)(2,1)}, u32[]{:S(2)}) %copy-start) | copy-done | bytes 1048600
  1.2 0.0 copy-start.5
  1.2 0.0 copy-start.6
  1.2 0.0 copy-start.3
  1.2 0.0 copy-start.4
  1.2 3.4 %collective-permute-start.1 = (bf16[128,4096]{1,0:T(8,128)(2,1)S(1)}, bf16[128,4096]{1,0:T(8,128)(2,1)S(1)}, u32[]{:S(2)}, u32[]{:S(2)}) collective-permute-start(bf16[128,4096]{1,0:T(8,128)(2,1)S(1)} %copy-done), channel_id=1, source_target_pairs={{0,6},{1,7},{4,2},{5,3},{2,4},{3,5},{6,0},{7,1},{8,14},{9,15},{12,... | collective-permute-start | bytes 3145736 | tf_op jit(solution)/shard_map/ppermute | solution.py:151
  4.6 0.0 copy-done.2
  4.6 0.0 copy-done.1
  4.6 0.0 copy-start.7
  4.6 1.1 %grads.1.low_ref = f32[128,64]{1,0:T(8,128)S(1)} custom-call(bf16[1,128,14336]{2,1,0:T(8,128)(2,1)S(1)} %copy-done.1, bf16[64,14336]{1,0:T(8,128)(2,1)S(1)} %bitcast.7), custom_call_target="tpu_custom_call" | custom-call | tf_op jit(solution)/shard_map/grads/pallas_call | solution.py:69
  5.7 0.0 copy-start.8
  5.7 0.0 copy-done.5
  5.8 0.0 copy-done.6
  5.8 0.1 take.1.take_ref
  5.9 0.0 copy-done.3
  5.9 0.0 copy-done.4
  5.9 0.6 %pack.1 = bf16[256,128]{1,0:T(8,128)(2,1)S(1)} custom-call(bf16[1,128,4096]{2,1,0:T(8,128)(2,1)S(1)} %copy-done.3, bf16[64,4096]{1,0:T(8,128)(2,1)S(1)} %bitcast.8, bf16[256,128]{1,0:T(8,128)(2,1)S(1)} %take.1.take_ref, f32[128,64]{1,0:T(8,128)S(1)} %grads.1.low_ref), custom_call_target="tpu_custom_call" | custom-call | tf_op jit(solution)/shard_map/pack/pallas_call | solution.py:69
  6.6 18.4 %all_to_all.5 = bf16[64,4,128]{2,1,0:T(4,128)(2,1)S(1)} all-to-all(bf16[64,4,128]{2,1,0:T(4,128)(2,1)S(1)} %bitcast.9), channel_id=1, replica_groups={{248,252,240,244,232,236,224,228,216,220,208,212,200,204,192,196,184,18..., dimensions={0} | all-to-all | bytes 131072 | tf_op jit(solution)/shard_map/all_to_all | solution.py:164
  24.9 0.0 copy-done.7
  25.0 0.4 %documents.1.grads_ref = bf16[8,4096]{1,0:T(8,128)(2,1)S(1)} custom-call(s32[1,64]{1,0:T(1,128)S(1)} %bitcast.13, bf16[64,256]{1,0:T(8,128)(2,1)S(1)} %spread.1.spread_ref, bf16[256,128]{1,0:T(8,128)(2,1)S(1)} %bitcast.10, bf16[128,4096]{1,0:T(8,128)(2,1)S(1)} %copy-done), custom_call_target="tpu_custom_call" | custom-call | tf_op jit(solution)/shard_map/documents/pallas_call | solution.py:69
  25.3 2.1 %collective-permute-start = (bf16[8,4096]{1,0:T(8,128)(2,1)S(1)}, bf16[8,4096]{1,0:T(8,128)(2,1)S(1)}, u32[]{:S(2)}, u32[]{:S(2)}) collective-permute-start(bf16[8,4096]{1,0:T(8,128)(2,1)S(1)} %documents.1.grads_ref), channel_id=1, source_target_pairs={{0,1},{1,0},{4,5},{5,4},{2,3},{3,2},{6,7},{7,6},{8,9},{9,8},{12,13... | collective-permute-start | bytes 196616 | tf_op jit(solution)/shard_map/ppermute | solution.py:151
  27.4 0.4 %near.1.near_ref = f32[8,128]{1,0:T(8,128)S(1)} custom-call(bf16[8,4096]{1,0:T(8,128)(2,1)S(1)} %documents.1.grads_ref, bf16[128,4096]{1,0:T(8,128)(2,1)S(1)} %copy-done), custom_call_target="tpu_custom_call" | custom-call | tf_op jit(solution)/shard_map/near/pallas_call | solution.py:69
  27.8 0.5 %collective-permute-done.mate_grads_ref = bf16[8,4096]{1,0:T(8,128)(2,1)S(1)} collective-permute-done((bf16[8,4096]{1,0:T(8,128)(2,1)S(1)}, bf16[8,4096]{1,0:T(8,128)(2,1)S(1)}, u32[]{:S(2)}, u32[]{:S(2)}) %collective-permute-start) | collective-permute-done | bytes 65568 | tf_op jit(solution)/shard_map/ppermute | solution.py:151
  28.3 0.0 collective-permute-done.1.across_ref
  28.3 0.6 %far.1 = (f32[8,128]{1,0:T(8,128)S(1)}, f32[8,256]{1,0:T(8,128)S(1)}) custom-call(bf16[8,4096]{1,0:T(8,128)(2,1)S(1)} %documents.1.grads_ref, bf16[8,4096]{1,0:T(8,128)(2,1)S(1)} %collective-permute-done.mate_grads_ref, bf16[128,4096]{1,0:T(8,128)(2,1)S(1)} %copy-done, bf16[128,4096]{1,0:T(8,128)(2,1)S(1)} %collective-permute-done.1.across_ref), custom_call_target="tpu_custom_call" | custom-call | tf_op jit(solution)/shard_map/far/pallas_call | solution.py:69
  28.9 0.5 %collective-permute-start.2 = (f32[8,256]{1,0:T(8,128)S(1)}, f32[8,256]{1,0:T(8,128)S(1)}, u32[]{:S(2)}, u32[]{:S(2)}) collective-permute-start(f32[8,256]{1,0:T(8,128)S(1)} %get-tuple-element.16), channel_id=1, source_target_pairs={{0,1},{1,0},{4,5},{5,4},{2,3},{3,2},{6,7},{7,6},{8,9},{9,8},{12,13... | collective-permute-start | bytes 24584 | tf_op jit(solution)/shard_map/ppermute | solution.py:151
  29.4 0.8 %collective-permute-done.2.mate_ref = f32[8,256]{1,0:T(8,128)S(1)} collective-permute-done((f32[8,256]{1,0:T(8,128)S(1)}, f32[8,256]{1,0:T(8,128)S(1)}, u32[]{:S(2)}, u32[]{:S(2)}) %collective-permute-start.2) | collective-permute-done | bytes 8224 | tf_op jit(solution)/shard_map/ppermute | solution.py:151
  30.2 0.0 copy-done.8
  30.2 0.7 %last.1 = f32[1,8,512]{2,1,0:T(8,128)} custom-call(s32[1,4]{1,0:T(1,128)S(1)} %copy-done.8, f32[8,128]{1,0:T(8,128)S(1)} %near.1.near_ref, f32[8,128]{1,0:T(8,128)S(1)} %get-tuple-element.15.far_ref, f32[8,256]{1,0:T(8,128)S(1)} %collective-permute-done.2.mate_ref), custom_call_target="tpu_custom_call" | custom-call | tf_op jit(solution)/shard_map/last/pallas_call | solution.py:69
  (1 shorter events, 0.0 us)
Async XLA Ops:
  0.0 1.2 %copy-start = (bf16[128,4096]{1,0:T(8,128)(2,1)S(1)}, bf16[128,4096]{1,0:T(8,128)(2,1)}, u32[]{:S(2)}) copy-start(bf16[128,4096]{1,0:T(8,128)(2,1)} %own_ref.3) | copy-start | bytes 3145732
  0.0 4.6 %copy-start.2 = (bf16[14336,64]{0,1:T(8,128)(2,1)S(1)}, bf16[14336,64]{0,1:T(8,128)(2,1)}, u32[]{:S(2)}) copy-start(bf16[14336,64]{0,1:T(8,128)(2,1)} %param.12) | copy-start | bytes 5505028
  0.0 4.6 %copy-start.1 = (bf16[1,128,14336]{2,1,0:T(8,128)(2,1)S(1)}, bf16[1,128,14336]{2,1,0:T(8,128)(2,1)}, u32[]{:S(2)}) copy-start(bf16[1,128,14336]{2,1,0:T(8,128)(2,1)} %grad_ref.1) | copy-start | bytes 11010052
  1.2 4.5 %copy-start.5 = (s32[1,1,64]{2,1,0:T(1,128)S(1)}, s32[1,1,64]{2,1,0:T(1,128)}, u32[]{:S(2)}) copy-start(s32[1,1,64]{2,1,0:T(1,128)} %param.14) | copy-start | bytes 772
  1.2 4.5 %copy-start.6 = (s32[1,1,64]{2,1,0:T(1,128)S(1)}, s32[1,1,64]{2,1,0:T(1,128)}, u32[]{:S(2)}) copy-start(s32[1,1,64]{2,1,0:T(1,128)} %param.15) | copy-start | bytes 772
  1.2 4.7 %copy-start.3 = (bf16[1,128,4096]{2,1,0:T(8,128)(2,1)S(1)}, bf16[1,128,4096]{2,1,0:T(8,128)(2,1)}, u32[]{:S(2)}) copy-start(bf16[1,128,4096]{2,1,0:T(8,128)(2,1)} %act_ref.1) | copy-start | bytes 3145732
  1.2 4.7 %copy-start.4 = (bf16[4096,64]{0,1:T(8,128)(2,1)S(1)}, bf16[4096,64]{0,1:T(8,128)(2,1)}, u32[]{:S(2)}) copy-start(bf16[4096,64]{0,1:T(8,128)(2,1)} %param.11) | copy-start | bytes 1572868
  1.2 27.1 %collective-permute-start.1 = (bf16[128,4096]{1,0:T(8,128)(2,1)S(1)}, bf16[128,4096]{1,0:T(8,128)(2,1)S(1)}, u32[]{:S(2)}, u32[]{:S(2)}) collective-permute-start(bf16[128,4096]{1,0:T(8,128)(2,1)S(1)} %copy-done), channel_id=1, source_target_pairs={{0,6},{1,7},{4,2},{5,3},{2,4},{3,5},{6,0},{7,1},{8,14},{9,15},{12,... | collective-permute-start | bytes 3145736 | tf_op jit(solution)/shard_map/ppermute | solution.py:151
  4.6 20.3 %copy-start.7 = (s32[1,64,1]{1,2,0:T(1,128)S(1)}, s32[1,64,1]{1,2,0:T(1,128)}, u32[]{:S(2)}) copy-start(s32[1,64,1]{1,2,0:T(1,128)} %param.16) | copy-start | bytes 772
  5.7 24.5 %copy-start.8 = (s32[1,4]{1,0:T(1,128)S(1)}, s32[1,4]{1,0:T(1,128)}, u32[]{:S(2)}) copy-start(s32[1,4]{1,0:T(1,128)} %order_ref.1) | copy-start | bytes 52
  25.3 3.0 %collective-permute-start = (bf16[8,4096]{1,0:T(8,128)(2,1)S(1)}, bf16[8,4096]{1,0:T(8,128)(2,1)S(1)}, u32[]{:S(2)}, u32[]{:S(2)}) collective-permute-start(bf16[8,4096]{1,0:T(8,128)(2,1)S(1)} %documents.1.grads_ref), channel_id=1, source_target_pairs={{0,1},{1,0},{4,5},{5,4},{2,3},{3,2},{6,7},{7,6},{8,9},{9,8},{12,13... | collective-permute-start | bytes 196616 | tf_op jit(solution)/shard_map/ppermute | solution.py:151
  28.9 1.3 %collective-permute-start.2 = (f32[8,256]{1,0:T(8,128)S(1)}, f32[8,256]{1,0:T(8,128)S(1)}, u32[]{:S(2)}, u32[]{:S(2)}) collective-permute-start(f32[8,256]{1,0:T(8,128)S(1)} %get-tuple-element.16), channel_id=1, source_target_pairs={{0,1},{1,0},{4,5},{5,4},{2,3},{3,2},{6,7},{7,6},{8,9},{9,8},{12,13... | collective-permute-start | bytes 24584 | tf_op jit(solution)/shard_map/ppermute | solution.py:151

commit v7 on v6

--- a/solution.py
+++ b/solution.py
@@ -55,6 +55,7 @@
         take_kernel, jax.ShapeDtypeStruct((ROWS, TOK), jnp.bfloat16), 0, [vmem] * 2,
         lengths, piece_owner, name="take",
     )
+    take, out_grads = lax.optimization_barrier((take, out_grads))
     grad_low = call(
         grad_kernel, jax.ShapeDtypeStruct((TOK, R), jnp.float32), 0, [vmem] * 2,
         out_grads, proj_out.T, name="grads",
@@ -108,12 +109,9 @@
     )
 
 
-def far_kernel(grads_ref, mate_grads_ref, own_ref, across_ref, out_ref, mate_out_ref):
-    mate_grads = mate_grads_ref[...]
-    mate_out_ref[:, :PANEL] = lax.dot_general(
-        mate_grads, own_ref[...], NT, preferred_element_type=jnp.float32
-    )
-    both = jnp.concatenate([grads_ref[...], mate_grads], axis=0)
+def far_kernel(grads_ref, mate_grads_ref, mate_near_ref, across_ref, out_ref, mate_out_ref):
+    mate_out_ref[:, :PANEL] = mate_near_ref[...]
+    both = jnp.concatenate([grads_ref[...], mate_grads_ref[...]], axis=0)
     both = lax.dot_general(both, across_ref[...], NT, preferred_element_type=jnp.float32)
     out_ref[...] = both[:DOC_OWN]
     mate_out_ref[:, PANEL:] = both[DOC_OWN:]
@@ -156,10 +154,10 @@
 ):
     vmem = pl.BlockSpec(memory_space=pltpu.VMEM)
     spread = call(
-        spread_kernel, jax.ShapeDtypeStruct((DOCS, ROWS), jnp.bfloat16), 10, [], name="spread",
-    )
-    leaving, spread = lax.optimization_barrier((panels, spread))
-    across = send(leaving, TO_CROSS)
+        spread_kernel, jax.ShapeDtypeStruct((DOCS, ROWS), jnp.bfloat16), 3, [], name="spread",
+    )
+    across = send(panels, TO_CROSS)
+    spread, proj_out = lax.optimization_barrier((spread, proj_out))
     packed = project(activations, out_grads, proj_in, proj_out, lengths[0], piece_owner[0])
     arrived = lax.all_to_all(
         packed.reshape(DOCS, CAP, 2 * R), "docs", split_axis=0, concat_axis=0, tiled=True,
@@ -176,9 +174,10 @@
     mate_grads = send(grads, TO_CORE)
     near = call(near_kernel, block(PANEL), 0, [vmem] * 2, grads, panels, name="near")
     near, mate_grads = lax.optimization_barrier((near, mate_grads))
+    mate_near = call(near_kernel, block(PANEL), 0, [vmem] * 2, mate_grads, panels, name="mate")
     far, mate_scores = call(
         far_kernel, (block(PANEL), block(2 * PANEL)), 0, [vmem] * 4,
-        grads, mate_grads, panels, across, name="far",
+        grads, mate_grads, mate_near, across, name="far",
     )
     mate_scores = send(mate_scores, TO_CORE)
     return call(

time: 31 us -> 30.4 us (0.981)
  local copies, waits for them, and re-layouts: 1.23 us -> 0.06 us
  blocking collectives: 18.4 us -> 19.1 us
  starting transfers between devices: 5.94 us -> 5.6 us
    unnamed x18, local copies, waits for them, and re-layouts: 1.23 us -> 0.06 us
    all_to_all x1, blocking collectives: 18.4 us -> 19.1 us  [shards(): lax.all_to_all(packed.reshape(DOCS, CAP, 2 * R), 'docs', split_axis=0, co...]
    ppermute x3, starting transfers between devices: 5.94 us -> 5.6 us  [send(): return lax.ppermute(value, ('docs', 'query'), pairs)]
    pallas_call x8 -> x9, Pallas kernels: 3.95 us -> 4.07 us  [call(): pl.pallas_call(kernel, out_shape=out_shape, in_specs=in_specs, out_specs=...]
  transfers between devices with their start and end apart: 3 -> 3, of which waited for: 2 -> 2; matrix products, arithmetic and copies ran while one was open for 0% -> 0% of each run, Pallas kernels for 8% -> 10%
where the time goes in v7:
time: 30.4 us; the launch traced here: 30.3 us
  blocking collectives  19.1 us (63%)
  starting transfers between devices  5.6 us (18%)
  Pallas kernels  4.07 us (13%)
  waiting for transfers between devices  1.36 us (4%)
    all_to_all x1, blocking collectives, shards(): lax.all_to_all(packed.reshape(DOCS, CAP, 2 * R), 'docs', split_axis=0, co...  19.1 us
    ppermute x3, starting transfers between devices, send(): return lax.ppermute(value, ('docs', 'query'), pairs)  5.6 us
    pallas_call x9, Pallas kernels, call(): pl.pallas_call(kernel, out_shape=out_shape, in_specs=in_specs, out_specs=...  4.07 us
    ppermute x3, waiting for transfers between devices, send(): return lax.ppermute(value, ('docs', 'query'), pairs)  1.36 us
  transfers between devices with their start and end apart: 3, of which 2 were waited for; matrix products, arithmetic and copies ran while one was open for 0% of the time, Pallas kernels for 10%

profile of v7, /device:TPU:1, one launch (start us, length us, event | category | flops | bytes accessed | tf_op | source)
XLA Modules:
  0.0 30.3 jit_solution(1065931528646848500)
XLA Ops:
  0.0 0.0 copy-start.2
  0.0 0.0 copy-start.6
  0.0 0.0 copy-start.5
  0.0 0.0 copy-start.1
  0.0 3.4 %collective-permute-start.1 = (bf16[128,4096]{1,0:T(8,128)(2,1)}, bf16[128,4096]{1,0:T(8,128)(2,1)S(1)}, u32[]{:S(2)}, u32[]{:S(2)}) collective-permute-start(bf16[128,4096]{1,0:T(8,128)(2,1)} %own_ref.3), channel_id=1, source_target_pairs={{0,6},{1,7},{4,2},{5,3},{2,4},{3,5},{6,0},{7,1},{8,14},{9,15},{12,... | collective-permute-start | bytes 3145736 | tf_op jit(solution)/shard_map/ppermute | solution.py:149
  3.4 0.0 copy-start.3
  3.4 0.0 copy-start.4
  3.5 0.0 copy-done.6
  3.5 0.0 copy-done.5
  3.5 0.1 take.1.take_ref
  3.6 0.0 copy-done.2
  3.6 0.0 copy-done.1
  3.6 0.0 copy-start
  3.6 0.0 copy-start.7
  3.6 1.1 %grads.1.low_ref = f32[128,64]{1,0:T(8,128)S(1)} custom-call(bf16[1,128,14336]{2,1,0:T(8,128)(2,1)S(1)} %copy-done.1, bf16[64,14336]{1,0:T(8,128)(2,1)S(1)} %bitcast.7), custom_call_target="tpu_custom_call" | custom-call | tf_op jit(solution)/shard_map/grads/pallas_call | solution.py:70
  4.7 0.0 copy-start.8
  4.8 0.0 copy-done.3
  4.8 0.0 copy-done.4
  4.8 0.6 %pack.1 = bf16[256,128]{1,0:T(8,128)(2,1)S(1)} custom-call(bf16[1,128,4096]{2,1,0:T(8,128)(2,1)S(1)} %copy-done.3, bf16[64,4096]{1,0:T(8,128)(2,1)S(1)} %bitcast.8, bf16[256,128]{1,0:T(8,128)(2,1)S(1)} %take.1.take_ref, f32[128,64]{1,0:T(8,128)S(1)} %grads.1.low_ref), custom_call_target="tpu_custom_call" | custom-call | tf_op jit(solution)/shard_map/pack/pallas_call | solution.py:70
  5.4 19.1 %all_to_all.5 = bf16[64,4,128]{2,1,0:T(4,128)(2,1)S(1)} all-to-all(bf16[64,4,128]{2,1,0:T(4,128)(2,1)S(1)} %bitcast.9), channel_id=1, replica_groups={{248,252,240,244,232,236,224,228,216,220,208,212,200,204,192,196,184,18..., dimensions={0} | all-to-all | bytes 131072 | tf_op jit(solution)/shard_map/all_to_all | solution.py:162
  24.5 0.0 copy-done
  24.5 0.0 copy-done.7
  24.5 0.4 %documents.1.grads_ref = bf16[8,4096]{1,0:T(8,128)(2,1)S(1)} custom-call(s32[1,64]{1,0:T(1,128)S(1)} %bitcast.13, bf16[64,256]{1,0:T(8,128)(2,1)S(1)} %spread.1.spread_ref, bf16[256,128]{1,0:T(8,128)(2,1)S(1)} %bitcast.10, bf16[128,4096]{1,0:T(8,128)(2,1)S(1)} %copy-done), custom_call_target="tpu_custom_call" | custom-call | tf_op jit(solution)/shard_map/documents/pallas_call | solution.py:70
  24.9 1.8 %collective-permute-start = (bf16[8,4096]{1,0:T(8,128)(2,1)S(1)}, bf16[8,4096]{1,0:T(8,128)(2,1)S(1)}, u32[]{:S(2)}, u32[]{:S(2)}) collective-permute-start(bf16[8,4096]{1,0:T(8,128)(2,1)S(1)} %documents.1.grads_ref), channel_id=1, source_target_pairs={{0,1},{1,0},{4,5},{5,4},{2,3},{3,2},{6,7},{7,6},{8,9},{9,8},{12,13... | collective-permute-start | bytes 196616 | tf_op jit(solution)/shard_map/ppermute | solution.py:149
  26.7 0.4 %near.1.near_ref = f32[8,128]{1,0:T(8,128)S(1)} custom-call(bf16[8,4096]{1,0:T(8,128)(2,1)S(1)} %documents.1.grads_ref, bf16[128,4096]{1,0:T(8,128)(2,1)S(1)} %copy-done), custom_call_target="tpu_custom_call" | custom-call | tf_op jit(solution)/shard_map/near/pallas_call | solution.py:70
  27.1 0.5 %collective-permute-done.grads_ref.mate_grads_ref = bf16[8,4096]{1,0:T(8,128)(2,1)S(1)} collective-permute-done((bf16[8,4096]{1,0:T(8,128)(2,1)S(1)}, bf16[8,4096]{1,0:T(8,128)(2,1)S(1)}, u32[]{:S(2)}, u32[]{:S(2)}) %collective-permute-start) | collective-permute-done | bytes 65568 | tf_op jit(solution)/shard_map/ppermute | solution.py:149
  27.6 0.4 %mate.1.mate_near_ref = f32[8,128]{1,0:T(8,128)S(1)} custom-call(bf16[8,4096]{1,0:T(8,128)(2,1)S(1)} %collective-permute-done.grads_ref.mate_grads_ref, bf16[128,4096]{1,0:T(8,128)(2,1)S(1)} %copy-done), custom_call_target="tpu_custom_call" | custom-call | tf_op jit(solution)/shard_map/mate/pallas_call | solution.py:70
  28.0 0.0 collective-permute-done.1.across_ref
  28.0 0.4 %far.1 = (f32[8,128]{1,0:T(8,128)S(1)}, f32[8,256]{1,0:T(8,128)S(1)}) custom-call(bf16[8,4096]{1,0:T(8,128)(2,1)S(1)} %documents.1.grads_ref, bf16[8,4096]{1,0:T(8,128)(2,1)S(1)} %collective-permute-done.grads_ref.mate_grads_ref, f32[8,128]{1,0:T(8,128)S(1)} %mate.1.mate_near_ref, bf16[128,4096]{1,0:T(8,128)(2,1)S(1)} %collective-permute-done.1.across_ref), custom_call_target="tpu_custom_call" | custom-call | tf_op jit(solution)/shard_map/far/pallas_call | solution.py:70
  28.4 0.4 %collective-permute-start.2 = (f32[8,256]{1,0:T(8,128)S(1)}, f32[8,256]{1,0:T(8,128)S(1)}, u32[]{:S(2)}, u32[]{:S(2)}) collective-permute-start(f32[8,256]{1,0:T(8,128)S(1)} %get-tuple-element.20), channel_id=1, source_target_pairs={{0,1},{1,0},{4,5},{5,4},{2,3},{3,2},{6,7},{7,6},{8,9},{9,8},{12,13... | collective-permute-start | bytes 24584 | tf_op jit(solution)/shard_map/ppermute | solution.py:149
  28.7 0.8 %collective-permute-done.2.mate_ref = f32[8,256]{1,0:T(8,128)S(1)} collective-permute-done((f32[8,256]{1,0:T(8,128)S(1)}, f32[8,256]{1,0:T(8,128)S(1)}, u32[]{:S(2)}, u32[]{:S(2)}) %collective-permute-start.2) | collective-permute-done | bytes 8224 | tf_op jit(solution)/shard_map/ppermute | solution.py:149
  29.6 0.0 copy-done.8
  29.6 0.7 %last.1 = f32[1,8,512]{2,1,0:T(8,128)} custom-call(s32[1,4]{1,0:T(1,128)S(1)} %copy-done.8, f32[8,128]{1,0:T(8,128)S(1)} %near.1.near_ref, f32[8,128]{1,0:T(8,128)S(1)} %get-tuple-element.19.far_ref, f32[8,256]{1,0:T(8,128)S(1)} %collective-permute-done.2.mate_ref), custom_call_target="tpu_custom_call" | custom-call | tf_op jit(solution)/shard_map/last/pallas_call | solution.py:70
  (1 shorter events, 0.0 us)
Async XLA Ops:
  0.0 3.6 %copy-start.2 = (bf16[14336,64]{0,1:T(8,128)(2,1)S(1)}, bf16[14336,64]{0,1:T(8,128)(2,1)}, u32[]{:S(2)}) copy-start(bf16[14336,64]{0,1:T(8,128)(2,1)} %param.12) | copy-start | bytes 5505028
  0.0 3.5 %copy-start.6 = (s32[1,1,64]{2,1,0:T(1,128)S(1)}, s32[1,1,64]{2,1,0:T(1,128)}, u32[]{:S(2)}) copy-start(s32[1,1,64]{2,1,0:T(1,128)} %param.15) | copy-start | bytes 772
  0.0 3.5 %copy-start.5 = (s32[1,1,64]{2,1,0:T(1,128)S(1)}, s32[1,1,64]{2,1,0:T(1,128)}, u32[]{:S(2)}) copy-start(s32[1,1,64]{2,1,0:T(1,128)} %param.14) | copy-start | bytes 772
  0.0 3.6 %copy-start.1 = (bf16[1,128,14336]{2,1,0:T(8,128)(2,1)S(1)}, bf16[1,128,14336]{2,1,0:T(8,128)(2,1)}, u32[]{:S(2)}) copy-start(bf16[1,128,14336]{2,1,0:T(8,128)(2,1)} %grad_ref) | copy-start | bytes 11010052
  0.0 28.0 %collective-permute-start.1 = (bf16[128,4096]{1,0:T(8,128)(2,1)}, bf16[128,4096]{1,0:T(8,128)(2,1)S(1)}, u32[]{:S(2)}, u32[]{:S(2)}) collective-permute-start(bf16[128,4096]{1,0:T(8,128)(2,1)} %own_ref.3), channel_id=1, source_target_pairs={{0,6},{1,7},{4,2},{5,3},{2,4},{3,5},{6,0},{7,1},{8,14},{9,15},{12,... | collective-permute-start | bytes 3145736 | tf_op jit(solution)/shard_map/ppermute | solution.py:149
  3.4 1.3 %copy-start.3 = (bf16[1,128,4096]{2,1,0:T(8,128)(2,1)S(1)}, bf16[1,128,4096]{2,1,0:T(8,128)(2,1)}, u32[]{:S(2)}) copy-start(bf16[1,128,4096]{2,1,0:T(8,128)(2,1)} %act_ref.1) | copy-start | bytes 3145732
  3.4 1.3 %copy-start.4 = (bf16[4096,64]{0,1:T(8,128)(2,1)S(1)}, bf16[4096,64]{0,1:T(8,128)(2,1)}, u32[]{:S(2)}) copy-start(bf16[4096,64]{0,1:T(8,128)(2,1)} %param.11) | copy-start | bytes 1572868
  3.6 20.9 %copy-start = (bf16[128,4096]{1,0:T(8,128)(2,1)S(1)}, bf16[128,4096]{1,0:T(8,128)(2,1)}, u32[]{:S(2)}) copy-start(bf16[128,4096]{1,0:T(8,128)(2,1)} %own_ref.3) | copy-start | bytes 3145732
  3.6 20.9 %copy-start.7 = (s32[1,64,1]{1,2,0:T(1,128)S(1)}, s32[1,64,1]{1,2,0:T(1,128)}, u32[]{:S(2)}) copy-start(s32[1,64,1]{1,2,0:T(1,128)} %param.16) | copy-start | bytes 772
  4.7 24.8 %copy-start.8 = (s32[1,4]{1,0:T(1,128)S(1)}, s32[1,4]{1,0:T(1,128)}, u32[]{:S(2)}) copy-start(s32[1,4]{1,0:T(1,128)} %order_ref.1) | copy-start | bytes 52
  24.9 2.7 %collective-permute-start = (bf16[8,4096]{1,0:T(8,128)(2,1)S(1)}, bf16[8,4096]{1,0:T(8,128)(2,1)S(1)}, u32[]{:S(2)}, u32[]{:S(2)}) collective-permute-start(bf16[8,4096]{1,0:T(8,128)(2,1)S(1)} %documents.1.grads_ref), channel_id=1, source_target_pairs={{0,1},{1,0},{4,5},{5,4},{2,3},{3,2},{6,7},{7,6},{8,9},{9,8},{12,13... | collective-permute-start | bytes 196616 | tf_op jit(solution)/shard_map/ppermute | solution.py:149
  28.4 1.2 %collective-permute-start.2 = (f32[8,256]{1,0:T(8,128)S(1)}, f32[8,256]{1,0:T(8,128)S(1)}, u32[]{:S(2)}, u32[]{:S(2)}) collective-permute-start(f32[8,256]{1,0:T(8,128)S(1)} %get-tuple-element.20), channel_id=1, source_target_pairs={{0,1},{1,0},{4,5},{5,4},{2,3},{3,2},{6,7},{7,6},{8,9},{9,8},{12,13... | collective-permute-start | bytes 24584 | tf_op jit(solution)/shard_map/ppermute | solution.py:149

commit v8 on v7

--- a/solution.py
+++ b/solution.py
@@ -13,7 +13,7 @@
 ROWS = DOCS * CAP
 PANEL = 128
 NT = (((1,), (1,)), ((), ()))
-FIRST = 62
+FIRST = 45
 
 
 def spread_kernel(spread_ref):

time: 30.4 us -> 29.8 us (0.980)
  blocking collectives: 19.1 us -> 16.6 us
  starting transfers between devices: 5.6 us -> 7.47 us
    all_to_all x1, blocking collectives: 19.1 us -> 16.6 us  [shards(): lax.all_to_all(packed.reshape(DOCS, CAP, 2 * R), 'docs', split_axis=0, co...]
    ppermute x3, starting transfers between devices: 5.6 us -> 7.47 us  [send(): return lax.ppermute(value, ('docs', 'query'), pairs)]
where the time goes in v8:
time: 29.8 us; the launch traced here: 29.7 us
  blocking collectives  16.6 us (56%)
  starting transfers between devices  7.47 us (25%)
  Pallas kernels  4.07 us (14%)
  waiting for transfers between devices  1.36 us (5%)
    all_to_all x1, blocking collectives, shards(): lax.all_to_all(packed.reshape(DOCS, CAP, 2 * R), 'docs', split_axis=0, co...  16.6 us
    ppermute x3, starting transfers between devices, send(): return lax.ppermute(value, ('docs', 'query'), pairs)  7.47 us
    pallas_call x9, Pallas kernels, call(): pl.pallas_call(kernel, out_shape=out_shape, in_specs=in_specs, out_specs=...  4.07 us
    ppermute x3, waiting for transfers between devices, send(): return lax.ppermute(value, ('docs', 'query'), pairs)  1.36 us
  transfers between devices with their start and end apart: 3, of which 2 were waited for; matrix products, arithmetic and copies ran while one was open for 0% of the time, Pallas kernels for 10%

profile of v8, /device:TPU:1, one launch (start us, length us, event | category | flops | bytes accessed | tf_op | source)
XLA Modules:
  0.0 29.7 jit_solution(36484759450339205)
XLA Ops:
  0.0 0.0 copy-start.2
  0.0 0.0 copy-start.6
  0.0 0.0 copy-start.5
  0.0 0.0 copy-start.1
  0.0 3.4 %collective-permute-start.1 = (bf16[128,4096]{1,0:T(8,128)(2,1)}, bf16[128,4096]{1,0:T(8,128)(2,1)S(1)}, u32[]{:S(2)}, u32[]{:S(2)}) collective-permute-start(bf16[128,4096]{1,0:T(8,128)(2,1)} %own_ref.3), channel_id=1, source_target_pairs={{0,6},{1,7},{4,2},{5,3},{2,4},{3,5},{6,0},{7,1},{8,14},{9,15},{12,... | collective-permute-start | bytes 3145736 | tf_op jit(solution)/shard_map/ppermute | solution.py:149
  3.4 0.0 copy-start.3
  3.4 0.0 copy-start.4
  3.5 0.0 copy-done.6
  3.5 0.0 copy-done.5
  3.5 0.1 take.1.take_ref
  3.6 0.0 copy-done.2
  3.6 0.0 copy-done.1
  3.6 0.0 copy-start
  3.6 0.0 copy-start.7
  3.6 1.1 %grads.1.low_ref = f32[128,64]{1,0:T(8,128)S(1)} custom-call(bf16[1,128,14336]{2,1,0:T(8,128)(2,1)S(1)} %copy-done.1, bf16[64,14336]{1,0:T(8,128)(2,1)S(1)} %bitcast.7), custom_call_target="tpu_custom_call" | custom-call | tf_op jit(solution)/shard_map/grads/pallas_call | solution.py:70
  4.7 0.0 copy-start.8
  4.8 0.0 copy-done.3
  4.8 0.0 copy-done.4
  4.8 0.6 %pack.1 = bf16[256,128]{1,0:T(8,128)(2,1)S(1)} custom-call(bf16[1,128,4096]{2,1,0:T(8,128)(2,1)S(1)} %copy-done.3, bf16[64,4096]{1,0:T(8,128)(2,1)S(1)} %bitcast.8, bf16[256,128]{1,0:T(8,128)(2,1)S(1)} %take.1.take_ref, f32[128,64]{1,0:T(8,128)S(1)} %grads.1.low_ref), custom_call_target="tpu_custom_call" | custom-call | tf_op jit(solution)/shard_map/pack/pallas_call | solution.py:70
  5.4 16.6 %all_to_all.5 = bf16[64,4,128]{2,1,0:T(4,128)(2,1)S(1)} all-to-all(bf16[64,4,128]{2,1,0:T(4,128)(2,1)S(1)} %bitcast.9), channel_id=1, replica_groups={{180,176,188,184,164,160,172,168,148,144,156,152,132,128,140,136,244,24..., dimensions={0} | all-to-all | bytes 131072 | tf_op jit(solution)/shard_map/all_to_all | solution.py:162
  22.0 0.0 copy-done
  22.0 0.0 copy-done.7
  22.0 0.4 %documents.1.grads_ref = bf16[8,4096]{1,0:T(8,128)(2,1)S(1)} custom-call(s32[1,64]{1,0:T(1,128)S(1)} %bitcast.13, bf16[64,256]{1,0:T(8,128)(2,1)S(1)} %spread.1.spread_ref, bf16[256,128]{1,0:T(8,128)(2,1)S(1)} %bitcast.10, bf16[128,4096]{1,0:T(8,128)(2,1)S(1)} %copy-done), custom_call_target="tpu_custom_call" | custom-call | tf_op jit(solution)/shard_map/documents/pallas_call | solution.py:70
  22.4 2.2 %collective-permute-start = (bf16[8,4096]{1,0:T(8,128)(2,1)S(1)}, bf16[8,4096]{1,0:T(8,128)(2,1)S(1)}, u32[]{:S(2)}, u32[]{:S(2)}) collective-permute-start(bf16[8,4096]{1,0:T(8,128)(2,1)S(1)} %documents.1.grads_ref), channel_id=1, source_target_pairs={{0,1},{1,0},{4,5},{5,4},{2,3},{3,2},{6,7},{7,6},{8,9},{9,8},{12,13... | collective-permute-start | bytes 196616 | tf_op jit(solution)/shard_map/ppermute | solution.py:149
  24.6 0.4 %near.1.near_ref = f32[8,128]{1,0:T(8,128)S(1)} custom-call(bf16[8,4096]{1,0:T(8,128)(2,1)S(1)} %documents.1.grads_ref, bf16[128,4096]{1,0:T(8,128)(2,1)S(1)} %copy-done), custom_call_target="tpu_custom_call" | custom-call | tf_op jit(solution)/shard_map/near/pallas_call | solution.py:70
  25.0 0.5 %collective-permute-done.grads_ref.mate_grads_ref = bf16[8,4096]{1,0:T(8,128)(2,1)S(1)} collective-permute-done((bf16[8,4096]{1,0:T(8,128)(2,1)S(1)}, bf16[8,4096]{1,0:T(8,128)(2,1)S(1)}, u32[]{:S(2)}, u32[]{:S(2)}) %collective-permute-start) | collective-permute-done | bytes 65568 | tf_op jit(solution)/shard_map/ppermute | solution.py:149
  25.5 0.4 %mate.1.mate_near_ref = f32[8,128]{1,0:T(8,128)S(1)} custom-call(bf16[8,4096]{1,0:T(8,128)(2,1)S(1)} %collective-permute-done.grads_ref.mate_grads_ref, bf16[128,4096]{1,0:T(8,128)(2,1)S(1)} %copy-done), custom_call_target="tpu_custom_call" | custom-call | tf_op jit(solution)/shard_map/mate/pallas_call | solution.py:70
  25.9 0.0 collective-permute-done.1.across_ref
  25.9 0.4 %far.1 = (f32[8,128]{1,0:T(8,128)S(1)}, f32[8,256]{1,0:T(8,128)S(1)}) custom-call(bf16[8,4096]{1,0:T(8,128)(2,1)S(1)} %documents.1.grads_ref, bf16[8,4096]{1,0:T(8,128)(2,1)S(1)} %collective-permute-done.grads_ref.mate_grads_ref, f32[8,128]{1,0:T(8,128)S(1)} %mate.1.mate_near_ref, bf16[128,4096]{1,0:T(8,128)(2,1)S(1)} %collective-permute-done.1.across_ref), custom_call_target="tpu_custom_call" | custom-call | tf_op jit(solution)/shard_map/far/pallas_call | solution.py:70
  26.3 1.9 %collective-permute-start.2 = (f32[8,256]{1,0:T(8,128)S(1)}, f32[8,256]{1,0:T(8,128)S(1)}, u32[]{:S(2)}, u32[]{:S(2)}) collective-permute-start(f32[8,256]{1,0:T(8,128)S(1)} %get-tuple-element.20), channel_id=1, source_target_pairs={{0,1},{1,0},{4,5},{5,4},{2,3},{3,2},{6,7},{7,6},{8,9},{9,8},{12,13... | collective-permute-start | bytes 24584 | tf_op jit(solution)/shard_map/ppermute | solution.py:149
  28.1 0.8 %collective-permute-done.2.mate_ref = f32[8,256]{1,0:T(8,128)S(1)} collective-permute-done((f32[8,256]{1,0:T(8,128)S(1)}, f32[8,256]{1,0:T(8,128)S(1)}, u32[]{:S(2)}, u32[]{:S(2)}) %collective-permute-start.2) | collective-permute-done | bytes 8224 | tf_op jit(solution)/shard_map/ppermute | solution.py:149
  29.0 0.0 copy-done.8
  29.0 0.7 %last.1 = f32[1,8,512]{2,1,0:T(8,128)} custom-call(s32[1,4]{1,0:T(1,128)S(1)} %copy-done.8, f32[8,128]{1,0:T(8,128)S(1)} %near.1.near_ref, f32[8,128]{1,0:T(8,128)S(1)} %get-tuple-element.19.far_ref, f32[8,256]{1,0:T(8,128)S(1)} %collective-permute-done.2.mate_ref), custom_call_target="tpu_custom_call" | custom-call | tf_op jit(solution)/shard_map/last/pallas_call | solution.py:70
  (1 shorter events, 0.0 us)
Async XLA Ops:
  0.0 3.6 %copy-start.2 = (bf16[14336,64]{0,1:T(8,128)(2,1)S(1)}, bf16[14336,64]{0,1:T(8,128)(2,1)}, u32[]{:S(2)}) copy-start(bf16[14336,64]{0,1:T(8,128)(2,1)} %param.12) | copy-start | bytes 5505028
  0.0 3.5 %copy-start.6 = (s32[1,1,64]{2,1,0:T(1,128)S(1)}, s32[1,1,64]{2,1,0:T(1,128)}, u32[]{:S(2)}) copy-start(s32[1,1,64]{2,1,0:T(1,128)} %param.15) | copy-start | bytes 772
  0.0 3.5 %copy-start.5 = (s32[1,1,64]{2,1,0:T(1,128)S(1)}, s32[1,1,64]{2,1,0:T(1,128)}, u32[]{:S(2)}) copy-start(s32[1,1,64]{2,1,0:T(1,128)} %param.14) | copy-start | bytes 772
  0.0 3.6 %copy-start.1 = (bf16[1,128,14336]{2,1,0:T(8,128)(2,1)S(1)}, bf16[1,128,14336]{2,1,0:T(8,128)(2,1)}, u32[]{:S(2)}) copy-start(bf16[1,128,14336]{2,1,0:T(8,128)(2,1)} %grad_ref) | copy-start | bytes 11010052
  0.0 25.8 %collective-permute-start.1 = (bf16[128,4096]{1,0:T(8,128)(2,1)}, bf16[128,4096]{1,0:T(8,128)(2,1)S(1)}, u32[]{:S(2)}, u32[]{:S(2)}) collective-permute-start(bf16[128,4096]{1,0:T(8,128)(2,1)} %own_ref.3), channel_id=1, source_target_pairs={{0,6},{1,7},{4,2},{5,3},{2,4},{3,5},{6,0},{7,1},{8,14},{9,15},{12,... | collective-permute-start | bytes 3145736 | tf_op jit(solution)/shard_map/ppermute | solution.py:149
  3.4 1.3 %copy-start.3 = (bf16[1,128,4096]{2,1,0:T(8,128)(2,1)S(1)}, bf16[1,128,4096]{2,1,0:T(8,128)(2,1)}, u32[]{:S(2)}) copy-start(bf16[1,128,4096]{2,1,0:T(8,128)(2,1)} %act_ref.1) | copy-start | bytes 3145732
  3.4 1.3 %copy-start.4 = (bf16[4096,64]{0,1:T(8,128)(2,1)S(1)}, bf16[4096,64]{0,1:T(8,128)(2,1)}, u32[]{:S(2)}) copy-start(bf16[4096,64]{0,1:T(8,128)(2,1)} %param.11) | copy-start | bytes 1572868
  3.6 18.4 %copy-start = (bf16[128,4096]{1,0:T(8,128)(2,1)S(1)}, bf16[128,4096]{1,0:T(8,128)(2,1)}, u32[]{:S(2)}) copy-start(bf16[128,4096]{1,0:T(8,128)(2,1)} %own_ref.3) | copy-start | bytes 3145732
  3.6 18.4 %copy-start.7 = (s32[1,64,1]{1,2,0:T(1,128)S(1)}, s32[1,64,1]{1,2,0:T(1,128)}, u32[]{:S(2)}) copy-start(s32[1,64,1]{1,2,0:T(1,128)} %param.16) | copy-start | bytes 772
  4.7 24.2 %copy-start.8 = (s32[1,4]{1,0:T(1,128)S(1)}, s32[1,4]{1,0:T(1,128)}, u32[]{:S(2)}) copy-start(s32[1,4]{1,0:T(1,128)} %order_ref.1) | copy-start | bytes 52
  22.4 3.1 %collective-permute-start = (bf16[8,4096]{1,0:T(8,128)(2,1)S(1)}, bf16[8,4096]{1,0:T(8,128)(2,1)S(1)}, u32[]{:S(2)}, u32[]{:S(2)}) collective-permute-start(bf16[8,4096]{1,0:T(8,128)(2,1)S(1)} %documents.1.grads_ref), channel_id=1, source_target_pairs={{0,1},{1,0},{4,5},{5,4},{2,3},{3,2},{6,7},{7,6},{8,9},{9,8},{12,13... | collective-permute-start | bytes 196616 | tf_op jit(solution)/shard_map/ppermute | solution.py:149
  26.3 2.7 %collective-permute-start.2 = (f32[8,256]{1,0:T(8,128)S(1)}, f32[8,256]{1,0:T(8,128)S(1)}, u32[]{:S(2)}, u32[]{:S(2)}) collective-permute-start(f32[8,256]{1,0:T(8,128)S(1)} %get-tuple-element.20), channel_id=1, source_target_pairs={{0,1},{1,0},{4,5},{5,4},{2,3},{3,2},{6,7},{7,6},{8,9},{9,8},{12,13... | collective-permute-start | bytes 24584 | tf_op jit(solution)/shard_map/ppermute | solution.py:149

commit v9 on v8

--- a/solution.py
+++ b/solution.py
@@ -13,7 +13,7 @@
 ROWS = DOCS * CAP
 PANEL = 128
 NT = (((1,), (1,)), ((), ()))
-FIRST = 45
+FIRST = 37
 
 
 def spread_kernel(spread_ref):

time: 29.8 us -> 29.8 us (level)
  no operation moved by 1% of the time
where the time goes in v9:
time: 29.8 us; the launch traced here: 29.7 us
  blocking collectives  16.7 us (56%)
  starting transfers between devices  7.37 us (25%)
  Pallas kernels  4.07 us (14%)
  waiting for transfers between devices  1.36 us (5%)
    all_to_all x1, blocking collectives, shards(): lax.all_to_all(packed.reshape(DOCS, CAP, 2 * R), 'docs', split_axis=0, co...  16.7 us
    ppermute x3, starting transfers between devices, send(): return lax.ppermute(value, ('docs', 'query'), pairs)  7.37 us
    pallas_call x9, Pallas kernels, call(): pl.pallas_call(kernel, out_shape=out_shape, in_specs=in_specs, out_specs=...  4.07 us
    ppermute x3, waiting for transfers between devices, send(): return lax.ppermute(value, ('docs', 'query'), pairs)  1.36 us
  transfers between devices with their start and end apart: 3, of which 2 were waited for; matrix products, arithmetic and copies ran while one was open for 0% of the time, Pallas kernels for 10%

profile of v9, /device:TPU:1, one launch (start us, length us, event | category | flops | bytes accessed | tf_op | source)
XLA Modules:
  0.0 29.7 jit_solution(8232120639344336005)
XLA Ops:
  0.0 0.0 copy-start.2
  0.0 0.0 copy-start.6
  0.0 0.0 copy-start.5
  0.0 0.0 copy-start.1
  0.0 3.4 %collective-permute-start.1 = (bf16[128,4096]{1,0:T(8,128)(2,1)}, bf16[128,4096]{1,0:T(8,128)(2,1)S(1)}, u32[]{:S(2)}, u32[]{:S(2)}) collective-permute-start(bf16[128,4096]{1,0:T(8,128)(2,1)} %own_ref.3), channel_id=1, source_target_pairs={{0,6},{1,7},{4,2},{5,3},{2,4},{3,5},{6,0},{7,1},{8,14},{9,15},{12,... | collective-permute-start | bytes 3145736 | tf_op jit(solution)/shard_map/ppermute | solution.py:149
  3.4 0.0 copy-start.3
  3.4 0.0 copy-start.4
  3.5 0.0 copy-done.6
  3.5 0.0 copy-done.5
  3.5 0.1 take.1.take_ref
  3.6 0.0 copy-done.2
  3.6 0.0 copy-done.1
  3.6 0.0 copy-start
  3.6 0.0 copy-start.7
  3.6 1.1 %grads.1.low_ref = f32[128,64]{1,0:T(8,128)S(1)} custom-call(bf16[1,128,14336]{2,1,0:T(8,128)(2,1)S(1)} %copy-done.1, bf16[64,14336]{1,0:T(8,128)(2,1)S(1)} %bitcast.7), custom_call_target="tpu_custom_call" | custom-call | tf_op jit(solution)/shard_map/grads/pallas_call | solution.py:70
  4.7 0.0 copy-start.8
  4.8 0.0 copy-done.3
  4.8 0.0 copy-done.4
  4.8 0.6 %pack.1 = bf16[256,128]{1,0:T(8,128)(2,1)S(1)} custom-call(bf16[1,128,4096]{2,1,0:T(8,128)(2,1)S(1)} %copy-done.3, bf16[64,4096]{1,0:T(8,128)(2,1)S(1)} %bitcast.8, bf16[256,128]{1,0:T(8,128)(2,1)S(1)} %take.1.take_ref, f32[128,64]{1,0:T(8,128)S(1)} %grads.1.low_ref), custom_call_target="tpu_custom_call" | custom-call | tf_op jit(solution)/shard_map/pack/pallas_call | solution.py:70
  5.4 16.7 %all_to_all.5 = bf16[64,4,128]{2,1,0:T(4,128)(2,1)S(1)} all-to-all(bf16[64,4,128]{2,1,0:T(4,128)(2,1)S(1)} %bitcast.9), channel_id=1, replica_groups={{148,144,156,152,132,128,140,136,180,176,188,184,164,160,172,168,212,20..., dimensions={0} | all-to-all | bytes 131072 | tf_op jit(solution)/shard_map/all_to_all | solution.py:162
  22.1 0.0 copy-done
  22.1 0.0 copy-done.7
  22.1 0.4 %documents.1.grads_ref = bf16[8,4096]{1,0:T(8,128)(2,1)S(1)} custom-call(s32[1,64]{1,0:T(1,128)S(1)} %bitcast.13, bf16[64,256]{1,0:T(8,128)(2,1)S(1)} %spread.1.spread_ref, bf16[256,128]{1,0:T(8,128)(2,1)S(1)} %bitcast.10, bf16[128,4096]{1,0:T(8,128)(2,1)S(1)} %copy-done), custom_call_target="tpu_custom_call" | custom-call | tf_op jit(solution)/shard_map/documents/pallas_call | solution.py:70
  22.5 2.2 %collective-permute-start = (bf16[8,4096]{1,0:T(8,128)(2,1)S(1)}, bf16[8,4096]{1,0:T(8,128)(2,1)S(1)}, u32[]{:S(2)}, u32[]{:S(2)}) collective-permute-start(bf16[8,4096]{1,0:T(8,128)(2,1)S(1)} %documents.1.grads_ref), channel_id=1, source_target_pairs={{0,1},{1,0},{4,5},{5,4},{2,3},{3,2},{6,7},{7,6},{8,9},{9,8},{12,13... | collective-permute-start | bytes 196616 | tf_op jit(solution)/shard_map/ppermute | solution.py:149
  24.7 0.4 %near.1.near_ref = f32[8,128]{1,0:T(8,128)S(1)} custom-call(bf16[8,4096]{1,0:T(8,128)(2,1)S(1)} %documents.1.grads_ref, bf16[128,4096]{1,0:T(8,128)(2,1)S(1)} %copy-done), custom_call_target="tpu_custom_call" | custom-call | tf_op jit(solution)/shard_map/near/pallas_call | solution.py:70
  25.0 0.5 %collective-permute-done.grads_ref.mate_grads_ref = bf16[8,4096]{1,0:T(8,128)(2,1)S(1)} collective-permute-done((bf16[8,4096]{1,0:T(8,128)(2,1)S(1)}, bf16[8,4096]{1,0:T(8,128)(2,1)S(1)}, u32[]{:S(2)}, u32[]{:S(2)}) %collective-permute-start) | collective-permute-done | bytes 65568 | tf_op jit(solution)/shard_map/ppermute | solution.py:149
  25.6 0.4 %mate.1.mate_near_ref = f32[8,128]{1,0:T(8,128)S(1)} custom-call(bf16[8,4096]{1,0:T(8,128)(2,1)S(1)} %collective-permute-done.grads_ref.mate_grads_ref, bf16[128,4096]{1,0:T(8,128)(2,1)S(1)} %copy-done), custom_call_target="tpu_custom_call" | custom-call | tf_op jit(solution)/shard_map/mate/pallas_call | solution.py:70
  25.9 0.0 collective-permute-done.1.across_ref
  25.9 0.4 %far.1 = (f32[8,128]{1,0:T(8,128)S(1)}, f32[8,256]{1,0:T(8,128)S(1)}) custom-call(bf16[8,4096]{1,0:T(8,128)(2,1)S(1)} %documents.1.grads_ref, bf16[8,4096]{1,0:T(8,128)(2,1)S(1)} %collective-permute-done.grads_ref.mate_grads_ref, f32[8,128]{1,0:T(8,128)S(1)} %mate.1.mate_near_ref, bf16[128,4096]{1,0:T(8,128)(2,1)S(1)} %collective-permute-done.1.across_ref), custom_call_target="tpu_custom_call" | custom-call | tf_op jit(solution)/shard_map/far/pallas_call | solution.py:70
  26.3 1.8 %collective-permute-start.2 = (f32[8,256]{1,0:T(8,128)S(1)}, f32[8,256]{1,0:T(8,128)S(1)}, u32[]{:S(2)}, u32[]{:S(2)}) collective-permute-start(f32[8,256]{1,0:T(8,128)S(1)} %get-tuple-element.20), channel_id=1, source_target_pairs={{0,1},{1,0},{4,5},{5,4},{2,3},{3,2},{6,7},{7,6},{8,9},{9,8},{12,13... | collective-permute-start | bytes 24584 | tf_op jit(solution)/shard_map/ppermute | solution.py:149
  28.1 0.8 %collective-permute-done.2.mate_ref = f32[8,256]{1,0:T(8,128)S(1)} collective-permute-done((f32[8,256]{1,0:T(8,128)S(1)}, f32[8,256]{1,0:T(8,128)S(1)}, u32[]{:S(2)}, u32[]{:S(2)}) %collective-permute-start.2) | collective-permute-done | bytes 8224 | tf_op jit(solution)/shard_map/ppermute | solution.py:149
  29.0 0.0 copy-done.8
  29.0 0.7 %last.1 = f32[1,8,512]{2,1,0:T(8,128)} custom-call(s32[1,4]{1,0:T(1,128)S(1)} %copy-done.8, f32[8,128]{1,0:T(8,128)S(1)} %near.1.near_ref, f32[8,128]{1,0:T(8,128)S(1)} %get-tuple-element.19.far_ref, f32[8,256]{1,0:T(8,128)S(1)} %collective-permute-done.2.mate_ref), custom_call_target="tpu_custom_call" | custom-call | tf_op jit(solution)/shard_map/last/pallas_call | solution.py:70
  (1 shorter events, 0.0 us)
Async XLA Ops:
  0.0 3.6 %copy-start.2 = (bf16[14336,64]{0,1:T(8,128)(2,1)S(1)}, bf16[14336,64]{0,1:T(8,128)(2,1)}, u32[]{:S(2)}) copy-start(bf16[14336,64]{0,1:T(8,128)(2,1)} %param.12) | copy-start | bytes 5505028
  0.0 3.5 %copy-start.6 = (s32[1,1,64]{2,1,0:T(1,128)S(1)}, s32[1,1,64]{2,1,0:T(1,128)}, u32[]{:S(2)}) copy-start(s32[1,1,64]{2,1,0:T(1,128)} %param.15) | copy-start | bytes 772
  0.0 3.5 %copy-start.5 = (s32[1,1,64]{2,1,0:T(1,128)S(1)}, s32[1,1,64]{2,1,0:T(1,128)}, u32[]{:S(2)}) copy-start(s32[1,1,64]{2,1,0:T(1,128)} %param.14) | copy-start | bytes 772
  0.0 3.6 %copy-start.1 = (bf16[1,128,14336]{2,1,0:T(8,128)(2,1)S(1)}, bf16[1,128,14336]{2,1,0:T(8,128)(2,1)}, u32[]{:S(2)}) copy-start(bf16[1,128,14336]{2,1,0:T(8,128)(2,1)} %grad_ref) | copy-start | bytes 11010052
  0.0 25.9 %collective-permute-start.1 = (bf16[128,4096]{1,0:T(8,128)(2,1)}, bf16[128,4096]{1,0:T(8,128)(2,1)S(1)}, u32[]{:S(2)}, u32[]{:S(2)}) collective-permute-start(bf16[128,4096]{1,0:T(8,128)(2,1)} %own_ref.3), channel_id=1, source_target_pairs={{0,6},{1,7},{4,2},{5,3},{2,4},{3,5},{6,0},{7,1},{8,14},{9,15},{12,... | collective-permute-start | bytes 3145736 | tf_op jit(solution)/shard_map/ppermute | solution.py:149
  3.4 1.3 %copy-start.3 = (bf16[1,128,4096]{2,1,0:T(8,128)(2,1)S(1)}, bf16[1,128,4096]{2,1,0:T(8,128)(2,1)}, u32[]{:S(2)}) copy-start(bf16[1,128,4096]{2,1,0:T(8,128)(2,1)} %act_ref.1) | copy-start | bytes 3145732
  3.4 1.3 %copy-start.4 = (bf16[4096,64]{0,1:T(8,128)(2,1)S(1)}, bf16[4096,64]{0,1:T(8,128)(2,1)}, u32[]{:S(2)}) copy-start(bf16[4096,64]{0,1:T(8,128)(2,1)} %param.11) | copy-start | bytes 1572868
  3.6 18.5 %copy-start = (bf16[128,4096]{1,0:T(8,128)(2,1)S(1)}, bf16[128,4096]{1,0:T(8,128)(2,1)}, u32[]{:S(2)}) copy-start(bf16[128,4096]{1,0:T(8,128)(2,1)} %own_ref.3) | copy-start | bytes 3145732
  3.6 18.5 %copy-start.7 = (s32[1,64,1]{1,2,0:T(1,128)S(1)}, s32[1,64,1]{1,2,0:T(1,128)}, u32[]{:S(2)}) copy-start(s32[1,64,1]{1,2,0:T(1,128)} %param.16) | copy-start | bytes 772
  4.7 24.2 %copy-start.8 = (s32[1,4]{1,0:T(1,128)S(1)}, s32[1,4]{1,0:T(1,128)}, u32[]{:S(2)}) copy-start(s32[1,4]{1,0:T(1,128)} %order_ref.1) | copy-start | bytes 52
  22.5 3.1 %collective-permute-start = (bf16[8,4096]{1,0:T(8,128)(2,1)S(1)}, bf16[8,4096]{1,0:T(8,128)(2,1)S(1)}, u32[]{:S(2)}, u32[]{:S(2)}) collective-permute-start(bf16[8,4096]{1,0:T(8,128)(2,1)S(1)} %documents.1.grads_ref), channel_id=1, source_target_pairs={{0,1},{1,0},{4,5},{5,4},{2,3},{3,2},{6,7},{7,6},{8,9},{9,8},{12,13... | collective-permute-start | bytes 196616 | tf_op jit(solution)/shard_map/ppermute | solution.py:149
  26.3 2.6 %collective-permute-start.2 = (f32[8,256]{1,0:T(8,128)S(1)}, f32[8,256]{1,0:T(8,128)S(1)}, u32[]{:S(2)}, u32[]{:S(2)}) collective-permute-start(f32[8,256]{1,0:T(8,128)S(1)} %get-tuple-element.20), channel_id=1, source_target_pairs={{0,1},{1,0},{4,5},{5,4},{2,3},{3,2},{6,7},{7,6},{8,9},{9,8},{12,13... | collective-permute-start | bytes 24584 | tf_op jit(solution)/shard_map/ppermute | solution.py:149

commit v10 on v9

--- a/solution.py
+++ b/solution.py
@@ -13,7 +13,7 @@
 ROWS = DOCS * CAP
 PANEL = 128
 NT = (((1,), (1,)), ((), ()))
-FIRST = 37
+FIRST = 36
 
 
 def spread_kernel(spread_ref):

time: 29.8 us -> 29.8 us (level)
  starting transfers between devices: 7.37 us -> 6.65 us
  blocking collectives: 16.7 us -> 17.4 us
    all_to_all x1, blocking collectives: 16.7 us -> 17.4 us  [shards(): lax.all_to_all(packed.reshape(DOCS, CAP, 2 * R), 'docs', split_axis=0, co...]
    ppermute x3, starting transfers between devices: 7.37 us -> 6.65 us  [send(): return lax.ppermute(value, ('docs', 'query'), pairs)]
where the time goes in v10:
time: 29.8 us; the launch traced here: 29.7 us
  blocking collectives  17.4 us (58%)
  starting transfers between devices  6.65 us (22%)
  Pallas kernels  4.07 us (14%)
  waiting for transfers between devices  1.36 us (5%)
    all_to_all x1, blocking collectives, shards(): lax.all_to_all(packed.reshape(DOCS, CAP, 2 * R), 'docs', split_axis=0, co...  17.4 us
    ppermute x3, starting transfers between devices, send(): return lax.ppermute(value, ('docs', 'query'), pairs)  6.65 us
    pallas_call x9, Pallas kernels, call(): pl.pallas_call(kernel, out_shape=out_shape, in_specs=in_specs, out_specs=...  4.07 us
    ppermute x3, waiting for transfers between devices, send(): return lax.ppermute(value, ('docs', 'query'), pairs)  1.36 us
  transfers between devices with their start and end apart: 3, of which 2 were waited for; matrix products, arithmetic and copies ran while one was open for 0% of the time, Pallas kernels for 10%

profile of v10, /device:TPU:1, one launch (start us, length us, event | category | flops | bytes accessed | tf_op | source)
XLA Modules:
  0.0 29.7 jit_solution(10301450807342959847)
XLA Ops:
  0.0 0.0 copy-start.2
  0.0 0.0 copy-start.6
  0.0 0.0 copy-start.5
  0.0 0.0 copy-start.1
  0.0 3.4 %collective-permute-start.1 = (bf16[128,4096]{1,0:T(8,128)(2,1)}, bf16[128,4096]{1,0:T(8,128)(2,1)S(1)}, u32[]{:S(2)}, u32[]{:S(2)}) collective-permute-start(bf16[128,4096]{1,0:T(8,128)(2,1)} %own_ref.3), channel_id=1, source_target_pairs={{0,6},{1,7},{4,2},{5,3},{2,4},{3,5},{6,0},{7,1},{8,14},{9,15},{12,... | collective-permute-start | bytes 3145736 | tf_op jit(solution)/shard_map/ppermute | solution.py:149
  3.4 0.0 copy-start.3
  3.4 0.0 copy-start.4
  3.5 0.0 copy-done.6
  3.5 0.0 copy-done.5
  3.5 0.1 take.1.take_ref
  3.6 0.0 copy-done.2
  3.6 0.0 copy-done.1
  3.6 0.0 copy-start
  3.6 0.0 copy-start.7
  3.6 1.1 %grads.1.low_ref = f32[128,64]{1,0:T(8,128)S(1)} custom-call(bf16[1,128,14336]{2,1,0:T(8,128)(2,1)S(1)} %copy-done.1, bf16[64,14336]{1,0:T(8,128)(2,1)S(1)} %bitcast.7), custom_call_target="tpu_custom_call" | custom-call | tf_op jit(solution)/shard_map/grads/pallas_call | solution.py:70
  4.7 0.0 copy-start.8
  4.8 0.0 copy-done.3
  4.8 0.0 copy-done.4
  4.8 0.6 %pack.1 = bf16[256,128]{1,0:T(8,128)(2,1)S(1)} custom-call(bf16[1,128,4096]{2,1,0:T(8,128)(2,1)S(1)} %copy-done.3, bf16[64,4096]{1,0:T(8,128)(2,1)S(1)} %bitcast.8, bf16[256,128]{1,0:T(8,128)(2,1)S(1)} %take.1.take_ref, f32[128,64]{1,0:T(8,128)S(1)} %grads.1.low_ref), custom_call_target="tpu_custom_call" | custom-call | tf_op jit(solution)/shard_map/pack/pallas_call | solution.py:70
  5.4 17.4 %all_to_all.5 = bf16[64,4,128]{2,1,0:T(4,128)(2,1)S(1)} all-to-all(bf16[64,4,128]{2,1,0:T(4,128)(2,1)S(1)} %bitcast.9), channel_id=1, replica_groups={{144,148,152,156,128,132,136,140,176,180,184,188,160,164,168,172,208,21..., dimensions={0} | all-to-all | bytes 131072 | tf_op jit(solution)/shard_map/all_to_all | solution.py:162
  22.8 0.0 copy-done
  22.8 0.0 copy-done.7
  22.9 0.4 %documents.1.grads_ref = bf16[8,4096]{1,0:T(8,128)(2,1)S(1)} custom-call(s32[1,64]{1,0:T(1,128)S(1)} %bitcast.13, bf16[64,256]{1,0:T(8,128)(2,1)S(1)} %spread.1.spread_ref, bf16[256,128]{1,0:T(8,128)(2,1)S(1)} %bitcast.10, bf16[128,4096]{1,0:T(8,128)(2,1)S(1)} %copy-done), custom_call_target="tpu_custom_call" | custom-call | tf_op jit(solution)/shard_map/documents/pallas_call | solution.py:70
  23.2 1.9 %collective-permute-start = (bf16[8,4096]{1,0:T(8,128)(2,1)S(1)}, bf16[8,4096]{1,0:T(8,128)(2,1)S(1)}, u32[]{:S(2)}, u32[]{:S(2)}) collective-permute-start(bf16[8,4096]{1,0:T(8,128)(2,1)S(1)} %documents.1.grads_ref), channel_id=1, source_target_pairs={{0,1},{1,0},{4,5},{5,4},{2,3},{3,2},{6,7},{7,6},{8,9},{9,8},{12,13... | collective-permute-start | bytes 196616 | tf_op jit(solution)/shard_map/ppermute | solution.py:149
  25.1 0.4 %near.1.near_ref = f32[8,128]{1,0:T(8,128)S(1)} custom-call(bf16[8,4096]{1,0:T(8,128)(2,1)S(1)} %documents.1.grads_ref, bf16[128,4096]{1,0:T(8,128)(2,1)S(1)} %copy-done), custom_call_target="tpu_custom_call" | custom-call | tf_op jit(solution)/shard_map/near/pallas_call | solution.py:70
  25.5 0.5 %collective-permute-done.grads_ref.mate_grads_ref = bf16[8,4096]{1,0:T(8,128)(2,1)S(1)} collective-permute-done((bf16[8,4096]{1,0:T(8,128)(2,1)S(1)}, bf16[8,4096]{1,0:T(8,128)(2,1)S(1)}, u32[]{:S(2)}, u32[]{:S(2)}) %collective-permute-start) | collective-permute-done | bytes 65568 | tf_op jit(solution)/shard_map/ppermute | solution.py:149
  26.0 0.4 %mate.1.mate_near_ref = f32[8,128]{1,0:T(8,128)S(1)} custom-call(bf16[8,4096]{1,0:T(8,128)(2,1)S(1)} %collective-permute-done.grads_ref.mate_grads_ref, bf16[128,4096]{1,0:T(8,128)(2,1)S(1)} %copy-done), custom_call_target="tpu_custom_call" | custom-call | tf_op jit(solution)/shard_map/mate/pallas_call | solution.py:70
  26.4 0.0 collective-permute-done.1.across_ref
  26.4 0.4 %far.1 = (f32[8,128]{1,0:T(8,128)S(1)}, f32[8,256]{1,0:T(8,128)S(1)}) custom-call(bf16[8,4096]{1,0:T(8,128)(2,1)S(1)} %documents.1.grads_ref, bf16[8,4096]{1,0:T(8,128)(2,1)S(1)} %collective-permute-done.grads_ref.mate_grads_ref, f32[8,128]{1,0:T(8,128)S(1)} %mate.1.mate_near_ref, bf16[128,4096]{1,0:T(8,128)(2,1)S(1)} %collective-permute-done.1.across_ref), custom_call_target="tpu_custom_call" | custom-call | tf_op jit(solution)/shard_map/far/pallas_call | solution.py:70
  26.8 1.4 %collective-permute-start.2 = (f32[8,256]{1,0:T(8,128)S(1)}, f32[8,256]{1,0:T(8,128)S(1)}, u32[]{:S(2)}, u32[]{:S(2)}) collective-permute-start(f32[8,256]{1,0:T(8,128)S(1)} %get-tuple-element.20), channel_id=1, source_target_pairs={{0,1},{1,0},{4,5},{5,4},{2,3},{3,2},{6,7},{7,6},{8,9},{9,8},{12,13... | collective-permute-start | bytes 24584 | tf_op jit(solution)/shard_map/ppermute | solution.py:149
  28.1 0.8 %collective-permute-done.2.mate_ref = f32[8,256]{1,0:T(8,128)S(1)} collective-permute-done((f32[8,256]{1,0:T(8,128)S(1)}, f32[8,256]{1,0:T(8,128)S(1)}, u32[]{:S(2)}, u32[]{:S(2)}) %collective-permute-start.2) | collective-permute-done | bytes 8224 | tf_op jit(solution)/shard_map/ppermute | solution.py:149
  29.0 0.0 copy-done.8
  29.0 0.7 %last.1 = f32[1,8,512]{2,1,0:T(8,128)} custom-call(s32[1,4]{1,0:T(1,128)S(1)} %copy-done.8, f32[8,128]{1,0:T(8,128)S(1)} %near.1.near_ref, f32[8,128]{1,0:T(8,128)S(1)} %get-tuple-element.19.far_ref, f32[8,256]{1,0:T(8,128)S(1)} %collective-permute-done.2.mate_ref), custom_call_target="tpu_custom_call" | custom-call | tf_op jit(solution)/shard_map/last/pallas_call | solution.py:70
  (1 shorter events, 0.0 us)
Async XLA Ops:
  0.0 3.6 %copy-start.2 = (bf16[14336,64]{0,1:T(8,128)(2,1)S(1)}, bf16[14336,64]{0,1:T(8,128)(2,1)}, u32[]{:S(2)}) copy-start(bf16[14336,64]{0,1:T(8,128)(2,1)} %param.12) | copy-start | bytes 5505028
  0.0 3.5 %copy-start.6 = (s32[1,1,64]{2,1,0:T(1,128)S(1)}, s32[1,1,64]{2,1,0:T(1,128)}, u32[]{:S(2)}) copy-start(s32[1,1,64]{2,1,0:T(1,128)} %param.15) | copy-start | bytes 772
  0.0 3.5 %copy-start.5 = (s32[1,1,64]{2,1,0:T(1,128)S(1)}, s32[1,1,64]{2,1,0:T(1,128)}, u32[]{:S(2)}) copy-start(s32[1,1,64]{2,1,0:T(1,128)} %param.14) | copy-start | bytes 772
  0.0 3.6 %copy-start.1 = (bf16[1,128,14336]{2,1,0:T(8,128)(2,1)S(1)}, bf16[1,128,14336]{2,1,0:T(8,128)(2,1)}, u32[]{:S(2)}) copy-start(bf16[1,128,14336]{2,1,0:T(8,128)(2,1)} %grad_ref) | copy-start | bytes 11010052
  0.0 26.4 %collective-permute-start.1 = (bf16[128,4096]{1,0:T(8,128)(2,1)}, bf16[128,4096]{1,0:T(8,128)(2,1)S(1)}, u32[]{:S(2)}, u32[]{:S(2)}) collective-permute-start(bf16[128,4096]{1,0:T(8,128)(2,1)} %own_ref.3), channel_id=1, source_target_pairs={{0,6},{1,7},{4,2},{5,3},{2,4},{3,5},{6,0},{7,1},{8,14},{9,15},{12,... | collective-permute-start | bytes 3145736 | tf_op jit(solution)/shard_map/ppermute | solution.py:149
  3.4 1.3 %copy-start.3 = (bf16[1,128,4096]{2,1,0:T(8,128)(2,1)S(1)}, bf16[1,128,4096]{2,1,0:T(8,128)(2,1)}, u32[]{:S(2)}) copy-start(bf16[1,128,4096]{2,1,0:T(8,128)(2,1)} %act_ref.1) | copy-start | bytes 3145732
  3.4 1.3 %copy-start.4 = (bf16[4096,64]{0,1:T(8,128)(2,1)S(1)}, bf16[4096,64]{0,1:T(8,128)(2,1)}, u32[]{:S(2)}) copy-start(bf16[4096,64]{0,1:T(8,128)(2,1)} %param.11) | copy-start | bytes 1572868
  3.6 19.2 %copy-start = (bf16[128,4096]{1,0:T(8,128)(2,1)S(1)}, bf16[128,4096]{1,0:T(8,128)(2,1)}, u32[]{:S(2)}) copy-start(bf16[128,4096]{1,0:T(8,128)(2,1)} %own_ref.3) | copy-start | bytes 3145732
  3.6 19.2 %copy-start.7 = (s32[1,64,1]{1,2,0:T(1,128)S(1)}, s32[1,64,1]{1,2,0:T(1,128)}, u32[]{:S(2)}) copy-start(s32[1,64,1]{1,2,0:T(1,128)} %param.16) | copy-start | bytes 772
  4.7 24.2 %copy-start.8 = (s32[1,4]{1,0:T(1,128)S(1)}, s32[1,4]{1,0:T(1,128)}, u32[]{:S(2)}) copy-start(s32[1,4]{1,0:T(1,128)} %order_ref.1) | copy-start | bytes 52
  23.2 2.8 %collective-permute-start = (bf16[8,4096]{1,0:T(8,128)(2,1)S(1)}, bf16[8,4096]{1,0:T(8,128)(2,1)S(1)}, u32[]{:S(2)}, u32[]{:S(2)}) collective-permute-start(bf16[8,4096]{1,0:T(8,128)(2,1)S(1)} %documents.1.grads_ref), channel_id=1, source_target_pairs={{0,1},{1,0},{4,5},{5,4},{2,3},{3,2},{6,7},{7,6},{8,9},{9,8},{12,13... | collective-permute-start | bytes 196616 | tf_op jit(solution)/shard_map/ppermute | solution.py:149
  26.8 2.2 %collective-permute-start.2 = (f32[8,256]{1,0:T(8,128)S(1)}, f32[8,256]{1,0:T(8,128)S(1)}, u32[]{:S(2)}, u32[]{:S(2)}) collective-permute-start(f32[8,256]{1,0:T(8,128)S(1)} %get-tuple-element.20), channel_id=1, source_target_pairs={{0,1},{1,0},{4,5},{5,4},{2,3},{3,2},{6,7},{7,6},{8,9},{9,8},{12,13... | collective-permute-start | bytes 24584 | tf_op jit(solution)/shard_map/ppermute | solution.py:149
